TPU v7x, 32 devices: a whole 2x2x4 slice. The times are simulated.
32 devices in a mesh: seg: 2 (over y), strip: 4 (over z), tile: 4 (over x, core).
Axes of the slice: x: 2, y: 2, z: 4, core: 2. Of those that a mesh axis runs over, the one named last changes fastest.
Arguments:
- positions: float32 [4, 3, 65536], P('strip', None, ('seg', 'tile')), may hold values from -4 to 4, as said below
- lever_arm: float32 [4, 3, 65536], P('strip', None, ('seg', 'tile')), may hold values from -6 to 6
- spline_time: float32 [4, 65536], P('strip', ('seg', 'tile')), may hold values from 0 to 1
- covariance: float32 [4, 6, 65536], P('strip', None, ('seg', 'tile')), may hold values from -0.35 to 1, as said below
- partner: int32 [4, 65536], P('strip', ('seg', 'tile')), may hold values from 0 to 32767
- partner_side: int32 [4, 512], P('strip', ('seg', 'tile')), may hold values from 0 to 2, as said below
- tile_knot: int32 [4, 512], P('strip', ('seg', 'tile')), may hold values from 0 to 127
Outputs:
- adjusted: float32 [4, 3, 65536], P('strip', None, ('seg', 'tile'))
- corrections: float32 [4, 6, 256], P('strip', None, 'seg')
Inputs may be any that keep to these rules, and one draw needn't show every extreme that they name: `partner_side`: 0: the intersecting strip is the one below, 1: the one above, 2: the tile has no partner; the first strip never has 0 and the last never 1. Index of the partner among the 32768 points of the neighbour strip in the same along-track block. `tile_knot`: segment number within the tile's along-track block of 128 segments. `covariance`: each point's six entries form a positive definite matrix. `positions`: coordinates in a local frame.
All inputs are finite; a program needn't handle non-finite values.
Results may differ from a plain program's by a relative error of at most 0.00014.
Values sent between devices are 32-bit elements; how exact they have to be, the bound alone decides.
No kernel may reach another device: no remote copies, remote signals or barrier semaphores. Data moves between devices by JAX's collectives and lax.ppermute only.
A program may use at most 128 MiB of HBM per device.

v0:
```python
import functools

import jax
import jax.numpy as jnp
from jax import lax
from jax.experimental import pallas as pl
from jax.experimental.pallas import tpu as pltpu
from jax.sharding import PartitionSpec as P

KNOT_DEV = 128
TILE_PTS = 128
CHANNELS = 9
BLOCK_TILES = 4
SUM_ROWS = 80

damping = 1.0

PAIRS = [(a, b) for a in range(6) for b in range(a, 6)]


def params(mebibytes=48):
    return pltpu.CompilerParams(vmem_limit_bytes=mebibytes * 2**20)


def vmem(count):
    return [pl.BlockSpec(memory_space=pltpu.VMEM)] * count


def smem(count):
    return [pl.BlockSpec(memory_space=pltpu.SMEM)] * count


def pack_kernel(pos, cov, lever, time, partner, sides, knots, table_ref, points_ref, ints, small, sems):
    tiles = time.shape[0]
    base = 14 * tiles

    def span(first, count):
        return points_ref.at[pl.ds(first * tiles, count * tiles)]

    copies = [
        pltpu.make_async_copy(pos, table_ref.at[pl.ds(0, 3)], sems.at[0]),
        pltpu.make_async_copy(cov, table_ref.at[pl.ds(3, 6)], sems.at[1]),
        pltpu.make_async_copy(partner, ints, sems.at[2]),
        pltpu.make_async_copy(sides, small.at[0], sems.at[3]),
        pltpu.make_async_copy(knots, small.at[1], sems.at[4]),
        pltpu.make_async_copy(time, span(12, 1), sems.at[5]),
    ]
    copies += [
        pltpu.make_async_copy(lever.at[c], span(9 + c, 1), sems.at[6 + c]) for c in range(3)
    ]
    for copy in copies:
        copy.start()
    for copy in copies:
        copy.wait()
    for channel in range(CHANNELS):
        points_ref[channel * tiles : (channel + 1) * tiles, :] = table_ref[channel]
    points_ref[13 * tiles : 14 * tiles, :] = ints[...].astype(jnp.float32)
    for place in range(2):
        row = base + place
        points_ref[row : row + 1, 0:tiles] = small[place].astype(jnp.float32)


def split_two(value):
    high = value.astype(jnp.bfloat16)
    low = (value - high.astype(jnp.float32)).astype(jnp.bfloat16)
    return high, low


def list_tiles(names, tiles, order_ref):
    count = len(names) * tiles
    limit = order_ref.shape[0] // 2
    first = jnp.int32(0)
    second = jnp.int32(limit)
    for tile in range(count):
        side = names[tile // tiles][0, tile % tiles]
        order_ref[first] = tile
        first = first + (side == 0.0).astype(jnp.int32)
        order_ref[second] = tile
        second = second + (side == 1.0).astype(jnp.int32)
    last_first = order_ref[jnp.maximum(first - 1, 0)]
    last_second = order_ref[jnp.maximum(second - 1, limit)]
    for extra in range(BLOCK_TILES):
        order_ref[first + extra] = last_first
        order_ref[second + extra] = last_second
    blocks = lambda number: lax.shift_right_logical(number + BLOCK_TILES - 1, 2)
    return blocks(first), blocks(second - limit), limit


def gather_kernel(groups, *refs):
    points = refs[:groups]
    tables = (refs[groups : groups + 2], refs[groups + 2 : groups + 4])
    sums_ref = refs[groups + 4]
    target, key_ref, row_ref, live_ref, knot_ref, weights, totals_ref, parts_ref, order_ref, sems = refs[
        groups + 5 : groups + 15
    ]
    names = refs[groups + 15 :]
    tiles = tables[0][0].shape[1]
    base = 14 * tiles
    copies = [
        pltpu.make_async_copy(points[p].at[pl.ds(base, 8)], names[p], sems.at[p]) for p in range(groups)
    ]
    for copy in copies:
        copy.start()

    for side in range(2):
        for place in range(2):
            for channel in range(CHANNELS):
                high, low = split_two(tables[side][place][channel])
                rows = slice(channel * tiles, (channel + 1) * tiles)
                at = place * TILE_PTS
                weights[side, rows, at : at + TILE_PTS] = high
                weights[side, rows, at + 2 * TILE_PTS : at + 3 * TILE_PTS] = low
    member = lax.axis_index("tile")
    for p in range(groups):
        index = points[p][13 * tiles : 14 * tiles, :].astype(jnp.int32)
        point_row = lax.shift_right_logical(index, 7)
        lane = index & (TILE_PTS - 1)
        key = lane
        row = jnp.full_like(index, -1)
        for place in range(2):
            offset = point_row - (member ^ place) * tiles
            inside = (offset >= 0) & (offset < tiles)
            key = jnp.where(inside, lane + place * TILE_PTS, key)
            row = jnp.where(inside, offset, row)
        key_ref[p * tiles : (p + 1) * tiles, :] = key
        row_ref[p * tiles : (p + 1) * tiles, :] = row
    target[...] = jnp.zeros_like(target)
    for copy in copies:
        copy.wait()
    for p in range(groups):
        for tile in range(tiles):
            at = p * tiles + tile
            live = (names[p][0, tile] != 2.0).astype(jnp.float32)
            live_ref[at : at + 1, :] = jnp.full((1, TILE_PTS), live, jnp.float32)
            knot_ref[at : at + 1, :] = jnp.full((1, KNOT_DEV), names[p][1, tile], jnp.float32)
    first_blocks, second_blocks, limit = list_tiles(names, tiles, order_ref)
    blocks = first_blocks + second_blocks
    queries = BLOCK_TILES * TILE_PTS

    def one_block(block):
        block = jnp.minimum(block, blocks - 1)
        later_side = block >= first_blocks
        side = later_side.astype(jnp.int32)
        start = jnp.where(later_side, limit + (block - first_blocks) * BLOCK_TILES, block * BLOCK_TILES)
        ids = [order_ref[start + j] for j in range(BLOCK_TILES)]
        keys = jnp.concatenate([key_ref[pl.ds(i, 1), :] for i in ids], axis=1)
        rows = jnp.concatenate([row_ref[pl.ds(i, 1), :] for i in ids], axis=1)
        hot = jnp.where(
            lax.broadcasted_iota(jnp.int32, (2 * TILE_PTS, queries), 0) == keys, 1.0, 0.0
        ).astype(jnp.bfloat16)
        picked = jnp.dot(
            weights[side], jnp.concatenate([hot, hot], axis=0), preferred_element_type=jnp.float32
        )
        spread_rows = jnp.broadcast_to(rows, (8, queries))
        eight = lax.broadcasted_iota(jnp.int32, (8, queries), 0)
        found = [jnp.zeros((8, queries), jnp.float32) for _ in range(CHANNELS)]
        for step in range(tiles // 8):
            here = spread_rows == eight + 8 * step
            for channel in range(CHANNELS):
                begin = channel * tiles + 8 * step
                found[channel] = jnp.where(here, picked[begin : begin + 8], found[channel])
        return ids, [jnp.sum(entry, axis=0, keepdims=True) for entry in found]

    def body(step, carry):
        results = [one_block(2 * step), one_block(2 * step + 1)]
        for ids, flat in results:
            for channel in range(CHANNELS):
                for j in range(BLOCK_TILES):
                    piece = flat[channel][:, j * TILE_PTS : (j + 1) * TILE_PTS]
                    target[channel, pl.ds(ids[j], 1), :] = piece
        return carry

    lax.fori_loop(0, lax.shift_right_logical(blocks + 1, 1), body, 0)

    totals_ref[...] = jnp.zeros_like(totals_ref)
    for p in range(groups):
        sum_points(p, tiles, points[p], target, row_ref, live_ref, knot_ref, totals_ref, parts_ref)
    for place in range(SUM_ROWS):
        if place < 75:
            rows = totals_ref[place * 8 : (place + 1) * 8, :]
            sums_ref[place : place + 1, :] = jnp.sum(rows, axis=0, keepdims=True)
        else:
            sums_ref[place : place + 1, :] = jnp.zeros((1, KNOT_DEV), jnp.float32)


def sum_points(p, tiles, points, target, row_ref, live_ref, knot_ref, totals_ref, parts_ref):
    group = 16
    ones = jnp.ones((2 * TILE_PTS, KNOT_DEV), jnp.bfloat16)

    def body(step, carry):
        begin = pl.multiple_of(step * group, group)
        span = pl.ds(pl.multiple_of(p * tiles + begin, group), group)

        def own(channel):
            return points[pl.ds(pl.multiple_of(channel * tiles + begin, group), group), :]

        live = jnp.where(row_ref[span, :] >= 0, live_ref[span, :], 0.0)
        m = [own(3 + c) + target[3 + c, span, :] for c in range(6)]
        residual = [own(c) - target[c, span, :] for c in range(3)]
        lever = [own(9 + c) for c in range(3)]
        later = own(12)
        early = 1.0 - later
        adjunct = [
            m[1] * m[2] - m[5] * m[5],
            m[0] * m[2] - m[4] * m[4],
            m[0] * m[1] - m[3] * m[3],
            m[4] * m[5] - m[3] * m[2],
            m[3] * m[5] - m[4] * m[1],
            m[3] * m[4] - m[0] * m[5],
        ]
        determinant = m[0] * adjunct[0] + m[3] * adjunct[3] + m[4] * adjunct[4]
        scale = live / determinant
        inv = [entry * scale for entry in adjunct]
        info = [[inv[0], inv[3], inv[4]], [inv[3], inv[1], inv[5]], [inv[4], inv[5], inv[2]]]

        def turned(column):
            return [
                lever[1] * column[2] - lever[2] * column[1],
                lever[2] * column[0] - lever[0] * column[2],
                lever[0] * column[1] - lever[1] * column[0],
            ] + list(column)

        weighted = [turned(info[i]) for i in range(3)]
        pulled = [
            info[i][0] * residual[0] + info[i][1] * residual[1] + info[i][2] * residual[2]
            for i in range(3)
        ]
        gradient = turned(pulled)
        gram = {}
        for b in range(6):
            column = turned([weighted[i][b] for i in range(3)])
            for a in range(b + 1):
                gram[a, b] = column[a]
        both = early * later
        terms = []
        for weight in (early * early, both, later * later):
            terms += [gram[pair] * weight for pair in PAIRS]
        for weight in (early, later):
            terms += [entry * weight for entry in gradient]
        for place, term in enumerate(terms):
            rows = slice(place * group, (place + 1) * group)
            high, low = split_two(term)
            parts_ref[rows, 0:TILE_PTS] = high
            parts_ref[rows, TILE_PTS : 2 * TILE_PTS] = low
        tile_sums = jnp.dot(parts_ref[...], ones, preferred_element_type=jnp.float32)
        lanes = lax.broadcasted_iota(jnp.int32, (group, KNOT_DEV), 1).astype(jnp.float32)
        chosen = knot_ref[span, :] == lanes
        for place in range(len(terms)):
            piece = jnp.where(chosen, tile_sums[place * group : (place + 1) * group], 0.0)
            rows = slice(place * 8, (place + 1) * 8)
            totals_ref[rows, :] = totals_ref[rows, :] + piece[0:8] + piece[8:16]
        return carry

    lax.fori_loop(0, tiles // group, body, 0)


def gather_sums(points, lower, upper):
    groups = len(points)
    tiles = lower[0].shape[1]
    count = groups * tiles
    return pl.pallas_call(
        functools.partial(gather_kernel, groups),
        out_shape=jax.ShapeDtypeStruct((SUM_ROWS, KNOT_DEV), jnp.float32),
        in_specs=vmem(groups + 4),
        out_specs=pl.BlockSpec(memory_space=pltpu.VMEM),
        scratch_shapes=[
            pltpu.VMEM((CHANNELS, count, TILE_PTS), jnp.float32),
            pltpu.VMEM((count, TILE_PTS), jnp.int32),
            pltpu.VMEM((count, TILE_PTS), jnp.int32),
            pltpu.VMEM((count, TILE_PTS), jnp.float32),
            pltpu.VMEM((count, KNOT_DEV), jnp.float32),
            pltpu.VMEM((2, CHANNELS * tiles, 4 * TILE_PTS), jnp.bfloat16),
            pltpu.VMEM((75 * 8, KNOT_DEV), jnp.float32),
            pltpu.VMEM((75 * 16, 2 * TILE_PTS), jnp.bfloat16),
            pltpu.SMEM((2 * (count + 2 * BLOCK_TILES),), jnp.int32),
            pltpu.SemaphoreType.DMA((groups,)),
        ]
        + [pltpu.SMEM((8, TILE_PTS), jnp.float32) for _ in range(groups)],
        compiler_params=params(14),
    )(*points, *lower, *upper)


def cholesky(matrix):
    factor = {}
    inverse = []
    for column in range(6):
        pivot = matrix[column, column]
        for inner in range(column):
            pivot = pivot - factor[column, inner] * factor[column, inner]
        inverse.append(1.0 / jnp.sqrt(pivot))
        for row in range(column + 1, 6):
            entry = matrix[column, row]
            for inner in range(column):
                entry = entry - factor[row, inner] * factor[column, inner]
            factor[row, column] = entry * inverse[column]
    return factor, inverse


def solve(system, right_side):
    factor, inverse = system
    forward = []
    for row in range(6):
        entry = right_side[row]
        for inner in range(row):
            entry = entry - factor[row, inner] * forward[inner]
        forward.append(entry * inverse[row])
    answer = [None] * 6
    for row in reversed(range(6)):
        entry = forward[row]
        for inner in range(row + 1, 6):
            entry = entry - factor[inner, row] * answer[inner]
        answer[row] = entry * inverse[row]
    return answer


def step_kernel(segs, members, knot_ref, sums_ref, points_ref, adjusted_ref, out_ref, held, index_ref):
    tiles = knot_ref.shape[1]
    for tile in range(tiles):
        index_ref[tile : tile + 1, :] = jnp.full((1, KNOT_DEV), knot_ref[0, tile], jnp.int32)
    seg = lax.axis_index("seg")
    for place in range(3):
        wanted = seg + place - 1
        there = (wanted >= 0) & (wanted < segs)
        first = jnp.minimum(jnp.maximum(wanted, 0), segs - 1) * members
        total = sums_ref[first]
        for other in range(1, members):
            total = total + sums_ref[first + other]
        held[place * SUM_ROWS : (place + 1) * SUM_ROWS, :] = jnp.where(there, total, 0.0)
    for place in range(3, 8):
        held[place * SUM_ROWS : (place + 1) * SUM_ROWS, :] = jnp.zeros(
            (SUM_ROWS, KNOT_DEV), jnp.float32
        )
    shape = (8, KNOT_DEV)
    lanes = lax.broadcasted_iota(jnp.int32, shape, 1)
    rows = lax.broadcasted_iota(jnp.int32, shape, 0)

    def earlier(value):
        turned = pltpu.roll(value, 1, 1)
        return jnp.where(lanes == 0, pltpu.roll(turned, 1, 0), turned)

    def following(value):
        turned = pltpu.roll(value, KNOT_DEV - 1, 1)
        return jnp.where(lanes == KNOT_DEV - 1, pltpu.roll(turned, 7, 0), turned)

    def quantity(place):
        return held[pl.ds(place, 8, stride=SUM_ROWS), :]

    pair_place = {pair: place for place, pair in enumerate(PAIRS)}
    matrix, cross, cross_before = {}, {}, {}
    for pair, place in pair_place.items():
        value = quantity(place) + earlier(quantity(42 + place))
        matrix[pair] = value + damping if pair[0] == pair[1] else value
        cross[pair] = quantity(21 + place)
        cross_before[pair] = earlier(cross[pair])
    right_side = [quantity(63 + a) + earlier(quantity(69 + a)) for a in range(6)]
    system = cholesky(matrix)
    beyond = (rows >= 2) & (seg == segs - 1)
    first = [jnp.where(beyond, 0.0, -entry) for entry in solve(system, right_side)]
    before = [earlier(entry) for entry in first]
    after = [following(entry) for entry in first]
    corrected = []
    for a in range(6):
        total = right_side[a]
        for b in range(6):
            pair = (min(a, b), max(a, b))
            total = total + cross_before[pair] * before[b] + cross[pair] * after[b]
        corrected.append(total)
    second = [jnp.where(beyond, 0.0, -entry) for entry in solve(system, corrected)]
    upper = [following(entry) for entry in second]
    for a in range(6):
        out_ref[a] = second[a][1:2]
    low_rows = [jnp.broadcast_to(second[a][1:2], shape) for a in range(6)]
    high_rows = [jnp.broadcast_to(upper[a][1:2], shape) for a in range(6)]
    for begin in range(0, tiles, 8):
        span = slice(begin, begin + 8)
        knots = index_ref[span, :]
        later = points_ref[12 * tiles + begin : 12 * tiles + begin + 8, :]
        early = 1.0 - later
        pose = []
        for a in range(6):
            low = jnp.take_along_axis(low_rows[a], knots, axis=1, mode="promise_in_bounds")
            high = jnp.take_along_axis(high_rows[a], knots, axis=1, mode="promise_in_bounds")
            pose.append(early * low + later * high)
        lever = [
            points_ref[c * tiles + begin : c * tiles + begin + 8, :] for c in range(9, 12)
        ]
        moved = [
            pose[1] * lever[2] - pose[2] * lever[1] + pose[3],
            pose[2] * lever[0] - pose[0] * lever[2] + pose[4],
            pose[0] * lever[1] - pose[1] * lever[0] + pose[5],
        ]
        for c in range(3):
            coords = points_ref[c * tiles + begin : c * tiles + begin + 8, :]
            adjusted_ref[c, span, :] = coords + moved[c]


def local(positions, lever_arm, spline_time, covariance, partner, partner_side, tile_knot):
    tiles = positions.shape[2] // TILE_PTS
    strips = lax.axis_size("strip")
    members = lax.axis_size("tile")
    segs = lax.axis_size("seg")

    table, points = pl.pallas_call(
        pack_kernel,
        out_shape=(
            jax.ShapeDtypeStruct((CHANNELS, tiles, TILE_PTS), jnp.float32),
            jax.ShapeDtypeStruct((14 * tiles + 8, TILE_PTS), jnp.float32),
        ),
        in_specs=[pl.BlockSpec(memory_space=pltpu.HBM)] * 7,
        out_specs=(pl.BlockSpec(memory_space=pltpu.VMEM),) * 2,
        scratch_shapes=[
            pltpu.VMEM((tiles, TILE_PTS), jnp.int32),
            pltpu.VMEM((2, 1, tiles), jnp.int32),
            pltpu.SemaphoreType.DMA((9,)),
        ],
        compiler_params=params(63),
    )(
        positions.reshape(3, tiles, TILE_PTS),
        covariance.reshape(6, tiles, TILE_PTS),
        lever_arm.reshape(3, tiles, TILE_PTS),
        spline_time.reshape(tiles, TILE_PTS),
        partner.reshape(tiles, TILE_PTS),
        partner_side,
        tile_knot,
    )

    below = lax.ppermute(table, "strip", [(i, i + 1) for i in range(strips - 1)])
    above = lax.ppermute(table, "strip", [(i + 1, i) for i in range(strips - 1)])
    worked = [points]
    for hop in range(2, members, 2):
        pairs = [((member + hop) % members, member) for member in range(members)]
        worked.append(lax.ppermute(points, "tile", pairs))
    swap = [(member, member ^ 1) for member in range(members)]
    lower = [below, lax.ppermute(below, "tile", swap)]
    upper = [above, lax.ppermute(above, "tile", swap)]
    sums = gather_sums(worked, lower, upper)
    all_sums = lax.all_gather(sums, ("seg", "tile"), axis=0)
    adjusted, corrections = pl.pallas_call(
        functools.partial(step_kernel, segs, members),
        out_shape=(
            jax.ShapeDtypeStruct((3, tiles, TILE_PTS), jnp.float32),
            jax.ShapeDtypeStruct((6, 1, KNOT_DEV), jnp.float32),
        ),
        in_specs=smem(1) + vmem(2),
        out_specs=(pl.BlockSpec(memory_space=pltpu.VMEM),) * 2,
        scratch_shapes=[
            pltpu.VMEM((8 * SUM_ROWS, KNOT_DEV), jnp.float32),
            pltpu.VMEM((tiles, KNOT_DEV), jnp.int32),
        ],
        compiler_params=params(6),
    )(tile_knot, all_sums, points)
    return adjusted.reshape(positions.shape), corrections.reshape(1, 6, KNOT_DEV)


def solution(mesh):
    in_specs = (
        P("strip", None, ("seg", "tile")),
        P("strip", None, ("seg", "tile")),
        P("strip", ("seg", "tile")),
        P("strip", None, ("seg", "tile")),
        P("strip", ("seg", "tile")),
        P("strip", ("seg", "tile")),
        P("strip", ("seg", "tile")),
    )
    out_specs = (P("strip", None, ("seg", "tile")), P("strip", None, "seg"))
    return jax.shard_map(local, mesh=mesh, in_specs=in_specs, out_specs=out_specs, check_vma=False)
```

profile of v0, /device:TPU:0, one launch (start us, length us, event | category | flops | bytes accessed | tf_op | source)
XLA Modules:
  0.0 49.1 jit_solution(5106985550405142675)
XLA Ops:
  0.6 2.0 %shard_map.86 = (f32[9,64,128]{2,1,0:T(8,128)}, f32[904,128]{1,0:T(8,128)}) custom-call(f32[3,64,128]{2,1,0:T(8,128)} %bitcast.10, f32[6,64,128]{2,1,0:T(8,128)} %bitcast.9, f32[3,64,128]{2,1,0:T(8,128)} %bitcast.11, f32[64,128]{1,0:T(8,128)} %bitcast.12, s32[64,128]{1,0:T(8,128)} %bitcast.13, s32[1,64]{1,0:T(1,128)} %sides.1, s32[1,64]{1,0:T(1,128)} %knot_ref.1), custom_call_target="tpu_custom_call" | custom-call | tf_op jit(solution)/shard_map/pallas_call | solution.py:403
  2.6 1.3 %collective-permute-start.3 = (f32[9,64,128]{2,1,0:T(8,128)}, f32[9,64,128]{2,1,0:T(8,128)S(1)}, u32[]{:S(2)}, u32[]{:S(2)}) collective-permute-start(f32[9,64,128]{2,1,0:T(8,128)} %get-tuple-element.7), channel_id=1, source_target_pairs={{4,0},{8,4},{12,8},{5,1},{9,5},{13,9},{6,2},{10,6},{14,10},{7,3},{... | collective-permute-start | bytes 884744 | tf_op jit(solution)/shard_map/ppermute | solution.py:428
  3.9 5.6 %collective-permute-start.1 = (f32[9,64,128]{2,1,0:T(8,128)}, f32[9,64,128]{2,1,0:T(8,128)S(1)}, u32[]{:S(2)}, u32[]{:S(2)}) collective-permute-start(f32[9,64,128]{2,1,0:T(8,128)} %get-tuple-element.7), channel_id=1, source_target_pairs={{0,4},{4,8},{8,12},{1,5},{5,9},{9,13},{2,6},{6,10},{10,14},{3,7},{... | collective-permute-start | bytes 884744 | tf_op jit(solution)/shard_map/ppermute | solution.py:427
  9.5 2.0 %collective-permute-start = (f32[904,128]{1,0:T(8,128)}, f32[904,128]{1,0:T(8,128)S(1)}, u32[]{:S(2)}, u32[]{:S(2)}) collective-permute-start(f32[904,128]{1,0:T(8,128)} %get-tuple-element.6.refs_0_.points_ref), channel_id=1, source_target_pairs={{2,0},{3,1},{0,2},{1,3},{6,4},{7,5},{4,6},{5,7},{10,8},{11,9},{8,1... | collective-permute-start | bytes 1388552 | tf_op jit(solution)/shard_map/ppermute | solution.py:432
  11.5 3.3 %collective-permute-done.3.refs_4_ = f32[9,64,128]{2,1,0:T(8,128)S(1)} collective-permute-done((f32[9,64,128]{2,1,0:T(8,128)}, f32[9,64,128]{2,1,0:T(8,128)S(1)}, u32[]{:S(2)}, u32[]{:S(2)}) %collective-permute-start.3) | collective-permute-done | bytes 294944 | tf_op jit(solution)/shard_map/ppermute | solution.py:428
  14.8 0.0 collective-permute-start.4
  14.8 1.3 %collective-permute-done.1.refs_2_ = f32[9,64,128]{2,1,0:T(8,128)S(1)} collective-permute-done((f32[9,64,128]{2,1,0:T(8,128)}, f32[9,64,128]{2,1,0:T(8,128)S(1)}, u32[]{:S(2)}, u32[]{:S(2)}) %collective-permute-start.1) | collective-permute-done | bytes 294944 | tf_op jit(solution)/shard_map/ppermute | solution.py:427
  16.0 0.0 collective-permute-start.2
  16.1 5.8 %collective-permute-done.refs_1_ = f32[904,128]{1,0:T(8,128)S(1)} collective-permute-done((f32[904,128]{1,0:T(8,128)}, f32[904,128]{1,0:T(8,128)S(1)}, u32[]{:S(2)}, u32[]{:S(2)}) %collective-permute-start) | collective-permute-done | bytes 462880 | tf_op jit(solution)/shard_map/ppermute | solution.py:432
  21.8 0.0 collective-permute-done.4.refs_5_
  21.8 0.0 collective-permute-done.2.refs_3_
  21.9 0.0 copy-start
  21.9 1.0 %copy-done = f32[904,128]{1,0:T(8,128)S(1)} copy-done((f32[904,128]{1,0:T(8,128)S(1)}, f32[904,128]{1,0:T(8,128)}, u32[]{:S(2)}) %copy-start) | copy-done | bytes 462872
  22.9 13.3 %shard_map.87 = f32[80,128]{1,0:T(8,128)S(1)} custom-call(f32[904,128]{1,0:T(8,128)S(1)} %copy-done, f32[904,128]{1,0:T(8,128)S(1)} %collective-permute-done.refs_1_, f32[9,64,128]{2,1,0:T(8,128)S(1)} %collective-permute-done.1.refs_2_, f32[9,64,128]{2,1,0:T(8,128)S(1)} %collective-permute-done.2.refs_3_, f32[9,64,128]{2,1,0:T(8,128)S(1)} %collective-permute-done.3.refs_4_, ...), custom_call_target="tpu_custom_call" | custom-call | tf_op jit(solution)/shard_map/pallas_call | solution.py:261
  36.2 10.4 %all-gather = f32[640,128]{1,0:T(8,128)S(1)} all-gather(f32[80,128]{1,0:T(8,128)S(1)} %shard_map.87), channel_id=2, replica_groups=mesh['seg'=2,'strip'=4,'tile'=4] {'seg','tile'}, dimensions={0}, use_global_device_ids=true | all-gather | bytes 368640 | tf_op jit(solution)/shard_map/all_gather | solution.py:437
  46.6 0.0 copy-start.1
  46.6 0.7 %copy-done.1 = s32[1,64]{1,0:T(1,128)S(1)} copy-done((s32[1,64]{1,0:T(1,128)S(1)}, s32[1,64]{1,0:T(1,128)}, u32[]{:S(2)}) %copy-start.1) | copy-done | bytes 280
  47.3 1.8 %shard_map.88 = (f32[3,64,128]{2,1,0:T(8,128)}, f32[6,1,128]{2,1,0:T(1,128)}) custom-call(s32[1,64]{1,0:T(1,128)S(1)} %copy-done.1, f32[8,80,128]{2,1,0:T(8,128)S(1)} %bitcast.8, f32[904,128]{1,0:T(8,128)S(1)} %copy-done), custom_call_target="tpu_custom_call" | custom-call | tf_op jit(solution)/shard_map/pallas_call | solution.py:438
Async XLA Ops:
  2.6 12.1 %collective-permute-start.3 = (f32[9,64,128]{2,1,0:T(8,128)}, f32[9,64,128]{2,1,0:T(8,128)S(1)}, u32[]{:S(2)}, u32[]{:S(2)}) collective-permute-start(f32[9,64,128]{2,1,0:T(8,128)} %get-tuple-element.7), channel_id=1, source_target_pairs={{4,0},{8,4},{12,8},{5,1},{9,5},{13,9},{6,2},{10,6},{14,10},{7,3},{... | collective-permute-start | bytes 884744 | tf_op jit(solution)/shard_map/ppermute | solution.py:428
  3.9 12.1 %collective-permute-start.1 = (f32[9,64,128]{2,1,0:T(8,128)}, f32[9,64,128]{2,1,0:T(8,128)S(1)}, u32[]{:S(2)}, u32[]{:S(2)}) collective-permute-start(f32[9,64,128]{2,1,0:T(8,128)} %get-tuple-element.7), channel_id=1, source_target_pairs={{0,4},{4,8},{8,12},{1,5},{5,9},{9,13},{2,6},{6,10},{10,14},{3,7},{... | collective-permute-start | bytes 884744 | tf_op jit(solution)/shard_map/ppermute | solution.py:427
  9.5 12.3 %collective-permute-start = (f32[904,128]{1,0:T(8,128)}, f32[904,128]{1,0:T(8,128)S(1)}, u32[]{:S(2)}, u32[]{:S(2)}) collective-permute-start(f32[904,128]{1,0:T(8,128)} %get-tuple-element.6.refs_0_.points_ref), channel_id=1, source_target_pairs={{2,0},{3,1},{0,2},{1,3},{6,4},{7,5},{4,6},{5,7},{10,8},{11,9},{8,1... | collective-permute-start | bytes 1388552 | tf_op jit(solution)/shard_map/ppermute | solution.py:432
  14.8 7.1 %collective-permute-start.4 = (f32[9,64,128]{2,1,0:T(8,128)S(1)}, f32[9,64,128]{2,1,0:T(8,128)S(1)}, u32[]{:S(2)}, u32[]{:S(2)}) collective-permute-start(f32[9,64,128]{2,1,0:T(8,128)S(1)} %collective-permute-done.3.refs_4_), channel_id=1, source_target_pairs={{0,1},{1,0},{2,3},{3,2},{4,5},{5,4},{6,7},{7,6},{8,9},{9,8},{10,11... | collective-permute-start | bytes 884744 | tf_op jit(solution)/shard_map/ppermute | solution.py:435
  16.0 5.8 %collective-permute-start.2 = (f32[9,64,128]{2,1,0:T(8,128)S(1)}, f32[9,64,128]{2,1,0:T(8,128)S(1)}, u32[]{:S(2)}, u32[]{:S(2)}) collective-permute-start(f32[9,64,128]{2,1,0:T(8,128)S(1)} %collective-permute-done.1.refs_2_), channel_id=1, source_target_pairs={{0,1},{1,0},{2,3},{3,2},{4,5},{5,4},{6,7},{7,6},{8,9},{9,8},{10,11... | collective-permute-start | bytes 884744 | tf_op jit(solution)/shard_map/ppermute | solution.py:434
  21.9 1.0 %copy-start = (f32[904,128]{1,0:T(8,128)S(1)}, f32[904,128]{1,0:T(8,128)}, u32[]{:S(2)}) copy-start(f32[904,128]{1,0:T(8,128)} %get-tuple-element.6.refs_0_.points_ref) | copy-start | bytes 1388548
  46.6 0.7 %copy-start.1 = (s32[1,64]{1,0:T(1,128)S(1)}, s32[1,64]{1,0:T(1,128)}, u32[]{:S(2)}) copy-start(s32[1,64]{1,0:T(1,128)} %knot_ref.1) | copy-start | bytes 772
where the time goes:
time: 49.3 us; the launch traced here: 49.1 us
  Pallas kernels  17.1 us (35%)
  blocking collectives  10.4 us (21%)
  waiting for transfers between devices  10.3 us (21%)
  starting transfers between devices  8.86 us (18%)
  local copies, waits for them, and re-layouts  1.67 us (3%)
  between operations  0.67 us (1%)
    pallas_call x1, Pallas kernels, gather_sums(): pl.pallas_call(functools.partial(gather_kernel, groups), out_shape=jax.Sh...  13.3 us
    all_gather x1, blocking collectives, local(): all_sums = lax.all_gather(sums, ('seg', 'tile'), axis=0)  10.4 us
    ppermute x1, waiting for transfers between devices, local(): worked.append(lax.ppermute(points, 'tile', pairs))  5.79 us
    ppermute x1, starting transfers between devices, local(): lax.ppermute(table, 'strip', [(i, i + 1) for i in range(strips - 1)])  5.57 us
    ppermute x1, waiting for transfers between devices, local(): lax.ppermute(table, 'strip', [(i + 1, i) for i in range(strips - 1)])  3.27 us
    ppermute x1, starting transfers between devices, local(): worked.append(lax.ppermute(points, 'tile', pairs))  1.99 us
    pallas_call x1, Pallas kernels, local(): pl.pallas_call(pack_kernel, out_shape=(jax.ShapeDtypeStruct((CHANNELS, ti...  1.98 us
    pallas_call x1, Pallas kernels, local(): pl.pallas_call(functools.partial(step_kernel, segs, members), out_shape=(...  1.83 us
  transfers between devices with their start and end apart: 5, of which 3 were waited for; matrix products, arithmetic and copies ran while one was open for 0% of the time, Pallas kernels for 0%

commit v1 on v0

--- a/solution.py
+++ b/solution.py
@@ -66,52 +66,92 @@
     return high, low
 
 
-def list_tiles(names, tiles, order_ref):
+def list_tiles(names, tiles, order_ref, sides):
     count = len(names) * tiles
-    limit = order_ref.shape[0] // 2
-    first = jnp.int32(0)
-    second = jnp.int32(limit)
+    room = order_ref.shape[0] // len(sides)
+    starts = [jnp.int32(place * room) for place in range(len(sides))]
+    ends = list(starts)
     for tile in range(count):
         side = names[tile // tiles][0, tile % tiles]
-        order_ref[first] = tile
-        first = first + (side == 0.0).astype(jnp.int32)
-        order_ref[second] = tile
-        second = second + (side == 1.0).astype(jnp.int32)
-    last_first = order_ref[jnp.maximum(first - 1, 0)]
-    last_second = order_ref[jnp.maximum(second - 1, limit)]
-    for extra in range(BLOCK_TILES):
-        order_ref[first + extra] = last_first
-        order_ref[second + extra] = last_second
-    blocks = lambda number: lax.shift_right_logical(number + BLOCK_TILES - 1, 2)
-    return blocks(first), blocks(second - limit), limit
-
-
-def gather_kernel(groups, *refs):
+        for place in range(len(sides)):
+            order_ref[ends[place]] = tile
+            ends[place] = ends[place] + (side == sides[place]).astype(jnp.int32)
+    blocks = []
+    for start, end in zip(starts, ends):
+        last = order_ref[jnp.maximum(end - 1, start)]
+        for extra in range(BLOCK_TILES):
+            order_ref[end + extra] = last
+        blocks.append(lax.shift_right_logical(end - start + BLOCK_TILES - 1, 2))
+    return blocks, room
+
+
+def weigh_tables(tables, weights, slot):
+    tiles = tables[0].shape[1]
+    for place in range(2):
+        for channel in range(CHANNELS):
+            high, low = split_two(tables[place][channel])
+            rows = slice(channel * tiles, (channel + 1) * tiles)
+            at = place * TILE_PTS
+            weights[slot, rows, at : at + TILE_PTS] = high
+            weights[slot, rows, at + 2 * TILE_PTS : at + 3 * TILE_PTS] = low
+
+
+def near_kernel(points, first, second, weights, target, *work):
+    picking = start_picks((points,), work)
+    weigh_tables((first, second), weights, 0)
+    target[...] = jnp.zeros_like(target)
+    picks((points,), weights, (0,), target, picking, work)
+
+
+def far_kernel(points, first, second, near_weights, found, weights, totals_ref, *work):
+    target, live_ref, knot_ref, parts_ref = work[:4]
+    work = work[4:]
+    picking = start_picks((points,), work)
+    weights[0] = near_weights[0]
+    weigh_tables((first, second), weights, 1)
+    target[...] = found[...]
+    picks((points,), weights, (1,), target, picking, work)
+    add_points((points,), target, work, live_ref, knot_ref, totals_ref, parts_ref)
+
+
+def other_kernel(groups, *refs):
     points = refs[:groups]
-    tables = (refs[groups : groups + 2], refs[groups + 2 : groups + 4])
-    sums_ref = refs[groups + 4]
-    target, key_ref, row_ref, live_ref, knot_ref, weights, totals_ref, parts_ref, order_ref, sems = refs[
-        groups + 5 : groups + 15
-    ]
-    names = refs[groups + 15 :]
-    tiles = tables[0][0].shape[1]
-    base = 14 * tiles
+    weights, before_ref, sums_ref, totals_ref = refs[groups : groups + 4]
+    target, live_ref, knot_ref, parts_ref = refs[groups + 4 : groups + 8]
+    work = refs[groups + 8 :]
+    picking = start_picks(points, work)
+    target[...] = jnp.zeros_like(target)
+    picks(points, weights, (0, 1), target, picking, work)
+    add_points(points, target, work, live_ref, knot_ref, totals_ref, parts_ref)
+    for place in range(SUM_ROWS):
+        if place < 75:
+            rows = slice(place * 8, (place + 1) * 8)
+            value = totals_ref[rows, :] + before_ref[rows, :]
+            sums_ref[place : place + 1, :] = jnp.sum(value, axis=0, keepdims=True)
+        else:
+            sums_ref[place : place + 1, :] = jnp.zeros((1, KNOT_DEV), jnp.float32)
+
+
+def start_picks(points, work):
+    sems, names = work[3], work[4:]
+    base = points[0].shape[0] - 8
     copies = [
-        pltpu.make_async_copy(points[p].at[pl.ds(base, 8)], names[p], sems.at[p]) for p in range(groups)
+        pltpu.make_async_copy(points[p].at[pl.ds(base, 8)], names[p], sems.at[p])
+        for p in range(len(points))
     ]
     for copy in copies:
         copy.start()
-
-    for side in range(2):
-        for place in range(2):
-            for channel in range(CHANNELS):
-                high, low = split_two(tables[side][place][channel])
-                rows = slice(channel * tiles, (channel + 1) * tiles)
-                at = place * TILE_PTS
-                weights[side, rows, at : at + TILE_PTS] = high
-                weights[side, rows, at + 2 * TILE_PTS : at + 3 * TILE_PTS] = low
+    return copies
+
+
+def picks(points, weights, slots, target, copies, work):
+    key_ref, row_ref, order_ref = work[:3]
+    names = work[4:]
+    tiles = weights.shape[1] // CHANNELS
     member = lax.axis_index("tile")
-    for p in range(groups):
+    near = jnp.where(lax.axis_index("strip") % 2 == 1, 0.0, 1.0)
+    sides = [(near, 1.0 - near)[slot] for slot in slots]
+    for p in range(len(points)):
         index = points[p][13 * tiles : 14 * tiles, :].astype(jnp.int32)
         point_row = lax.shift_right_logical(index, 7)
         lane = index & (TILE_PTS - 1)
@@ -124,24 +164,21 @@
             row = jnp.where(inside, offset, row)
         key_ref[p * tiles : (p + 1) * tiles, :] = key
         row_ref[p * tiles : (p + 1) * tiles, :] = row
-    target[...] = jnp.zeros_like(target)
     for copy in copies:
         copy.wait()
-    for p in range(groups):
-        for tile in range(tiles):
-            at = p * tiles + tile
-            live = (names[p][0, tile] != 2.0).astype(jnp.float32)
-            live_ref[at : at + 1, :] = jnp.full((1, TILE_PTS), live, jnp.float32)
-            knot_ref[at : at + 1, :] = jnp.full((1, KNOT_DEV), names[p][1, tile], jnp.float32)
-    first_blocks, second_blocks, limit = list_tiles(names, tiles, order_ref)
-    blocks = first_blocks + second_blocks
+    counts, room = list_tiles(names, tiles, order_ref, sides)
+    blocks = sum(counts)
     queries = BLOCK_TILES * TILE_PTS
 
     def one_block(block):
         block = jnp.minimum(block, blocks - 1)
-        later_side = block >= first_blocks
-        side = later_side.astype(jnp.int32)
-        start = jnp.where(later_side, limit + (block - first_blocks) * BLOCK_TILES, block * BLOCK_TILES)
+        if len(slots) == 1:
+            slot = slots[0]
+            start = block * BLOCK_TILES
+        else:
+            second = block >= counts[0]
+            slot = second.astype(jnp.int32)
+            start = jnp.where(second, room + (block - counts[0]) * BLOCK_TILES, block * BLOCK_TILES)
         ids = [order_ref[start + j] for j in range(BLOCK_TILES)]
         keys = jnp.concatenate([key_ref[pl.ds(i, 1), :] for i in ids], axis=1)
         rows = jnp.concatenate([row_ref[pl.ds(i, 1), :] for i in ids], axis=1)
@@ -149,7 +186,7 @@
             lax.broadcasted_iota(jnp.int32, (2 * TILE_PTS, queries), 0) == keys, 1.0, 0.0
         ).astype(jnp.bfloat16)
         picked = jnp.dot(
-            weights[side], jnp.concatenate([hot, hot], axis=0), preferred_element_type=jnp.float32
+            weights[slot], jnp.concatenate([hot, hot], axis=0), preferred_element_type=jnp.float32
         )
         spread_rows = jnp.broadcast_to(rows, (8, queries))
         eight = lax.broadcasted_iota(jnp.int32, (8, queries), 0)
@@ -172,15 +209,19 @@
 
     lax.fori_loop(0, lax.shift_right_logical(blocks + 1, 1), body, 0)
 
+
+def add_points(points, target, work, live_ref, knot_ref, totals_ref, parts_ref):
+    row_ref, names = work[1], work[4:]
+    tiles = target.shape[1] // len(points)
+    for p in range(len(points)):
+        for tile in range(tiles):
+            at = p * tiles + tile
+            live = (names[p][0, tile] != 2.0).astype(jnp.float32)
+            live_ref[at : at + 1, :] = jnp.full((1, TILE_PTS), live, jnp.float32)
+            knot_ref[at : at + 1, :] = jnp.full((1, KNOT_DEV), names[p][1, tile], jnp.float32)
     totals_ref[...] = jnp.zeros_like(totals_ref)
-    for p in range(groups):
+    for p in range(len(points)):
         sum_points(p, tiles, points[p], target, row_ref, live_ref, knot_ref, totals_ref, parts_ref)
-    for place in range(SUM_ROWS):
-        if place < 75:
-            rows = totals_ref[place * 8 : (place + 1) * 8, :]
-            sums_ref[place : place + 1, :] = jnp.sum(rows, axis=0, keepdims=True)
-        else:
-            sums_ref[place : place + 1, :] = jnp.zeros((1, KNOT_DEV), jnp.float32)
 
 
 def sum_points(p, tiles, points, target, row_ref, live_ref, knot_ref, totals_ref, parts_ref):
@@ -254,30 +295,68 @@
     lax.fori_loop(0, tiles // group, body, 0)
 
 
-def gather_sums(points, lower, upper):
+def work_shapes(groups, tiles, slots, adding):
+    count = groups * tiles
+    found = [
+        pltpu.VMEM((CHANNELS, count, TILE_PTS), jnp.float32),
+        pltpu.VMEM((count, TILE_PTS), jnp.float32),
+        pltpu.VMEM((count, KNOT_DEV), jnp.float32),
+        pltpu.VMEM((75 * 16, 2 * TILE_PTS), jnp.bfloat16),
+    ]
+    picked = [
+        pltpu.VMEM((count, TILE_PTS), jnp.int32),
+        pltpu.VMEM((count, TILE_PTS), jnp.int32),
+        pltpu.SMEM((slots * (count + 2 * BLOCK_TILES),), jnp.int32),
+        pltpu.SemaphoreType.DMA((groups,)),
+    ] + [pltpu.SMEM((8, TILE_PTS), jnp.float32) for _ in range(groups)]
+    return found + picked if adding else picked
+
+
+def weight_shape(slots, tiles):
+    return jax.ShapeDtypeStruct((slots, CHANNELS * tiles, 4 * TILE_PTS), jnp.bfloat16)
+
+
+def near_picks(points, near):
+    tiles = near[0].shape[1]
+    return pl.pallas_call(
+        near_kernel,
+        out_shape=(
+            weight_shape(1, tiles),
+            jax.ShapeDtypeStruct((CHANNELS, tiles, TILE_PTS), jnp.float32),
+        ),
+        in_specs=vmem(3),
+        out_specs=(pl.BlockSpec(memory_space=pltpu.VMEM),) * 2,
+        scratch_shapes=work_shapes(1, tiles, 1, False),
+        compiler_params=params(14),
+    )(points, *near)
+
+
+def own_totals(points, far, weights, found):
+    tiles = far[0].shape[1]
+    return pl.pallas_call(
+        far_kernel,
+        out_shape=(
+            weight_shape(2, tiles),
+            jax.ShapeDtypeStruct((75 * 8, KNOT_DEV), jnp.float32),
+        ),
+        in_specs=vmem(5),
+        out_specs=(pl.BlockSpec(memory_space=pltpu.VMEM),) * 2,
+        scratch_shapes=work_shapes(1, tiles, 1, True),
+        compiler_params=params(14),
+    )(points, *far, weights, found)
+
+
+def all_totals(points, weights, totals):
     groups = len(points)
-    tiles = lower[0].shape[1]
-    count = groups * tiles
+    tiles = weights.shape[1] // CHANNELS
     return pl.pallas_call(
-        functools.partial(gather_kernel, groups),
+        functools.partial(other_kernel, groups),
         out_shape=jax.ShapeDtypeStruct((SUM_ROWS, KNOT_DEV), jnp.float32),
-        in_specs=vmem(groups + 4),
+        in_specs=vmem(groups + 2),
         out_specs=pl.BlockSpec(memory_space=pltpu.VMEM),
-        scratch_shapes=[
-            pltpu.VMEM((CHANNELS, count, TILE_PTS), jnp.float32),
-            pltpu.VMEM((count, TILE_PTS), jnp.int32),
-            pltpu.VMEM((count, TILE_PTS), jnp.int32),
-            pltpu.VMEM((count, TILE_PTS), jnp.float32),
-            pltpu.VMEM((count, KNOT_DEV), jnp.float32),
-            pltpu.VMEM((2, CHANNELS * tiles, 4 * TILE_PTS), jnp.bfloat16),
-            pltpu.VMEM((75 * 8, KNOT_DEV), jnp.float32),
-            pltpu.VMEM((75 * 16, 2 * TILE_PTS), jnp.bfloat16),
-            pltpu.SMEM((2 * (count + 2 * BLOCK_TILES),), jnp.int32),
-            pltpu.SemaphoreType.DMA((groups,)),
-        ]
-        + [pltpu.SMEM((8, TILE_PTS), jnp.float32) for _ in range(groups)],
+        scratch_shapes=[pltpu.VMEM((75 * 8, KNOT_DEV), jnp.float32)] + work_shapes(groups, tiles, 2, True),
         compiler_params=params(14),
-    )(*points, *lower, *upper)
+    )(*points, weights, totals)
 
 
 def cholesky(matrix):
@@ -413,27 +492,39 @@
             pltpu.VMEM((2, 1, tiles), jnp.int32),
             pltpu.SemaphoreType.DMA((9,)),
         ],
-        compiler_params=params(63),
+        compiler_params=params(14),
     )(
-        positions.reshape(3, tiles, TILE_PTS),
-        covariance.reshape(6, tiles, TILE_PTS),
-        lever_arm.reshape(3, tiles, TILE_PTS),
-        spline_time.reshape(tiles, TILE_PTS),
-        partner.reshape(tiles, TILE_PTS),
-        partner_side,
-        tile_knot,
+        *[
+            pltpu.with_memory_space_constraint(array, pltpu.HBM)
+            for array in (
+                positions.reshape(3, tiles, TILE_PTS),
+                covariance.reshape(6, tiles, TILE_PTS),
+                lever_arm.reshape(3, tiles, TILE_PTS),
+                spline_time.reshape(tiles, TILE_PTS),
+                partner.reshape(tiles, TILE_PTS),
+                partner_side,
+                tile_knot,
+            )
+        ]
     )
 
-    below = lax.ppermute(table, "strip", [(i, i + 1) for i in range(strips - 1)])
-    above = lax.ppermute(table, "strip", [(i + 1, i) for i in range(strips - 1)])
-    worked = [points]
+    def trade(first):
+        pairs = []
+        for strip in range(first, strips - 1, 2):
+            pairs += [(strip, strip + 1), (strip + 1, strip)]
+        return lax.ppermute(table, "strip", pairs)
+
+    near, far = trade(0), trade(1)
+    others = []
     for hop in range(2, members, 2):
         pairs = [((member + hop) % members, member) for member in range(members)]
-        worked.append(lax.ppermute(points, "tile", pairs))
+        others.append(lax.ppermute(points, "tile", pairs))
     swap = [(member, member ^ 1) for member in range(members)]
-    lower = [below, lax.ppermute(below, "tile", swap)]
-    upper = [above, lax.ppermute(above, "tile", swap)]
-    sums = gather_sums(worked, lower, upper)
+    near = [near, lax.ppermute(near, "tile", swap)]
+    far = [far, lax.ppermute(far, "tile", swap)]
+    weights, found = near_picks(points, near)
+    weights, totals = own_totals(points, far, weights, found)
+    sums = all_totals(others, weights, totals)
     all_sums = lax.all_gather(sums, ("seg", "tile"), axis=0)
     adjusted, corrections = pl.pallas_call(
         functools.partial(step_kernel, segs, members),

time: 49.3 us -> 42.5 us (0.86)
  the two profiles are of different devices: /device:TPU:0 before, /device:TPU:9 now
where the time goes in v1:
time: 42.5 us; the launch traced here: 43.3 us
  Pallas kernels  17.5 us (41%)
  blocking collectives  12.6 us (30%)
  starting transfers between devices  8.92 us (21%)
  waiting for transfers between devices  3.58 us (8%)
  between operations  0.71 us (2%)
    all_gather x1, blocking collectives, local(): all_sums = lax.all_gather(sums, ('seg', 'tile'), axis=0)  12.6 us
    pallas_call x1, Pallas kernels, all_totals(): pl.pallas_call(functools.partial(other_kernel, groups), out_shape=jax.Sha...  6.53 us
    pallas_call x1, Pallas kernels, own_totals(): pl.pallas_call(far_kernel, out_shape=(weight_shape(2, tiles), jax.ShapeDt...  5.56 us
    ppermute x2, starting transfers between devices, trade(): return lax.ppermute(table, 'strip', pairs)  4.55 us
    ppermute x2, waiting for transfers between devices, trade(): return lax.ppermute(table, 'strip', pairs)  3.58 us
    pallas_call x1, Pallas kernels, near_picks(): pl.pallas_call(near_kernel, out_shape=(weight_shape(1, tiles), jax.ShapeD...  2.43 us
    pallas_call x1, Pallas kernels, local(): pl.pallas_call(functools.partial(step_kernel, segs, members), out_shape=(...  1.83 us
    ppermute x1, starting transfers between devices, local(): near = [near, lax.ppermute(near, 'tile', swap)]  1.55 us
  transfers between devices with their start and end apart: 5, of which 2 were waited for; matrix products, arithmetic and copies ran while one was open for 0% of the time, Pallas kernels for 18%

profile of v1, /device:TPU:9, one launch (start us, length us, event | category | flops | bytes accessed | tf_op | source)
XLA Modules:
  0.0 43.3 jit_solution(11142056910767700398)
XLA Ops:
  0.6 1.1 %shard_map.86 = (f32[9,64,128]{2,1,0:T(8,128)S(1)}, f32[904,128]{1,0:T(8,128)S(1)}) custom-call(f32[3,64,128]{2,1,0:T(8,128)} %bitcast.10, f32[6,64,128]{2,1,0:T(8,128)} %bitcast.9, f32[3,64,128]{2,1,0:T(8,128)} %bitcast.11, f32[64,128]{1,0:T(8,128)} %bitcast.12, s32[64,128]{1,0:T(8,128)} %bitcast.13, s32[1,64]{1,0:T(1,128)} %sides.1, s32[1,64]{1,0:T(1,128)} %knot_ref.1), custom_call_target="tpu_custom_call" | custom-call | tf_op jit(solution)/shard_map/pallas_call | solution.py:482
  1.7 0.1 collective-permute-start.3
  1.8 4.5 %collective-permute-start.1 = (f32[9,64,128]{2,1,0:T(8,128)S(1)}, f32[9,64,128]{2,1,0:T(8,128)S(1)}, u32[]{:S(2)}, u32[]{:S(2)}) collective-permute-start(f32[9,64,128]{2,1,0:T(8,128)S(1)} %get-tuple-element.11), channel_id=1, source_target_pairs={{4,8},{8,4},{5,9},{9,5},{6,10},{10,6},{7,11},{11,7},{20,24},{24,20... | collective-permute-start | bytes 884744 | tf_op jit(solution)/shard_map/ppermute | solution.py:515
  6.3 1.3 %collective-permute-start = (f32[904,128]{1,0:T(8,128)S(1)}, f32[904,128]{1,0:T(8,128)S(1)}, u32[]{:S(2)}, u32[]{:S(2)}) collective-permute-start(f32[904,128]{1,0:T(8,128)S(1)} %get-tuple-element.10.points.points_ref), channel_id=1, source_target_pairs={{2,0},{3,1},{0,2},{1,3},{6,4},{7,5},{4,6},{5,7},{10,8},{11,9},{8,1... | collective-permute-start | bytes 1388552 | tf_op jit(solution)/shard_map/ppermute | solution.py:521
  7.6 2.1 %collective-permute-done.3.first = f32[9,64,128]{2,1,0:T(8,128)S(1)} collective-permute-done((f32[9,64,128]{2,1,0:T(8,128)S(1)}, f32[9,64,128]{2,1,0:T(8,128)S(1)}, u32[]{:S(2)}, u32[]{:S(2)}) %collective-permute-start.3) | collective-permute-done | bytes 294944 | tf_op jit(solution)/shard_map/ppermute | solution.py:515
  9.7 1.5 %collective-permute-start.4 = (f32[9,64,128]{2,1,0:T(8,128)S(1)}, f32[9,64,128]{2,1,0:T(8,128)S(1)}, u32[]{:S(2)}, u32[]{:S(2)}) collective-permute-start(f32[9,64,128]{2,1,0:T(8,128)S(1)} %collective-permute-done.3.first), channel_id=1, source_target_pairs={{0,1},{1,0},{2,3},{3,2},{4,5},{5,4},{6,7},{7,6},{8,9},{9,8},{10,11... | collective-permute-start | bytes 884744 | tf_op jit(solution)/shard_map/ppermute | solution.py:523
  11.2 1.5 %collective-permute-done.1.first = f32[9,64,128]{2,1,0:T(8,128)S(1)} collective-permute-done((f32[9,64,128]{2,1,0:T(8,128)S(1)}, f32[9,64,128]{2,1,0:T(8,128)S(1)}, u32[]{:S(2)}, u32[]{:S(2)}) %collective-permute-start.1) | collective-permute-done | bytes 294944 | tf_op jit(solution)/shard_map/ppermute | solution.py:515
  12.7 1.5 %collective-permute-start.2 = (f32[9,64,128]{2,1,0:T(8,128)S(1)}, f32[9,64,128]{2,1,0:T(8,128)S(1)}, u32[]{:S(2)}, u32[]{:S(2)}) collective-permute-start(f32[9,64,128]{2,1,0:T(8,128)S(1)} %collective-permute-done.1.first), channel_id=1, source_target_pairs={{0,1},{1,0},{2,3},{3,2},{4,5},{5,4},{6,7},{7,6},{8,9},{9,8},{10,11... | collective-permute-start | bytes 884744 | tf_op jit(solution)/shard_map/ppermute | solution.py:524
  14.2 0.0 collective-permute-done.4.second
  14.3 2.4 %shard_map.87 = (bf16[1,576,512]{2,1,0:T(8,128)(2,1)S(1)}, f32[9,64,128]{2,1,0:T(8,128)S(1)}) custom-call(f32[904,128]{1,0:T(8,128)S(1)} %get-tuple-element.10.points.points_ref, f32[9,64,128]{2,1,0:T(8,128)S(1)} %collective-permute-done.3.first, f32[9,64,128]{2,1,0:T(8,128)S(1)} %collective-permute-done.4.second), custom_call_target="tpu_custom_call" | custom-call | tf_op jit(solution)/shard_map/pallas_call | solution.py:321
  16.7 0.0 collective-permute-done.2.second
  16.7 5.6 %shard_map.88 = (bf16[2,576,512]{2,1,0:T(8,128)(2,1)S(1)}, f32[600,128]{1,0:T(8,128)S(1)}) custom-call(f32[904,128]{1,0:T(8,128)S(1)} %get-tuple-element.10.points.points_ref, f32[9,64,128]{2,1,0:T(8,128)S(1)} %collective-permute-done.1.first, f32[9,64,128]{2,1,0:T(8,128)S(1)} %collective-permute-done.2.second, ...), custom_call_target="tpu_custom_call" | custom-call | tf_op jit(solution)/shard_map/pallas_call | solution.py:336
  22.3 0.0 collective-permute-done.refs_0_
  22.3 0.0 copy-start
  22.3 6.5 %shard_map.89 = f32[80,128]{1,0:T(8,128)S(1)} custom-call(f32[904,128]{1,0:T(8,128)S(1)} %collective-permute-done.refs_0_, bf16[2,576,512]{2,1,0:T(8,128)(2,1)S(1)} %get-tuple-element.14.refs_1_, f32[600,128]{1,0:T(8,128)S(1)} %get-tuple-element.15.refs_2_), custom_call_target="tpu_custom_call" | custom-call | tf_op jit(solution)/shard_map/pallas_call | solution.py:352
  28.8 12.6 %all-gather = f32[640,128]{1,0:T(8,128)S(1)} all-gather(f32[80,128]{1,0:T(8,128)S(1)} %shard_map.89), channel_id=2, replica_groups=mesh['seg'=2,'strip'=4,'tile'=4] {'seg','tile'}, dimensions={0}, use_global_device_ids=true | all-gather | bytes 368640 | tf_op jit(solution)/shard_map/all_gather | solution.py:528
  41.4 0.0 copy-done
  41.4 1.8 %shard_map.90 = (f32[3,64,128]{2,1,0:T(8,128)}, f32[6,1,128]{2,1,0:T(1,128)}) custom-call(s32[1,64]{1,0:T(1,128)S(1)} %copy-done, f32[8,80,128]{2,1,0:T(8,128)S(1)} %bitcast.8, f32[904,128]{1,0:T(8,128)S(1)} %get-tuple-element.10.points.points_ref), custom_call_target="tpu_custom_call" | custom-call | tf_op jit(solution)/shard_map/pallas_call | solution.py:529
Async XLA Ops:
  1.7 7.9 %collective-permute-start.3 = (f32[9,64,128]{2,1,0:T(8,128)S(1)}, f32[9,64,128]{2,1,0:T(8,128)S(1)}, u32[]{:S(2)}, u32[]{:S(2)}) collective-permute-start(f32[9,64,128]{2,1,0:T(8,128)S(1)} %get-tuple-element.11), channel_id=1, source_target_pairs={{0,4},{4,0},{8,12},{12,8},{1,5},{5,1},{9,13},{13,9},{2,6},{6,2},{1... | collective-permute-start | bytes 884744 | tf_op jit(solution)/shard_map/ppermute | solution.py:515
  1.8 10.9 %collective-permute-start.1 = (f32[9,64,128]{2,1,0:T(8,128)S(1)}, f32[9,64,128]{2,1,0:T(8,128)S(1)}, u32[]{:S(2)}, u32[]{:S(2)}) collective-permute-start(f32[9,64,128]{2,1,0:T(8,128)S(1)} %get-tuple-element.11), channel_id=1, source_target_pairs={{4,8},{8,4},{5,9},{9,5},{6,10},{10,6},{7,11},{11,7},{20,24},{24,20... | collective-permute-start | bytes 884744 | tf_op jit(solution)/shard_map/ppermute | solution.py:515
  6.3 16.0 %collective-permute-start = (f32[904,128]{1,0:T(8,128)S(1)}, f32[904,128]{1,0:T(8,128)S(1)}, u32[]{:S(2)}, u32[]{:S(2)}) collective-permute-start(f32[904,128]{1,0:T(8,128)S(1)} %get-tuple-element.10.points.points_ref), channel_id=1, source_target_pairs={{2,0},{3,1},{0,2},{1,3},{6,4},{7,5},{4,6},{5,7},{10,8},{11,9},{8,1... | collective-permute-start | bytes 1388552 | tf_op jit(solution)/shard_map/ppermute | solution.py:521
  9.7 4.6 %collective-permute-start.4 = (f32[9,64,128]{2,1,0:T(8,128)S(1)}, f32[9,64,128]{2,1,0:T(8,128)S(1)}, u32[]{:S(2)}, u32[]{:S(2)}) collective-permute-start(f32[9,64,128]{2,1,0:T(8,128)S(1)} %collective-permute-done.3.first), channel_id=1, source_target_pairs={{0,1},{1,0},{2,3},{3,2},{4,5},{5,4},{6,7},{7,6},{8,9},{9,8},{10,11... | collective-permute-start | bytes 884744 | tf_op jit(solution)/shard_map/ppermute | solution.py:523
  12.7 4.0 %collective-permute-start.2 = (f32[9,64,128]{2,1,0:T(8,128)S(1)}, f32[9,64,128]{2,1,0:T(8,128)S(1)}, u32[]{:S(2)}, u32[]{:S(2)}) collective-permute-start(f32[9,64,128]{2,1,0:T(8,128)S(1)} %collective-permute-done.1.first), channel_id=1, source_target_pairs={{0,1},{1,0},{2,3},{3,2},{4,5},{5,4},{6,7},{7,6},{8,9},{9,8},{10,11... | collective-permute-start | bytes 884744 | tf_op jit(solution)/shard_map/ppermute | solution.py:524
  22.3 19.2 %copy-start = (s32[1,64]{1,0:T(1,128)S(1)}, s32[1,64]{1,0:T(1,128)}, u32[]{:S(2)}) copy-start(s32[1,64]{1,0:T(1,128)} %knot_ref.1) | copy-start | bytes 772

commit v2 on v0

v2 whole, which is shorter than its diff:
```python
import functools

import jax
import jax.numpy as jnp
from jax import lax
from jax.experimental import pallas as pl
from jax.experimental.pallas import tpu as pltpu
from jax.sharding import PartitionSpec as P

KNOT_DEV = 128
TILE_PTS = 128
CHANNELS = 9
BLOCK_TILES = 4
ROW_GROUP = 16
POINT_ROWS = 16
PARTNER = 13
KNOT = 14
SIDE = 15
VALID = 15
SUM_ROWS = 80

damping = 1.0

PAIRS = [(a, b) for a in range(6) for b in range(a, 6)]


def params(mebibytes=48):
    return pltpu.CompilerParams(vmem_limit_bytes=mebibytes * 2**20)


def vmem(count):
    return [pl.BlockSpec(memory_space=pltpu.VMEM)] * count


def smem(count):
    return [pl.BlockSpec(memory_space=pltpu.SMEM)] * count


def pack_kernel(pos, cov, lever, time, partner, sides, knots, table_ref, points_ref, ints, small, sems):
    tiles = time.shape[0]
    copies = [
        pltpu.make_async_copy(sides, small.at[0], sems.at[0]),
        pltpu.make_async_copy(knots, small.at[1], sems.at[1]),
        pltpu.make_async_copy(partner, ints, sems.at[2]),
        pltpu.make_async_copy(pos, table_ref.at[pl.ds(0, 3)], sems.at[3]),
        pltpu.make_async_copy(cov, table_ref.at[pl.ds(3, 6)], sems.at[4]),
        pltpu.make_async_copy(lever, points_ref.at[pl.ds(9, 3)], sems.at[5]),
        pltpu.make_async_copy(time, points_ref.at[12], sems.at[6]),
    ]
    for copy in copies:
        copy.start()
    for copy in copies:
        copy.wait()
    points_ref[0:CHANNELS] = table_ref[...]
    points_ref[PARTNER] = ints[...].astype(jnp.float32)
    for place, channel in ((0, SIDE), (1, KNOT)):
        for tile in range(tiles):
            value = jnp.full((1, TILE_PTS), small[place, 0, tile], jnp.int32)
            points_ref[channel, tile : tile + 1, :] = value.astype(jnp.float32)


def split_two(value):
    high = value.astype(jnp.bfloat16)
    low = (value - high.astype(jnp.float32)).astype(jnp.bfloat16)
    return high, low


def row_room(groups, tiles):
    return groups * tiles + 4 * ROW_GROUP


def arrange(points, packed, work):
    compact, numbers, counts, sems = work
    tiles = points[0].shape[1]
    upper = (
        lax.broadcasted_iota(jnp.int32, (TILE_PTS, TILE_PTS), 0)
        <= lax.broadcasted_iota(jnp.int32, (TILE_PTS, TILE_PTS), 1)
    )
    upper = jnp.where(upper, 1.0, 0.0).astype(jnp.bfloat16)
    member = lax.axis_index("tile")
    near = jnp.where(lax.axis_index("strip") % 2 == 1, 0.0, 1.0)
    copies = []
    for p, group in enumerate(points):
        index = group[PARTNER].astype(jnp.int32)
        offset = lax.shift_right_logical(index, 7) - member * tiles
        side = group[SIDE]
        wanted = (offset >= 0) & (offset < tiles) & (side != 2.0)
        marks = jnp.where(wanted, 1.0, 0.0).astype(jnp.bfloat16)
        ranks = jnp.dot(marks, upper, preferred_element_type=jnp.float32).astype(jnp.int32)
        numbers[p * tiles : (p + 1) * tiles, :] = ranks + jnp.where(side == near, 0, 256)
        span = pl.ds(p * tiles, tiles)
        copies.append(pltpu.make_async_copy(numbers.at[span], counts.at[span], sems.at[p]))
    for copy in copies:
        copy.start()
    lanes = lax.broadcasted_iota(jnp.int32, (tiles, TILE_PTS), 1)
    for p, group in enumerate(points):
        ranks = numbers[p * tiles : (p + 1) * tiles, :] & 255
        source = jnp.zeros_like(lanes)
        for jump in (64, 32, 16, 8, 4, 2, 1):
            there = jnp.take_along_axis(ranks, source + (jump - 1), axis=1, mode="promise_in_bounds")
            source = jnp.where(there <= lanes, source + jump, source)
        count = jnp.broadcast_to(ranks[:, TILE_PTS - 1 :], lanes.shape)
        for channel in range(POINT_ROWS):
            if channel == VALID:
                value = jnp.where(lanes < count, 1.0, 0.0)
            else:
                value = group[channel]
                if channel != KNOT:
                    value = jnp.take_along_axis(value, source, axis=1, mode="promise_in_bounds")
            at = p * tiles * POINT_ROWS + channel
            compact[pl.ds(at, tiles, stride=POINT_ROWS), :] = value
    for copy in copies:
        copy.wait()

    room = packed.shape[0] // POINT_ROWS
    last = room - 1
    blank = jnp.zeros((POINT_ROWS, TILE_PTS), jnp.float32)

    def rows_at(row):
        return pl.ds(pl.multiple_of(row * POINT_ROWS, POINT_ROWS), POINT_ROWS)

    packed[rows_at(0), :] = blank
    packed[rows_at(last), :] = blank
    wide = lax.broadcasted_iota(jnp.int32, (POINT_ROWS, TILE_PTS), 1)

    def place(tile, carry):
        near_row, near_start, far_row, far_start = carry
        code = counts[tile, TILE_PTS - 1]
        count = code & 255
        far = code >= 256
        row = jnp.where(far, far_row, near_row)
        start = jnp.where(far, far_start, near_start)
        full = start + count > TILE_PTS
        row = jnp.where(full, row + 1, row)
        start = jnp.where(full, 0, start)
        at = rows_at(jnp.where(far, last - row, row))
        value = pltpu.roll(compact[rows_at(tile), :], start, 1)
        packed[at, :] = jnp.where(wide >= start, value, packed[at, :])
        end = start + count
        return (
            jnp.where(far, near_row, row),
            jnp.where(far, near_start, end),
            jnp.where(far, row, far_row),
            jnp.where(far, end, far_start),
        )

    zero = jnp.int32(0)
    total = len(points) * tiles
    unroll = 8

    def several(step, carry):
        for tile in range(unroll):
            carry = place(step * unroll + tile, carry)
        return carry

    near_row, near_start, far_row, far_start = lax.fori_loop(
        0, total // unroll, several, (zero, zero, zero, zero)
    )
    near_rows = near_row + (near_start > 0).astype(jnp.int32)
    far_rows = far_row + (far_start > 0).astype(jnp.int32)
    for extra in range(ROW_GROUP):
        packed[rows_at(near_rows + extra), :] = blank
        packed[rows_at(last - far_rows - extra), :] = blank
    return near_rows, far_rows


def weigh_table(table, weights, slot):
    tiles = table.shape[1]
    for channel in range(CHANNELS):
        high, low = split_two(table[channel])
        rows = slice(channel * tiles, (channel + 1) * tiles)
        weights[slot, rows, 0:TILE_PTS] = high
        weights[slot, rows, TILE_PTS : 2 * TILE_PTS] = low


def process(packed, near_rows, far_rows, weights, totals_ref, work):
    target, key_ref, row_ref, terms_ref = work
    tiles = weights.shape[1] // CHANNELS
    room = packed.shape[0] // POINT_ROWS
    member = lax.axis_index("tile")

    def keys(step, carry):
        begin = pl.multiple_of(step * 8, 8)
        span = pl.ds(begin, 8)

        def channel(place):
            return packed[pl.ds(begin * POINT_ROWS + place, 8, stride=POINT_ROWS), :]

        index = channel(PARTNER).astype(jnp.int32)
        key_ref[span, :] = index & (TILE_PTS - 1)
        row = lax.shift_right_logical(index, 7) - member * tiles
        row_ref[span, :] = jnp.where(channel(VALID) > 0.0, row, -1)
        return carry

    lax.fori_loop(0, room // 8, keys, 0)
    target[...] = jnp.zeros_like(target)
    near_blocks = lax.shift_right_logical(near_rows + BLOCK_TILES - 1, 2)
    far_blocks = lax.shift_right_logical(far_rows + BLOCK_TILES - 1, 2)
    blocks = near_blocks + far_blocks
    queries = BLOCK_TILES * TILE_PTS

    def one_block(block):
        block = jnp.minimum(block, blocks - 1)
        far = block >= near_blocks
        slot = far.astype(jnp.int32)
        base = jnp.where(far, room - BLOCK_TILES * (block - near_blocks + 1), block * BLOCK_TILES)
        ids = [base + j for j in range(BLOCK_TILES)]
        keys = jnp.concatenate([key_ref[pl.ds(i, 1), :] for i in ids], axis=1)
        rows = jnp.concatenate([row_ref[pl.ds(i, 1), :] for i in ids], axis=1)
        hot = jnp.where(
            lax.broadcasted_iota(jnp.int32, (TILE_PTS, queries), 0) == keys, 1.0, 0.0
        ).astype(jnp.bfloat16)
        picked = jnp.dot(
            weights[slot], jnp.concatenate([hot, hot], axis=0), preferred_element_type=jnp.float32
        )
        spread_rows = jnp.broadcast_to(rows, (8, queries))
        eight = lax.broadcasted_iota(jnp.int32, (8, queries), 0)
        found = [jnp.zeros((8, queries), jnp.float32) for _ in range(CHANNELS)]
        for step in range(tiles // 8):
            here = spread_rows == eight + 8 * step
            for channel in range(CHANNELS):
                begin = channel * tiles + 8 * step
                found[channel] = jnp.where(here, picked[begin : begin + 8], found[channel])
        return ids, [jnp.sum(entry, axis=0, keepdims=True) for entry in found]

    def body(step, carry):
        results = [one_block(2 * step), one_block(2 * step + 1)]
        for ids, flat in results:
            for channel in range(CHANNELS):
                for j in range(BLOCK_TILES):
                    piece = flat[channel][:, j * TILE_PTS : (j + 1) * TILE_PTS]
                    target[channel, pl.ds(ids[j], 1), :] = piece
        return carry

    lax.fori_loop(0, lax.shift_right_logical(blocks + 1, 1), body, 0)

    totals_ref[...] = jnp.zeros_like(totals_ref)
    terms_ref[75 * ROW_GROUP :, :] = jnp.zeros((5 * ROW_GROUP, TILE_PTS), jnp.float32)
    near_groups = lax.shift_right_logical(near_rows + ROW_GROUP - 1, 4)
    far_groups = lax.shift_right_logical(far_rows + ROW_GROUP - 1, 4)

    def add(step, carry):
        far = step >= near_groups
        base = jnp.where(far, room - ROW_GROUP * (step - near_groups + 1), step * ROW_GROUP)
        add_rows(pl.multiple_of(base, ROW_GROUP), packed, target, totals_ref, terms_ref)
        return carry

    lax.fori_loop(0, near_groups + far_groups, add, 0)


def add_rows(base, packed, target, totals_ref, terms_ref):
    group = ROW_GROUP
    span = pl.ds(base, group)

    def own(channel):
        return packed[pl.ds(base * POINT_ROWS + channel, group, stride=POINT_ROWS), :]

    valid = own(VALID) > 0.0
    m = [own(3 + c) + target[3 + c, span, :] for c in range(6)]
    residual = [own(c) - target[c, span, :] for c in range(3)]
    lever = [own(9 + c) for c in range(3)]
    later = own(12)
    early = 1.0 - later
    adjunct = [
        m[1] * m[2] - m[5] * m[5],
        m[0] * m[2] - m[4] * m[4],
        m[0] * m[1] - m[3] * m[3],
        m[4] * m[5] - m[3] * m[2],
        m[3] * m[5] - m[4] * m[1],
        m[3] * m[4] - m[0] * m[5],
    ]
    determinant = m[0] * adjunct[0] + m[3] * adjunct[3] + m[4] * adjunct[4]
    scale = jnp.where(valid, 1.0 / determinant, 0.0)
    inv = [entry * scale for entry in adjunct]
    info = [[inv[0], inv[3], inv[4]], [inv[3], inv[1], inv[5]], [inv[4], inv[5], inv[2]]]

    def turned(column):
        return [
            lever[1] * column[2] - lever[2] * column[1],
            lever[2] * column[0] - lever[0] * column[2],
            lever[0] * column[1] - lever[1] * column[0],
        ] + list(column)

    weighted = [turned(info[i]) for i in range(3)]
    pulled = [
        info[i][0] * residual[0] + info[i][1] * residual[1] + info[i][2] * residual[2]
        for i in range(3)
    ]
    gradient = turned(pulled)
    gram = {}
    for b in range(6):
        column = turned([weighted[i][b] for i in range(3)])
        for a in range(b + 1):
            gram[a, b] = column[a]
    both = early * later
    terms = []
    for weight in (early * early, both, later * later):
        terms += [gram[pair] * weight for pair in PAIRS]
    for weight in (early, later):
        terms += [entry * weight for entry in gradient]
    for place, term in enumerate(terms):
        terms_ref[place * group : (place + 1) * group, :] = term
    knots = own(KNOT).astype(jnp.int32)
    stacked = lax.broadcasted_iota(jnp.int32, (KNOT_DEV, TILE_PTS), 0)
    total = totals_ref[...]
    for row in range(0, group, 2):
        parts, hots = [], []
        for r in (row, row + 1):
            high, low = split_two(terms_ref[pl.ds(r, SUM_ROWS, stride=group), :])
            parts.append(jnp.concatenate([high, low], axis=0))
            hots.append(jnp.where(stacked == knots[r : r + 1], 1.0, 0.0).astype(jnp.bfloat16))
        sums = lax.dot_general(
            jnp.concatenate(parts, axis=1),
            jnp.concatenate(hots, axis=1),
            (((1,), (1,)), ((), ())),
            preferred_element_type=jnp.float32,
        )
        total = total + sums[0:SUM_ROWS] + sums[SUM_ROWS:]
    totals_ref[...] = total


def early_kernel(groups, *refs):
    points = refs[:groups]
    packed, rows_ref = refs[groups : groups + 2]
    near_rows, far_rows = arrange(points, packed, refs[groups + 2 :])
    rows_ref[0:4, :] = jnp.full((4, TILE_PTS), near_rows, jnp.int32)
    rows_ref[4:8, :] = jnp.full((4, TILE_PTS), far_rows, jnp.int32)


def own_kernel(packed, rows_ref, near, far, weights, totals_ref, rows_here, sem, *work):
    copy = pltpu.make_async_copy(rows_ref, rows_here, sem.at[0])
    copy.start()
    weigh_table(near, weights, 0)
    weigh_table(far, weights, 1)
    copy.wait()
    process(packed, rows_here[0, 0], rows_here[4, 0], weights, totals_ref, work)


def other_kernel(groups, *refs):
    points = refs[:groups]
    weights, before_ref, totals_ref, packed = refs[groups : groups + 4]
    arranging, work = refs[groups + 4 : groups + 8], refs[groups + 8 :]
    near_rows, far_rows = arrange(points, packed, arranging)
    process(packed, near_rows, far_rows, weights, totals_ref, work)
    totals_ref[...] = totals_ref[...] + before_ref[...]


def arrange_shapes(groups, tiles):
    count = groups * tiles
    return [
        pltpu.VMEM((count * POINT_ROWS, TILE_PTS), jnp.float32),
        pltpu.VMEM((count, TILE_PTS), jnp.int32),
        pltpu.SMEM((count, TILE_PTS), jnp.int32),
        pltpu.SemaphoreType.DMA((groups,)),
    ]


def process_shapes(groups, tiles):
    room = row_room(groups, tiles)
    return [
        pltpu.VMEM((CHANNELS, room, TILE_PTS), jnp.float32),
        pltpu.VMEM((room, TILE_PTS), jnp.int32),
        pltpu.VMEM((room, TILE_PTS), jnp.int32),
        pltpu.VMEM((SUM_ROWS * ROW_GROUP, TILE_PTS), jnp.float32),
    ]


def packed_shape(groups, tiles):
    return (row_room(groups, tiles) * POINT_ROWS, TILE_PTS)


def early_rows(points):
    groups, tiles = len(points), points[0].shape[1]
    return pl.pallas_call(
        functools.partial(early_kernel, groups),
        out_shape=(
            jax.ShapeDtypeStruct(packed_shape(groups, tiles), jnp.float32),
            jax.ShapeDtypeStruct((8, TILE_PTS), jnp.int32),
        ),
        in_specs=vmem(groups),
        out_specs=(pl.BlockSpec(memory_space=pltpu.VMEM),) * 2,
        scratch_shapes=arrange_shapes(groups, tiles),
        compiler_params=params(14),
    )(*points)


def own_totals(groups, packed, rows, near, far):
    tiles = near.shape[1]
    return pl.pallas_call(
        own_kernel,
        out_shape=(
            jax.ShapeDtypeStruct((2, CHANNELS * tiles, 2 * TILE_PTS), jnp.bfloat16),
            jax.ShapeDtypeStruct((SUM_ROWS, KNOT_DEV), jnp.float32),
        ),
        in_specs=vmem(4),
        out_specs=(pl.BlockSpec(memory_space=pltpu.VMEM),) * 2,
        scratch_shapes=[pltpu.SMEM((8, TILE_PTS), jnp.int32), pltpu.SemaphoreType.DMA((1,))]
        + process_shapes(groups, tiles),
        compiler_params=params(14),
    )(packed, rows, near, far)


def all_totals(points, weights, totals):
    groups, tiles = len(points), points[0].shape[1]
    return pl.pallas_call(
        functools.partial(other_kernel, groups),
        out_shape=jax.ShapeDtypeStruct((SUM_ROWS, KNOT_DEV), jnp.float32),
        in_specs=vmem(groups + 2),
        out_specs=pl.BlockSpec(memory_space=pltpu.VMEM),
        scratch_shapes=[pltpu.VMEM(packed_shape(groups, tiles), jnp.float32)]
        + arrange_shapes(groups, tiles)
        + process_shapes(groups, tiles),
        compiler_params=params(24),
    )(*points, weights, totals)


def cholesky(matrix):
    factor = {}
    inverse = []
    for column in range(6):
        pivot = matrix[column, column]
        for inner in range(column):
            pivot = pivot - factor[column, inner] * factor[column, inner]
        inverse.append(1.0 / jnp.sqrt(pivot))
        for row in range(column + 1, 6):
            entry = matrix[column, row]
            for inner in range(column):
                entry = entry - factor[row, inner] * factor[column, inner]
            factor[row, column] = entry * inverse[column]
    return factor, inverse


def solve(system, right_side):
    factor, inverse = system
    forward = []
    for row in range(6):
        entry = right_side[row]
        for inner in range(row):
            entry = entry - factor[row, inner] * forward[inner]
        forward.append(entry * inverse[row])
    answer = [None] * 6
    for row in reversed(range(6)):
        entry = forward[row]
        for inner in range(row + 1, 6):
            entry = entry - factor[inner, row] * answer[inner]
        answer[row] = entry * inverse[row]
    return answer


def step_kernel(segs, members, knot_ref, sums_ref, points_ref, adjusted_ref, out_ref, held, index_ref):
    tiles = knot_ref.shape[1]
    for tile in range(tiles):
        index_ref[tile : tile + 1, :] = jnp.full((1, KNOT_DEV), knot_ref[0, tile], jnp.int32)
    seg = lax.axis_index("seg")
    for place in range(3):
        wanted = seg + place - 1
        there = (wanted >= 0) & (wanted < segs)
        first = jnp.minimum(jnp.maximum(wanted, 0), segs - 1) * members
        total = sums_ref[first]
        for other in range(1, members):
            total = total + sums_ref[first + other]
        held[place * SUM_ROWS : (place + 1) * SUM_ROWS, :] = jnp.where(there, total, 0.0)
    for place in range(3, 8):
        held[place * SUM_ROWS : (place + 1) * SUM_ROWS, :] = jnp.zeros(
            (SUM_ROWS, KNOT_DEV), jnp.float32
        )
    shape = (8, KNOT_DEV)
    lanes = lax.broadcasted_iota(jnp.int32, shape, 1)
    rows = lax.broadcasted_iota(jnp.int32, shape, 0)

    def earlier(value):
        turned = pltpu.roll(value, 1, 1)
        return jnp.where(lanes == 0, pltpu.roll(turned, 1, 0), turned)

    def following(value):
        turned = pltpu.roll(value, KNOT_DEV - 1, 1)
        return jnp.where(lanes == KNOT_DEV - 1, pltpu.roll(turned, 7, 0), turned)

    def quantity(place):
        return held[pl.ds(place, 8, stride=SUM_ROWS), :]

    pair_place = {pair: place for place, pair in enumerate(PAIRS)}
    matrix, cross, cross_before = {}, {}, {}
    for pair, place in pair_place.items():
        value = quantity(place) + earlier(quantity(42 + place))
        matrix[pair] = value + damping if pair[0] == pair[1] else value
        cross[pair] = quantity(21 + place)
        cross_before[pair] = earlier(cross[pair])
    right_side = [quantity(63 + a) + earlier(quantity(69 + a)) for a in range(6)]
    system = cholesky(matrix)
    beyond = (rows >= 2) & (seg == segs - 1)
    first = [jnp.where(beyond, 0.0, -entry) for entry in solve(system, right_side)]
    before = [earlier(entry) for entry in first]
    after = [following(entry) for entry in first]
    corrected = []
    for a in range(6):
        total = right_side[a]
        for b in range(6):
            pair = (min(a, b), max(a, b))
            total = total + cross_before[pair] * before[b] + cross[pair] * after[b]
        corrected.append(total)
    second = [jnp.where(beyond, 0.0, -entry) for entry in solve(system, corrected)]
    upper = [following(entry) for entry in second]
    for a in range(6):
        out_ref[a] = second[a][1:2]
    low_rows = [jnp.broadcast_to(second[a][1:2], shape) for a in range(6)]
    high_rows = [jnp.broadcast_to(upper[a][1:2], shape) for a in range(6)]
    for begin in range(0, tiles, 8):
        span = slice(begin, begin + 8)
        knots = index_ref[span, :]
        later = points_ref[12, span, :]
        early = 1.0 - later
        pose = []
        for a in range(6):
            low = jnp.take_along_axis(low_rows[a], knots, axis=1, mode="promise_in_bounds")
            high = jnp.take_along_axis(high_rows[a], knots, axis=1, mode="promise_in_bounds")
            pose.append(early * low + later * high)
        lever = [points_ref[c, span, :] for c in range(9, 12)]
        moved = [
            pose[1] * lever[2] - pose[2] * lever[1] + pose[3],
            pose[2] * lever[0] - pose[0] * lever[2] + pose[4],
            pose[0] * lever[1] - pose[1] * lever[0] + pose[5],
        ]
        for c in range(3):
            adjusted_ref[c, span, :] = points_ref[c, span, :] + moved[c]


def local(positions, lever_arm, spline_time, covariance, partner, partner_side, tile_knot):
    tiles = positions.shape[2] // TILE_PTS
    strips = lax.axis_size("strip")
    members = lax.axis_size("tile")
    segs = lax.axis_size("seg")

    table, points = pl.pallas_call(
        pack_kernel,
        out_shape=(
            jax.ShapeDtypeStruct((CHANNELS, tiles, TILE_PTS), jnp.float32),
            jax.ShapeDtypeStruct((POINT_ROWS, tiles, TILE_PTS), jnp.float32),
        ),
        in_specs=[pl.BlockSpec(memory_space=pltpu.HBM)] * 7,
        out_specs=(pl.BlockSpec(memory_space=pltpu.VMEM),) * 2,
        scratch_shapes=[
            pltpu.VMEM((tiles, TILE_PTS), jnp.int32),
            pltpu.SMEM((2, 1, tiles), jnp.int32),
            pltpu.SemaphoreType.DMA((7,)),
        ],
        compiler_params=params(14),
    )(
        *[
            pltpu.with_memory_space_constraint(array, pltpu.HBM)
            for array in (
                positions.reshape(3, tiles, TILE_PTS),
                covariance.reshape(6, tiles, TILE_PTS),
                lever_arm.reshape(3, tiles, TILE_PTS),
                spline_time.reshape(tiles, TILE_PTS),
                partner.reshape(tiles, TILE_PTS),
                partner_side,
                tile_knot,
            )
        ]
    )

    def trade(first):
        pairs = []
        for strip in range(first, strips - 1, 2):
            pairs += [(strip, strip + 1), (strip + 1, strip)]
        return lax.ppermute(table, "strip", pairs)

    swap = [(member, member ^ 1) for member in range(members)]
    arrived = []
    for hop in range(2, members, 2):
        pairs = [((member + hop) % members, member) for member in range(members)]
        arrived.append(lax.ppermute(points, "tile", pairs))
    near, far = trade(0), trade(1)
    packed, rows = early_rows([points, lax.ppermute(points, "tile", swap)])
    weights, totals = own_totals(2, packed, rows, near, far)
    arrived = lax.optimization_barrier((arrived, near, far, packed))[0]
    others = arrived + [lax.ppermute(group, "tile", swap) for group in arrived]
    sums = all_totals(others, weights, totals)
    all_sums = lax.all_gather(sums, ("seg", "tile"), axis=0)
    adjusted, corrections = pl.pallas_call(
        functools.partial(step_kernel, segs, members),
        out_shape=(
            jax.ShapeDtypeStruct((3, tiles, TILE_PTS), jnp.float32),
            jax.ShapeDtypeStruct((6, 1, KNOT_DEV), jnp.float32),
        ),
        in_specs=smem(1) + vmem(2),
        out_specs=(pl.BlockSpec(memory_space=pltpu.VMEM),) * 2,
        scratch_shapes=[
            pltpu.VMEM((8 * SUM_ROWS, KNOT_DEV), jnp.float32),
            pltpu.VMEM((tiles, KNOT_DEV), jnp.int32),
        ],
        compiler_params=params(6),
    )(tile_knot, all_sums, points)
    return adjusted.reshape(positions.shape), corrections.reshape(1, 6, KNOT_DEV)


def solution(mesh):
    in_specs = (
        P("strip", None, ("seg", "tile")),
        P("strip", None, ("seg", "tile")),
        P("strip", ("seg", "tile")),
        P("strip", None, ("seg", "tile")),
        P("strip", ("seg", "tile")),
        P("strip", ("seg", "tile")),
        P("strip", ("seg", "tile")),
    )
    out_specs = (P("strip", None, ("seg", "tile")), P("strip", None, "seg"))
    return jax.shard_map(local, mesh=mesh, in_specs=in_specs, out_specs=out_specs, check_vma=False)
```

time: 49.3 us -> 39.8 us (0.81)
  the two profiles are of different devices: /device:TPU:0 before, /device:TPU:9 now
where the time goes in v2:
time: 39.8 us; the launch traced here: 39.9 us
  Pallas kernels  17.9 us (45%)
  blocking collectives  9.78 us (25%)
  starting transfers between devices  7.3 us (18%)
  waiting for transfers between devices  4.22 us (11%)
  between operations  0.7 us (2%)
    all_gather x1, blocking collectives, local(): all_sums = lax.all_gather(sums, ('seg', 'tile'), axis=0)  9.78 us
    pallas_call x1, Pallas kernels, all_totals(): pl.pallas_call(functools.partial(other_kernel, groups), out_shape=jax.Sha...  7.91 us
    ppermute x2, starting transfers between devices, trade(): return lax.ppermute(table, 'strip', pairs)  4.49 us
    pallas_call x1, Pallas kernels, early_rows(): pl.pallas_call(functools.partial(early_kernel, groups), out_shape=(jax.Sh...  3.54 us
    pallas_call x1, Pallas kernels, own_totals(): pl.pallas_call(own_kernel, out_shape=(jax.ShapeDtypeStruct((2, CHANNELS *...  3.45 us
    ppermute x2, waiting for transfers between devices, trade(): return lax.ppermute(table, 'strip', pairs)  3.21 us
    pallas_call x1, Pallas kernels, local(): pl.pallas_call(functools.partial(step_kernel, segs, members), out_shape=(...  1.83 us
    ppermute x1, starting transfers between devices, local(): arrived.append(lax.ppermute(points, 'tile', pairs))  1.23 us
  transfers between devices with their start and end apart: 5, of which 3 were waited for; matrix products, arithmetic and copies ran while one was open for 0% of the time, Pallas kernels for 18%

profile of v2, /device:TPU:9, one launch (start us, length us, event | category | flops | bytes accessed | tf_op | source)
XLA Modules:
  0.0 39.9 jit_solution(1253631736696484080)
XLA Ops:
  0.6 1.2 %shard_map.86 = (f32[9,64,128]{2,1,0:T(8,128)S(1)}, f32[16,64,128]{2,1,0:T(8,128)S(1)}) custom-call(f32[3,64,128]{2,1,0:T(8,128)} %bitcast.10, f32[6,64,128]{2,1,0:T(8,128)} %bitcast.9, f32[3,64,128]{2,1,0:T(8,128)} %bitcast.11, f32[64,128]{1,0:T(8,128)} %bitcast.12, s32[64,128]{1,0:T(8,128)} %bitcast.13, s32[1,64]{1,0:T(1,128)} %sides.1, s32[1,64]{1,0:T(1,128)} %knot_ref.1), custom_call_target="tpu_custom_call" | custom-call | tf_op jit(solution)/shard_map/pallas_call | solution.py:534
  1.8 0.7 %collective-permute-start.3 = (f32[16,64,128]{2,1,0:T(8,128)S(1)}, f32[16,64,128]{2,1,0:T(8,128)S(1)}, u32[]{:S(2)}, u32[]{:S(2)}) collective-permute-start(f32[16,64,128]{2,1,0:T(8,128)S(1)} %get-tuple-element.11.refs_0_.points_ref), channel_id=1, source_target_pairs={{0,1},{1,0},{2,3},{3,2},{4,5},{5,4},{6,7},{7,6},{8,9},{9,8},{10,11... | collective-permute-start | bytes 1572872 | tf_op jit(solution)/shard_map/ppermute | solution.py:575
  2.6 1.2 %collective-permute-start = (f32[16,64,128]{2,1,0:T(8,128)S(1)}, f32[16,64,128]{2,1,0:T(8,128)S(1)}, u32[]{:S(2)}, u32[]{:S(2)}) collective-permute-start(f32[16,64,128]{2,1,0:T(8,128)S(1)} %get-tuple-element.11.refs_0_.points_ref), channel_id=1, source_target_pairs={{2,0},{3,1},{0,2},{1,3},{6,4},{7,5},{4,6},{5,7},{10,8},{11,9},{8,1... | collective-permute-start | bytes 1572872 | tf_op jit(solution)/shard_map/ppermute | solution.py:573
  3.8 0.2 collective-permute-start.1
  4.0 4.3 %collective-permute-start.2 = (f32[9,64,128]{2,1,0:T(8,128)S(1)}, f32[9,64,128]{2,1,0:T(8,128)S(1)}, u32[]{:S(2)}, u32[]{:S(2)}) collective-permute-start(f32[9,64,128]{2,1,0:T(8,128)S(1)} %get-tuple-element.12), channel_id=1, source_target_pairs={{4,8},{8,4},{5,9},{9,5},{6,10},{10,6},{7,11},{11,7},{20,24},{24,20... | collective-permute-start | bytes 884744 | tf_op jit(solution)/shard_map/ppermute | solution.py:567
  8.3 0.0 collective-permute-done.3.refs_1_
  8.3 3.5 %shard_map.87 = (f32[3072,128]{1,0:T(8,128)S(1)}, s32[8,128]{1,0:T(8,128)S(1)}) custom-call(f32[16,64,128]{2,1,0:T(8,128)S(1)} %get-tuple-element.11.refs_0_.points_ref, f32[16,64,128]{2,1,0:T(8,128)S(1)} %collective-permute-done.3.refs_1_), custom_call_target="tpu_custom_call" | custom-call | tf_op jit(solution)/shard_map/pallas_call | solution.py:374
  11.8 0.2 collective-permute-done.1.near
  12.0 3.0 %collective-permute-done.2.far = f32[9,64,128]{2,1,0:T(8,128)S(1)} collective-permute-done((f32[9,64,128]{2,1,0:T(8,128)S(1)}, f32[9,64,128]{2,1,0:T(8,128)S(1)}, u32[]{:S(2)}, u32[]{:S(2)}) %collective-permute-start.2) | collective-permute-done | bytes 294944 | tf_op jit(solution)/shard_map/ppermute | solution.py:567
  15.1 1.0 %collective-permute-done.refs_0_ = f32[16,64,128]{2,1,0:T(8,128)S(1)} collective-permute-done((f32[16,64,128]{2,1,0:T(8,128)S(1)}, f32[16,64,128]{2,1,0:T(8,128)S(1)}, u32[]{:S(2)}, u32[]{:S(2)}) %collective-permute-start) | collective-permute-done | bytes 524320 | tf_op jit(solution)/shard_map/ppermute | solution.py:573
  16.1 0.8 %collective-permute-start.4 = (f32[16,64,128]{2,1,0:T(8,128)S(1)}, f32[16,64,128]{2,1,0:T(8,128)S(1)}, u32[]{:S(2)}, u32[]{:S(2)}) collective-permute-start(f32[16,64,128]{2,1,0:T(8,128)S(1)} %collective-permute-done.refs_0_), channel_id=1, source_target_pairs={{0,1},{1,0},{2,3},{3,2},{4,5},{5,4},{6,7},{7,6},{8,9},{9,8},{10,11... | collective-permute-start | bytes 1572872 | tf_op jit(solution)/shard_map/ppermute | solution.py:578
  16.9 3.4 %shard_map.88 = (bf16[2,576,256]{2,1,0:T(8,128)(2,1)S(1)}, f32[80,128]{1,0:T(8,128)S(1)}) custom-call(f32[3072,128]{1,0:T(8,128)S(1)} %get-tuple-element.13.packed, s32[8,128]{1,0:T(8,128)S(1)} %get-tuple-element.15.rows_ref, f32[9,64,128]{2,1,0:T(8,128)S(1)} %collective-permute-done.1.near, f32[9,64,128]{2,1,0:T(8,128)S(1)} %collective-permute-done.2.far), custom_call_target="tpu_custom_call" | custom-call | tf_op jit(solution)/shard_map/pallas_call | solution.py:389
  20.4 0.0 copy-start
  20.4 0.0 collective-permute-done.4.refs_1_
  20.4 7.9 %shard_map.89 = f32[80,128]{1,0:T(8,128)S(1)} custom-call(f32[16,64,128]{2,1,0:T(8,128)S(1)} %collective-permute-done.refs_0_, f32[16,64,128]{2,1,0:T(8,128)S(1)} %collective-permute-done.4.refs_1_, bf16[2,576,256]{2,1,0:T(8,128)(2,1)S(1)} %get-tuple-element.16.refs_2_, f32[80,128]{1,0:T(8,128)S(1)} %get-tuple-element.17.refs_3_), custom_call_target="tpu_custom_call" | custom-call | tf_op jit(solution)/shard_map/pallas_call | solution.py:405
  28.3 9.8 %all-gather = f32[640,128]{1,0:T(8,128)S(1)} all-gather(f32[80,128]{1,0:T(8,128)S(1)} %shard_map.89), channel_id=2, replica_groups=mesh['seg'=2,'strip'=4,'tile'=4] {'seg','tile'}, dimensions={0}, use_global_device_ids=true | all-gather | bytes 368640 | tf_op jit(solution)/shard_map/all_gather | solution.py:580
  38.1 0.0 copy-done
  38.1 1.8 %shard_map.90 = (f32[3,64,128]{2,1,0:T(8,128)}, f32[6,1,128]{2,1,0:T(1,128)}) custom-call(s32[1,64]{1,0:T(1,128)S(1)} %copy-done, f32[8,80,128]{2,1,0:T(8,128)S(1)} %bitcast.8, f32[16,64,128]{2,1,0:T(8,128)S(1)} %get-tuple-element.11.refs_0_.points_ref), custom_call_target="tpu_custom_call" | custom-call | tf_op jit(solution)/shard_map/pallas_call | solution.py:581
Async XLA Ops:
  1.8 6.5 %collective-permute-start.3 = (f32[16,64,128]{2,1,0:T(8,128)S(1)}, f32[16,64,128]{2,1,0:T(8,128)S(1)}, u32[]{:S(2)}, u32[]{:S(2)}) collective-permute-start(f32[16,64,128]{2,1,0:T(8,128)S(1)} %get-tuple-element.11.refs_0_.points_ref), channel_id=1, source_target_pairs={{0,1},{1,0},{2,3},{3,2},{4,5},{5,4},{6,7},{7,6},{8,9},{9,8},{10,11... | collective-permute-start | bytes 1572872 | tf_op jit(solution)/shard_map/ppermute | solution.py:575
  2.6 13.5 %collective-permute-start = (f32[16,64,128]{2,1,0:T(8,128)S(1)}, f32[16,64,128]{2,1,0:T(8,128)S(1)}, u32[]{:S(2)}, u32[]{:S(2)}) collective-permute-start(f32[16,64,128]{2,1,0:T(8,128)S(1)} %get-tuple-element.11.refs_0_.points_ref), channel_id=1, source_target_pairs={{2,0},{3,1},{0,2},{1,3},{6,4},{7,5},{4,6},{5,7},{10,8},{11,9},{8,1... | collective-permute-start | bytes 1572872 | tf_op jit(solution)/shard_map/ppermute | solution.py:573
  3.8 8.2 %collective-permute-start.1 = (f32[9,64,128]{2,1,0:T(8,128)S(1)}, f32[9,64,128]{2,1,0:T(8,128)S(1)}, u32[]{:S(2)}, u32[]{:S(2)}) collective-permute-start(f32[9,64,128]{2,1,0:T(8,128)S(1)} %get-tuple-element.12), channel_id=1, source_target_pairs={{0,4},{4,0},{8,12},{12,8},{1,5},{5,1},{9,13},{13,9},{2,6},{6,2},{1... | collective-permute-start | bytes 884744 | tf_op jit(solution)/shard_map/ppermute | solution.py:567
  4.0 11.1 %collective-permute-start.2 = (f32[9,64,128]{2,1,0:T(8,128)S(1)}, f32[9,64,128]{2,1,0:T(8,128)S(1)}, u32[]{:S(2)}, u32[]{:S(2)}) collective-permute-start(f32[9,64,128]{2,1,0:T(8,128)S(1)} %get-tuple-element.12), channel_id=1, source_target_pairs={{4,8},{8,4},{5,9},{9,5},{6,10},{10,6},{7,11},{11,7},{20,24},{24,20... | collective-permute-start | bytes 884744 | tf_op jit(solution)/shard_map/ppermute | solution.py:567
  16.1 4.3 %collective-permute-start.4 = (f32[16,64,128]{2,1,0:T(8,128)S(1)}, f32[16,64,128]{2,1,0:T(8,128)S(1)}, u32[]{:S(2)}, u32[]{:S(2)}) collective-permute-start(f32[16,64,128]{2,1,0:T(8,128)S(1)} %collective-permute-done.refs_0_), channel_id=1, source_target_pairs={{0,1},{1,0},{2,3},{3,2},{4,5},{5,4},{6,7},{7,6},{8,9},{9,8},{10,11... | collective-permute-start | bytes 1572872 | tf_op jit(solution)/shard_map/ppermute | solution.py:578
  20.4 17.7 %copy-start = (s32[1,64]{1,0:T(1,128)S(1)}, s32[1,64]{1,0:T(1,128)}, u32[]{:S(2)}) copy-start(s32[1,64]{1,0:T(1,128)} %knot_ref.1) | copy-start | bytes 772

commit v3 on v2

--- a/solution.py
+++ b/solution.py
@@ -15,8 +15,8 @@
 POINT_ROWS = 16
 PARTNER = 13
 KNOT = 14
-SIDE = 15
 VALID = 15
+TILE_ROW = 14
 SUM_ROWS = 80
 
 damping = 1.0
@@ -38,25 +38,30 @@
 
 def pack_kernel(pos, cov, lever, time, partner, sides, knots, table_ref, points_ref, ints, small, sems):
     tiles = time.shape[0]
+    base = TILE_ROW * tiles
+
+    def span(first):
+        return points_ref.at[pl.ds(first * tiles, tiles)]
+
     copies = [
-        pltpu.make_async_copy(sides, small.at[0], sems.at[0]),
-        pltpu.make_async_copy(knots, small.at[1], sems.at[1]),
-        pltpu.make_async_copy(partner, ints, sems.at[2]),
+        pltpu.make_async_copy(partner, ints, sems.at[0]),
+        pltpu.make_async_copy(sides, small.at[0], sems.at[1]),
+        pltpu.make_async_copy(knots, small.at[1], sems.at[2]),
         pltpu.make_async_copy(pos, table_ref.at[pl.ds(0, 3)], sems.at[3]),
         pltpu.make_async_copy(cov, table_ref.at[pl.ds(3, 6)], sems.at[4]),
-        pltpu.make_async_copy(lever, points_ref.at[pl.ds(9, 3)], sems.at[5]),
-        pltpu.make_async_copy(time, points_ref.at[12], sems.at[6]),
+        pltpu.make_async_copy(time, span(12), sems.at[5]),
     ]
+    copies += [pltpu.make_async_copy(lever.at[c], span(9 + c), sems.at[6 + c]) for c in range(3)]
     for copy in copies:
         copy.start()
     for copy in copies:
         copy.wait()
-    points_ref[0:CHANNELS] = table_ref[...]
-    points_ref[PARTNER] = ints[...].astype(jnp.float32)
-    for place, channel in ((0, SIDE), (1, KNOT)):
-        for tile in range(tiles):
-            value = jnp.full((1, TILE_PTS), small[place, 0, tile], jnp.int32)
-            points_ref[channel, tile : tile + 1, :] = value.astype(jnp.float32)
+    for channel in range(CHANNELS):
+        points_ref[channel * tiles : (channel + 1) * tiles, :] = table_ref[channel]
+    points_ref[PARTNER * tiles : (PARTNER + 1) * tiles, :] = ints[...].astype(jnp.float32)
+    points_ref[base : base + 8, :] = jnp.zeros((8, TILE_PTS), jnp.float32)
+    for place in range(2):
+        points_ref[base + place : base + place + 1, 0:tiles] = small[place].astype(jnp.float32)
 
 
 def split_two(value):
@@ -70,97 +75,100 @@
 
 
 def arrange(points, packed, work):
-    compact, numbers, counts, sems = work
-    tiles = points[0].shape[1]
-    upper = (
-        lax.broadcasted_iota(jnp.int32, (TILE_PTS, TILE_PTS), 0)
-        <= lax.broadcasted_iota(jnp.int32, (TILE_PTS, TILE_PTS), 1)
-    )
-    upper = jnp.where(upper, 1.0, 0.0).astype(jnp.bfloat16)
+    compact, codes, places, sem = work
+    tiles = (points[0].shape[0] - 8) // TILE_ROW
+    total = len(points) * tiles
+    room = packed.shape[0] // POINT_ROWS
+    shape = (tiles, TILE_PTS)
+    lanes = lax.broadcasted_iota(jnp.int32, shape, 1)
+    own_tile = lax.broadcasted_iota(jnp.int32, shape, 0)
+
+    def ordered(size, test):
+        rows = lax.broadcasted_iota(jnp.int32, (size, size), 0)
+        return jnp.where(test(rows, lax.broadcasted_iota(jnp.int32, (size, size), 1)), 1.0, 0.0)
+
+    upper = ordered(TILE_PTS, lambda row, lane: row <= lane).astype(jnp.bfloat16)
+    lower = ordered(total, lambda row, lane: row > lane).astype(jnp.bfloat16)
     member = lax.axis_index("tile")
     near = jnp.where(lax.axis_index("strip") % 2 == 1, 0.0, 1.0)
-    copies = []
-    for p, group in enumerate(points):
-        index = group[PARTNER].astype(jnp.int32)
+
+    def tile_value(group, place):
+        at = TILE_ROW * tiles + place
+        return jnp.take_along_axis(
+            jnp.broadcast_to(group[at : at + 1, :], shape), own_tile, axis=1, mode="promise_in_bounds"
+        )
+
+    ranks, numbers, farther = [], [], []
+    for group in points:
+        index = group[PARTNER * tiles : (PARTNER + 1) * tiles, :].astype(jnp.int32)
         offset = lax.shift_right_logical(index, 7) - member * tiles
-        side = group[SIDE]
+        side = tile_value(group, 0)
         wanted = (offset >= 0) & (offset < tiles) & (side != 2.0)
         marks = jnp.where(wanted, 1.0, 0.0).astype(jnp.bfloat16)
-        ranks = jnp.dot(marks, upper, preferred_element_type=jnp.float32).astype(jnp.int32)
-        numbers[p * tiles : (p + 1) * tiles, :] = ranks + jnp.where(side == near, 0, 256)
-        span = pl.ds(p * tiles, tiles)
-        copies.append(pltpu.make_async_copy(numbers.at[span], counts.at[span], sems.at[p]))
-    for copy in copies:
-        copy.start()
-    lanes = lax.broadcasted_iota(jnp.int32, (tiles, TILE_PTS), 1)
+        rank = jnp.dot(marks, upper, preferred_element_type=jnp.float32)
+        ranks.append(rank.astype(jnp.int32))
+        numbers.append(jnp.broadcast_to(rank[:, TILE_PTS - 1 :], shape))
+        farther.append(jnp.where(side == near, 0.0, 1.0))
+    number, far = jnp.concatenate(numbers, axis=0), jnp.concatenate(farther, axis=0)
+    ends = []
+    for chosen in (number * (1.0 - far), number * far):
+        before = jnp.dot(lower, chosen.astype(jnp.bfloat16), preferred_element_type=jnp.float32)
+        ends.append((before.astype(jnp.int32), (before + chosen).astype(jnp.int32)))
+    start = jnp.where(far > 0.0, ends[1][0], ends[0][0])
+    row = lax.shift_right_logical(start, 7)
+    first = jnp.where(far > 0.0, room - 1 - row, row) * POINT_ROWS
+    second = jnp.where(far > 0.0, first - POINT_ROWS, first + POINT_ROWS)
+    lane = lax.broadcasted_iota(jnp.int32, (total, TILE_PTS), 1)
+    code = jnp.where(lane == 0, first, jnp.where(lane == 1, second, start & (TILE_PTS - 1)))
+    code = jnp.where(lane == 3, ends[0][1], jnp.where(lane == 4, ends[1][1], code))
+    codes[...] = code
+    copy = pltpu.make_async_copy(codes, places, sem.at[0])
+    copy.start()
     for p, group in enumerate(points):
-        ranks = numbers[p * tiles : (p + 1) * tiles, :] & 255
         source = jnp.zeros_like(lanes)
         for jump in (64, 32, 16, 8, 4, 2, 1):
-            there = jnp.take_along_axis(ranks, source + (jump - 1), axis=1, mode="promise_in_bounds")
+            there = jnp.take_along_axis(
+                ranks[p], source + (jump - 1), axis=1, mode="promise_in_bounds"
+            )
             source = jnp.where(there <= lanes, source + jump, source)
-        count = jnp.broadcast_to(ranks[:, TILE_PTS - 1 :], lanes.shape)
         for channel in range(POINT_ROWS):
             if channel == VALID:
-                value = jnp.where(lanes < count, 1.0, 0.0)
+                value = jnp.where(lanes.astype(jnp.float32) < numbers[p], 1.0, 0.0)
+            elif channel == KNOT:
+                value = tile_value(group, 1)
             else:
-                value = group[channel]
-                if channel != KNOT:
-                    value = jnp.take_along_axis(value, source, axis=1, mode="promise_in_bounds")
+                value = group[channel * tiles : (channel + 1) * tiles, :]
+                value = jnp.take_along_axis(value, source, axis=1, mode="promise_in_bounds")
             at = p * tiles * POINT_ROWS + channel
             compact[pl.ds(at, tiles, stride=POINT_ROWS), :] = value
-    for copy in copies:
-        copy.wait()
-
-    room = packed.shape[0] // POINT_ROWS
-    last = room - 1
-    blank = jnp.zeros((POINT_ROWS, TILE_PTS), jnp.float32)
-
-    def rows_at(row):
-        return pl.ds(pl.multiple_of(row * POINT_ROWS, POINT_ROWS), POINT_ROWS)
-
-    packed[rows_at(0), :] = blank
-    packed[rows_at(last), :] = blank
+    copy.wait()
+
     wide = lax.broadcasted_iota(jnp.int32, (POINT_ROWS, TILE_PTS), 1)
 
-    def place(tile, carry):
-        near_row, near_start, far_row, far_start = carry
-        code = counts[tile, TILE_PTS - 1]
-        count = code & 255
-        far = code >= 256
-        row = jnp.where(far, far_row, near_row)
-        start = jnp.where(far, far_start, near_start)
-        full = start + count > TILE_PTS
-        row = jnp.where(full, row + 1, row)
-        start = jnp.where(full, 0, start)
-        at = rows_at(jnp.where(far, last - row, row))
-        value = pltpu.roll(compact[rows_at(tile), :], start, 1)
-        packed[at, :] = jnp.where(wide >= start, value, packed[at, :])
-        end = start + count
-        return (
-            jnp.where(far, near_row, row),
-            jnp.where(far, near_start, end),
-            jnp.where(far, row, far_row),
-            jnp.where(far, end, far_start),
-        )
-
-    zero = jnp.int32(0)
-    total = len(points) * tiles
-    unroll = 8
+    def span(first):
+        return pl.ds(pl.multiple_of(first, POINT_ROWS), POINT_ROWS)
+
+    def place(tile):
+        shift = places[tile, 2]
+        value = pltpu.roll(compact[span(tile * POINT_ROWS), :], shift, 1)
+        at = span(places[tile, 0])
+        packed[at, :] = jnp.where(wide >= shift, value, packed[at, :])
+        packed[span(places[tile, 1]), :] = jnp.where(wide < shift, value, 0.0)
+
+    unroll = 16
 
     def several(step, carry):
         for tile in range(unroll):
-            carry = place(step * unroll + tile, carry)
+            place(step * unroll + tile)
         return carry
 
-    near_row, near_start, far_row, far_start = lax.fori_loop(
-        0, total // unroll, several, (zero, zero, zero, zero)
-    )
-    near_rows = near_row + (near_start > 0).astype(jnp.int32)
-    far_rows = far_row + (far_start > 0).astype(jnp.int32)
+    lax.fori_loop(0, total // unroll, several, 0)
+    near_rows = lax.shift_right_logical(places[total - 1, 3] + TILE_PTS - 1, 7)
+    far_rows = lax.shift_right_logical(places[total - 1, 4] + TILE_PTS - 1, 7)
+    blank = jnp.zeros((POINT_ROWS, TILE_PTS), jnp.float32)
     for extra in range(ROW_GROUP):
-        packed[rows_at(near_rows + extra), :] = blank
-        packed[rows_at(last - far_rows - extra), :] = blank
+        packed[span((near_rows + extra) * POINT_ROWS), :] = blank
+        packed[span((room - 1 - far_rows - extra) * POINT_ROWS), :] = blank
     return near_rows, far_rows
 
 
@@ -174,26 +182,10 @@
 
 
 def process(packed, near_rows, far_rows, weights, totals_ref, work):
-    target, key_ref, row_ref, terms_ref = work
+    target, terms_ref = work
     tiles = weights.shape[1] // CHANNELS
     room = packed.shape[0] // POINT_ROWS
     member = lax.axis_index("tile")
-
-    def keys(step, carry):
-        begin = pl.multiple_of(step * 8, 8)
-        span = pl.ds(begin, 8)
-
-        def channel(place):
-            return packed[pl.ds(begin * POINT_ROWS + place, 8, stride=POINT_ROWS), :]
-
-        index = channel(PARTNER).astype(jnp.int32)
-        key_ref[span, :] = index & (TILE_PTS - 1)
-        row = lax.shift_right_logical(index, 7) - member * tiles
-        row_ref[span, :] = jnp.where(channel(VALID) > 0.0, row, -1)
-        return carry
-
-    lax.fori_loop(0, room // 8, keys, 0)
-    target[...] = jnp.zeros_like(target)
     near_blocks = lax.shift_right_logical(near_rows + BLOCK_TILES - 1, 2)
     far_blocks = lax.shift_right_logical(far_rows + BLOCK_TILES - 1, 2)
     blocks = near_blocks + far_blocks
@@ -205,8 +197,18 @@
         slot = far.astype(jnp.int32)
         base = jnp.where(far, room - BLOCK_TILES * (block - near_blocks + 1), block * BLOCK_TILES)
         ids = [base + j for j in range(BLOCK_TILES)]
-        keys = jnp.concatenate([key_ref[pl.ds(i, 1), :] for i in ids], axis=1)
-        rows = jnp.concatenate([row_ref[pl.ds(i, 1), :] for i in ids], axis=1)
+
+        def channel(place):
+            rows = [
+                packed[pl.ds(base * POINT_ROWS + j * POINT_ROWS + place, 1), :]
+                for j in range(BLOCK_TILES)
+            ]
+            return jnp.concatenate(rows, axis=1)
+
+        index = channel(PARTNER).astype(jnp.int32)
+        keys = index & (TILE_PTS - 1)
+        rows = lax.shift_right_logical(index, 7) - member * tiles
+        rows = jnp.where(channel(VALID) > 0.0, rows, -1)
         hot = jnp.where(
             lax.broadcasted_iota(jnp.int32, (TILE_PTS, queries), 0) == keys, 1.0, 0.0
         ).astype(jnp.bfloat16)
@@ -257,7 +259,7 @@
 
     valid = own(VALID) > 0.0
     m = [own(3 + c) + target[3 + c, span, :] for c in range(6)]
-    residual = [own(c) - target[c, span, :] for c in range(3)]
+    residual = [jnp.where(valid, own(c) - target[c, span, :], 0.0) for c in range(3)]
     lever = [own(9 + c) for c in range(3)]
     later = own(12)
     early = 1.0 - later
@@ -270,8 +272,7 @@
         m[3] * m[4] - m[0] * m[5],
     ]
     determinant = m[0] * adjunct[0] + m[3] * adjunct[3] + m[4] * adjunct[4]
-    scale = jnp.where(valid, 1.0 / determinant, 0.0)
-    inv = [entry * scale for entry in adjunct]
+    inv = [jnp.where(valid, entry / determinant, 0.0) for entry in adjunct]
     info = [[inv[0], inv[3], inv[4]], [inv[3], inv[1], inv[5]], [inv[4], inv[5], inv[2]]]
 
     def turned(column):
@@ -351,16 +352,13 @@
         pltpu.VMEM((count * POINT_ROWS, TILE_PTS), jnp.float32),
         pltpu.VMEM((count, TILE_PTS), jnp.int32),
         pltpu.SMEM((count, TILE_PTS), jnp.int32),
-        pltpu.SemaphoreType.DMA((groups,)),
+        pltpu.SemaphoreType.DMA((1,)),
     ]
 
 
 def process_shapes(groups, tiles):
-    room = row_room(groups, tiles)
     return [
-        pltpu.VMEM((CHANNELS, room, TILE_PTS), jnp.float32),
-        pltpu.VMEM((room, TILE_PTS), jnp.int32),
-        pltpu.VMEM((room, TILE_PTS), jnp.int32),
+        pltpu.VMEM((CHANNELS, row_room(groups, tiles), TILE_PTS), jnp.float32),
         pltpu.VMEM((SUM_ROWS * ROW_GROUP, TILE_PTS), jnp.float32),
     ]
 
@@ -370,7 +368,7 @@
 
 
 def early_rows(points):
-    groups, tiles = len(points), points[0].shape[1]
+    groups, tiles = len(points), (points[0].shape[0] - 8) // TILE_ROW
     return pl.pallas_call(
         functools.partial(early_kernel, groups),
         out_shape=(
@@ -401,7 +399,7 @@
 
 
 def all_totals(points, weights, totals):
-    groups, tiles = len(points), points[0].shape[1]
+    groups, tiles = len(points), (points[0].shape[0] - 8) // TILE_ROW
     return pl.pallas_call(
         functools.partial(other_kernel, groups),
         out_shape=jax.ShapeDtypeStruct((SUM_ROWS, KNOT_DEV), jnp.float32),
@@ -508,21 +506,25 @@
     for begin in range(0, tiles, 8):
         span = slice(begin, begin + 8)
         knots = index_ref[span, :]
-        later = points_ref[12, span, :]
+
+        def own(channel):
+            return points_ref[channel * tiles + begin : channel * tiles + begin + 8, :]
+
+        later = own(12)
         early = 1.0 - later
         pose = []
         for a in range(6):
             low = jnp.take_along_axis(low_rows[a], knots, axis=1, mode="promise_in_bounds")
             high = jnp.take_along_axis(high_rows[a], knots, axis=1, mode="promise_in_bounds")
             pose.append(early * low + later * high)
-        lever = [points_ref[c, span, :] for c in range(9, 12)]
+        lever = [own(c) for c in range(9, 12)]
         moved = [
             pose[1] * lever[2] - pose[2] * lever[1] + pose[3],
             pose[2] * lever[0] - pose[0] * lever[2] + pose[4],
             pose[0] * lever[1] - pose[1] * lever[0] + pose[5],
         ]
         for c in range(3):
-            adjusted_ref[c, span, :] = points_ref[c, span, :] + moved[c]
+            adjusted_ref[c, span, :] = own(c) + moved[c]
 
 
 def local(positions, lever_arm, spline_time, covariance, partner, partner_side, tile_knot):
@@ -535,14 +537,14 @@
         pack_kernel,
         out_shape=(
             jax.ShapeDtypeStruct((CHANNELS, tiles, TILE_PTS), jnp.float32),
-            jax.ShapeDtypeStruct((POINT_ROWS, tiles, TILE_PTS), jnp.float32),
+            jax.ShapeDtypeStruct((TILE_ROW * tiles + 8, TILE_PTS), jnp.float32),
         ),
         in_specs=[pl.BlockSpec(memory_space=pltpu.HBM)] * 7,
         out_specs=(pl.BlockSpec(memory_space=pltpu.VMEM),) * 2,
         scratch_shapes=[
             pltpu.VMEM((tiles, TILE_PTS), jnp.int32),
-            pltpu.SMEM((2, 1, tiles), jnp.int32),
-            pltpu.SemaphoreType.DMA((7,)),
+            pltpu.VMEM((2, 1, tiles), jnp.int32),
+            pltpu.SemaphoreType.DMA((9,)),
         ],
         compiler_params=params(14),
     )(

time: 39.8 us -> 36.9 us (0.927)
  the two profiles are of different devices: /device:TPU:9 before, /device:TPU:0 now
where the time goes in v3:
time: 36.9 us; the launch traced here: 36.7 us
  Pallas kernels  14.4 us (39%)
  blocking collectives  10.7 us (29%)
  waiting for transfers between devices  5.58 us (15%)
  starting transfers between devices  5.33 us (14%)
  between operations  0.69 us (2%)
    all_gather x1, blocking collectives, local(): all_sums = lax.all_gather(sums, ('seg', 'tile'), axis=0)  10.7 us
    pallas_call x1, Pallas kernels, all_totals(): pl.pallas_call(functools.partial(other_kernel, groups), out_shape=jax.Sha...  5.95 us
    ppermute x2, waiting for transfers between devices, trade(): return lax.ppermute(table, 'strip', pairs)  3.46 us
    pallas_call x1, Pallas kernels, early_rows(): pl.pallas_call(functools.partial(early_kernel, groups), out_shape=(jax.Sh...  3.36 us
    ppermute x1, starting transfers between devices, local(): arrived.append(lax.ppermute(points, 'tile', pairs))  2.56 us
    ppermute x2, starting transfers between devices, trade(): return lax.ppermute(table, 'strip', pairs)  2.24 us
    pallas_call x1, Pallas kernels, own_totals(): pl.pallas_call(own_kernel, out_shape=(jax.ShapeDtypeStruct((2, CHANNELS *...  2.15 us
    ppermute x1, waiting for transfers between devices, local(): arrived.append(lax.ppermute(points, 'tile', pairs))  2.12 us
  transfers between devices with their start and end apart: 5, of which 2 were waited for; matrix products, arithmetic and copies ran while one was open for 0% of the time, Pallas kernels for 15%

profile of v3, /device:TPU:0, one launch (start us, length us, event | category | flops | bytes accessed | tf_op | source)
XLA Modules:
  0.0 36.7 jit_solution(14583358158795265139)
XLA Ops:
  0.6 1.1 %shard_map.86 = (f32[9,64,128]{2,1,0:T(8,128)S(1)}, f32[904,128]{1,0:T(8,128)S(1)}) custom-call(f32[3,64,128]{2,1,0:T(8,128)} %bitcast.10, f32[6,64,128]{2,1,0:T(8,128)} %bitcast.9, f32[3,64,128]{2,1,0:T(8,128)} %bitcast.11, f32[64,128]{1,0:T(8,128)} %bitcast.12, s32[64,128]{1,0:T(8,128)} %bitcast.13, s32[1,64]{1,0:T(1,128)} %sides.1, s32[1,64]{1,0:T(1,128)} %knot_ref.1), custom_call_target="tpu_custom_call" | custom-call | tf_op jit(solution)/shard_map/pallas_call | solution.py:536
  1.8 0.5 %collective-permute-start.3 = (f32[904,128]{1,0:T(8,128)S(1)}, f32[904,128]{1,0:T(8,128)S(1)}, u32[]{:S(2)}, u32[]{:S(2)}) collective-permute-start(f32[904,128]{1,0:T(8,128)S(1)} %get-tuple-element.11.refs_0_.points_ref), channel_id=1, source_target_pairs={{0,1},{1,0},{2,3},{3,2},{4,5},{5,4},{6,7},{7,6},{8,9},{9,8},{10,11... | collective-permute-start | bytes 1388552 | tf_op jit(solution)/shard_map/ppermute | solution.py:577
  2.3 2.6 %collective-permute-start = (f32[904,128]{1,0:T(8,128)S(1)}, f32[904,128]{1,0:T(8,128)S(1)}, u32[]{:S(2)}, u32[]{:S(2)}) collective-permute-start(f32[904,128]{1,0:T(8,128)S(1)} %get-tuple-element.11.refs_0_.points_ref), channel_id=1, source_target_pairs={{2,0},{3,1},{0,2},{1,3},{6,4},{7,5},{4,6},{5,7},{10,8},{11,9},{8,1... | collective-permute-start | bytes 1388552 | tf_op jit(solution)/shard_map/ppermute | solution.py:575
  4.9 1.6 %collective-permute-start.1 = (f32[9,64,128]{2,1,0:T(8,128)S(1)}, f32[9,64,128]{2,1,0:T(8,128)S(1)}, u32[]{:S(2)}, u32[]{:S(2)}) collective-permute-start(f32[9,64,128]{2,1,0:T(8,128)S(1)} %get-tuple-element.12), channel_id=1, source_target_pairs={{0,4},{4,0},{8,12},{12,8},{1,5},{5,1},{9,13},{13,9},{2,6},{6,2},{1... | collective-permute-start | bytes 884744 | tf_op jit(solution)/shard_map/ppermute | solution.py:569
  6.4 0.7 %collective-permute-start.2 = (f32[9,64,128]{2,1,0:T(8,128)S(1)}, f32[9,64,128]{2,1,0:T(8,128)S(1)}, u32[]{:S(2)}, u32[]{:S(2)}) collective-permute-start(f32[9,64,128]{2,1,0:T(8,128)S(1)} %get-tuple-element.12), channel_id=1, source_target_pairs={{4,8},{8,4},{5,9},{9,5},{6,10},{10,6},{7,11},{11,7},{20,24},{24,20... | collective-permute-start | bytes 884744 | tf_op jit(solution)/shard_map/ppermute | solution.py:569
  7.1 0.0 collective-permute-done.3.refs_1_
  7.1 3.4 %shard_map.87 = (f32[3072,128]{1,0:T(8,128)S(1)}, s32[8,128]{1,0:T(8,128)S(1)}) custom-call(f32[904,128]{1,0:T(8,128)S(1)} %get-tuple-element.11.refs_0_.points_ref, f32[904,128]{1,0:T(8,128)S(1)} %collective-permute-done.3.refs_1_), custom_call_target="tpu_custom_call" | custom-call | tf_op jit(solution)/shard_map/pallas_call | solution.py:372
  10.5 3.5 %collective-permute-done.1.near = f32[9,64,128]{2,1,0:T(8,128)S(1)} collective-permute-done((f32[9,64,128]{2,1,0:T(8,128)S(1)}, f32[9,64,128]{2,1,0:T(8,128)S(1)}, u32[]{:S(2)}, u32[]{:S(2)}) %collective-permute-start.1) | collective-permute-done | bytes 294944 | tf_op jit(solution)/shard_map/ppermute | solution.py:569
  13.9 0.0 collective-permute-done.2.far
  13.9 2.1 %collective-permute-done.refs_0_ = f32[904,128]{1,0:T(8,128)S(1)} collective-permute-done((f32[904,128]{1,0:T(8,128)S(1)}, f32[904,128]{1,0:T(8,128)S(1)}, u32[]{:S(2)}, u32[]{:S(2)}) %collective-permute-start) | collective-permute-done | bytes 462880 | tf_op jit(solution)/shard_map/ppermute | solution.py:575
  16.1 0.0 collective-permute-start.4
  16.1 0.0 copy-start
  16.1 2.1 %shard_map.88 = (bf16[2,576,256]{2,1,0:T(8,128)(2,1)S(1)}, f32[80,128]{1,0:T(8,128)S(1)}) custom-call(f32[3072,128]{1,0:T(8,128)S(1)} %get-tuple-element.13.packed, s32[8,128]{1,0:T(8,128)S(1)} %get-tuple-element.15.rows_ref, f32[9,64,128]{2,1,0:T(8,128)S(1)} %collective-permute-done.1.near, f32[9,64,128]{2,1,0:T(8,128)S(1)} %collective-permute-done.2.far), custom_call_target="tpu_custom_call" | custom-call | tf_op jit(solution)/shard_map/pallas_call | solution.py:387
  18.2 0.0 collective-permute-done.4.refs_1_
  18.2 5.9 %shard_map.89 = f32[80,128]{1,0:T(8,128)S(1)} custom-call(f32[904,128]{1,0:T(8,128)S(1)} %collective-permute-done.refs_0_, f32[904,128]{1,0:T(8,128)S(1)} %collective-permute-done.4.refs_1_, bf16[2,576,256]{2,1,0:T(8,128)(2,1)S(1)} %get-tuple-element.16.refs_2_, f32[80,128]{1,0:T(8,128)S(1)} %get-tuple-element.17.refs_3_), custom_call_target="tpu_custom_call" | custom-call | tf_op jit(solution)/shard_map/pallas_call | solution.py:403
  24.2 10.7 %all-gather = f32[640,128]{1,0:T(8,128)S(1)} all-gather(f32[80,128]{1,0:T(8,128)S(1)} %shard_map.89), channel_id=2, replica_groups=mesh['seg'=2,'strip'=4,'tile'=4] {'seg','tile'}, dimensions={0}, use_global_device_ids=true | all-gather | bytes 368640 | tf_op jit(solution)/shard_map/all_gather | solution.py:582
  34.9 0.0 copy-done
  34.9 1.8 %shard_map.90 = (f32[3,64,128]{2,1,0:T(8,128)}, f32[6,1,128]{2,1,0:T(1,128)}) custom-call(s32[1,64]{1,0:T(1,128)S(1)} %copy-done, f32[8,80,128]{2,1,0:T(8,128)S(1)} %bitcast.8, f32[904,128]{1,0:T(8,128)S(1)} %get-tuple-element.11.refs_0_.points_ref), custom_call_target="tpu_custom_call" | custom-call | tf_op jit(solution)/shard_map/pallas_call | solution.py:583
Async XLA Ops:
  1.8 5.3 %collective-permute-start.3 = (f32[904,128]{1,0:T(8,128)S(1)}, f32[904,128]{1,0:T(8,128)S(1)}, u32[]{:S(2)}, u32[]{:S(2)}) collective-permute-start(f32[904,128]{1,0:T(8,128)S(1)} %get-tuple-element.11.refs_0_.points_ref), channel_id=1, source_target_pairs={{0,1},{1,0},{2,3},{3,2},{4,5},{5,4},{6,7},{7,6},{8,9},{9,8},{10,11... | collective-permute-start | bytes 1388552 | tf_op jit(solution)/shard_map/ppermute | solution.py:577
  2.3 13.8 %collective-permute-start = (f32[904,128]{1,0:T(8,128)S(1)}, f32[904,128]{1,0:T(8,128)S(1)}, u32[]{:S(2)}, u32[]{:S(2)}) collective-permute-start(f32[904,128]{1,0:T(8,128)S(1)} %get-tuple-element.11.refs_0_.points_ref), channel_id=1, source_target_pairs={{2,0},{3,1},{0,2},{1,3},{6,4},{7,5},{4,6},{5,7},{10,8},{11,9},{8,1... | collective-permute-start | bytes 1388552 | tf_op jit(solution)/shard_map/ppermute | solution.py:575
  4.9 9.1 %collective-permute-start.1 = (f32[9,64,128]{2,1,0:T(8,128)S(1)}, f32[9,64,128]{2,1,0:T(8,128)S(1)}, u32[]{:S(2)}, u32[]{:S(2)}) collective-permute-start(f32[9,64,128]{2,1,0:T(8,128)S(1)} %get-tuple-element.12), channel_id=1, source_target_pairs={{0,4},{4,0},{8,12},{12,8},{1,5},{5,1},{9,13},{13,9},{2,6},{6,2},{1... | collective-permute-start | bytes 884744 | tf_op jit(solution)/shard_map/ppermute | solution.py:569
  6.4 7.5 %collective-permute-start.2 = (f32[9,64,128]{2,1,0:T(8,128)S(1)}, f32[9,64,128]{2,1,0:T(8,128)S(1)}, u32[]{:S(2)}, u32[]{:S(2)}) collective-permute-start(f32[9,64,128]{2,1,0:T(8,128)S(1)} %get-tuple-element.12), channel_id=1, source_target_pairs={{4,8},{8,4},{5,9},{9,5},{6,10},{10,6},{7,11},{11,7},{20,24},{24,20... | collective-permute-start | bytes 884744 | tf_op jit(solution)/shard_map/ppermute | solution.py:569
  16.1 2.2 %collective-permute-start.4 = (f32[904,128]{1,0:T(8,128)S(1)}, f32[904,128]{1,0:T(8,128)S(1)}, u32[]{:S(2)}, u32[]{:S(2)}) collective-permute-start(f32[904,128]{1,0:T(8,128)S(1)} %collective-permute-done.refs_0_), channel_id=1, source_target_pairs={{0,1},{1,0},{2,3},{3,2},{4,5},{5,4},{6,7},{7,6},{8,9},{9,8},{10,11... | collective-permute-start | bytes 1388552 | tf_op jit(solution)/shard_map/ppermute | solution.py:580
  16.1 18.8 %copy-start = (s32[1,64]{1,0:T(1,128)S(1)}, s32[1,64]{1,0:T(1,128)}, u32[]{:S(2)}) copy-start(s32[1,64]{1,0:T(1,128)} %knot_ref.1) | copy-start | bytes 772

commit v4 on v3

--- a/solution.py
+++ b/solution.py
@@ -85,10 +85,9 @@
 
     def ordered(size, test):
         rows = lax.broadcasted_iota(jnp.int32, (size, size), 0)
-        return jnp.where(test(rows, lax.broadcasted_iota(jnp.int32, (size, size), 1)), 1.0, 0.0)
-
-    upper = ordered(TILE_PTS, lambda row, lane: row <= lane).astype(jnp.bfloat16)
-    lower = ordered(total, lambda row, lane: row > lane).astype(jnp.bfloat16)
+        marks = test(rows, lax.broadcasted_iota(jnp.int32, (size, size), 1))
+        return jnp.where(marks, 1.0, 0.0).astype(jnp.bfloat16)
+
     member = lax.axis_index("tile")
     near = jnp.where(lax.axis_index("strip") % 2 == 1, 0.0, 1.0)
 
@@ -98,42 +97,56 @@
             jnp.broadcast_to(group[at : at + 1, :], shape), own_tile, axis=1, mode="promise_in_bounds"
         )
 
-    ranks, numbers, farther = [], [], []
+    marks = []
     for group in points:
         index = group[PARTNER * tiles : (PARTNER + 1) * tiles, :].astype(jnp.int32)
         offset = lax.shift_right_logical(index, 7) - member * tiles
-        side = tile_value(group, 0)
-        wanted = (offset >= 0) & (offset < tiles) & (side != 2.0)
-        marks = jnp.where(wanted, 1.0, 0.0).astype(jnp.bfloat16)
-        rank = jnp.dot(marks, upper, preferred_element_type=jnp.float32)
-        ranks.append(rank.astype(jnp.int32))
-        numbers.append(jnp.broadcast_to(rank[:, TILE_PTS - 1 :], shape))
-        farther.append(jnp.where(side == near, 0.0, 1.0))
-    number, far = jnp.concatenate(numbers, axis=0), jnp.concatenate(farther, axis=0)
-    ends = []
-    for chosen in (number * (1.0 - far), number * far):
-        before = jnp.dot(lower, chosen.astype(jnp.bfloat16), preferred_element_type=jnp.float32)
-        ends.append((before.astype(jnp.int32), (before + chosen).astype(jnp.int32)))
-    start = jnp.where(far > 0.0, ends[1][0], ends[0][0])
+        wanted = (offset >= 0) & (offset < tiles) & (tile_value(group, 0) != 2.0)
+        marks.append(jnp.where(wanted, 1.0, 0.0).astype(jnp.bfloat16))
+    marks = jnp.concatenate(marks, axis=0)
+    number = lax.dot_general(
+        jnp.ones((16, TILE_PTS), jnp.bfloat16),
+        marks,
+        (((1,), (1,)), ((), ())),
+        preferred_element_type=jnp.float32,
+    )
+    base = TILE_ROW * tiles
+    sides = jnp.concatenate([group[base : base + 1, 0:tiles] for group in points], axis=1)
+    far = jnp.broadcast_to(jnp.where(sides == near, 0.0, 1.0), number.shape)
+    upper_rows = lax.broadcasted_iota(jnp.int32, number.shape, 0) < 8
+    chosen = jnp.where(upper_rows, number * (1.0 - far), number * far)
+    before = jnp.dot(
+        chosen.astype(jnp.bfloat16),
+        ordered(total, lambda row, lane: row < lane),
+        preferred_element_type=jnp.float32,
+    )
+    ends = (before + chosen).astype(jnp.int32)
+    before = before.astype(jnp.int32)
+    far = far[0:8] > 0.0
+    start = jnp.where(far, before[8:16], before[0:8])
     row = lax.shift_right_logical(start, 7)
-    first = jnp.where(far > 0.0, room - 1 - row, row) * POINT_ROWS
-    second = jnp.where(far > 0.0, first - POINT_ROWS, first + POINT_ROWS)
-    lane = lax.broadcasted_iota(jnp.int32, (total, TILE_PTS), 1)
-    code = jnp.where(lane == 0, first, jnp.where(lane == 1, second, start & (TILE_PTS - 1)))
-    code = jnp.where(lane == 3, ends[0][1], jnp.where(lane == 4, ends[1][1], code))
+    first = jnp.where(far, room - 1 - row, row) * POINT_ROWS
+    second = jnp.where(far, first - POINT_ROWS, first + POINT_ROWS)
+    line = lax.broadcasted_iota(jnp.int32, (8, total), 0)
+    code = jnp.where(line == 0, first, jnp.where(line == 1, second, start & (TILE_PTS - 1)))
+    code = jnp.where(line == 3, ends[0:8], jnp.where(line == 4, ends[8:16], code))
     codes[...] = code
     copy = pltpu.make_async_copy(codes, places, sem.at[0])
     copy.start()
+    ranks = jnp.dot(
+        marks, ordered(TILE_PTS, lambda row, lane: row <= lane), preferred_element_type=jnp.float32
+    ).astype(jnp.int32)
     for p, group in enumerate(points):
+        rank = ranks[p * tiles : (p + 1) * tiles]
         source = jnp.zeros_like(lanes)
         for jump in (64, 32, 16, 8, 4, 2, 1):
             there = jnp.take_along_axis(
-                ranks[p], source + (jump - 1), axis=1, mode="promise_in_bounds"
+                rank, source + (jump - 1), axis=1, mode="promise_in_bounds"
             )
             source = jnp.where(there <= lanes, source + jump, source)
         for channel in range(POINT_ROWS):
             if channel == VALID:
-                value = jnp.where(lanes.astype(jnp.float32) < numbers[p], 1.0, 0.0)
+                value = jnp.where(lanes < jnp.broadcast_to(rank[:, TILE_PTS - 1 :], shape), 1.0, 0.0)
             elif channel == KNOT:
                 value = tile_value(group, 1)
             else:
@@ -149,13 +162,13 @@
         return pl.ds(pl.multiple_of(first, POINT_ROWS), POINT_ROWS)
 
     def place(tile):
-        shift = places[tile, 2]
+        shift = places[2, tile]
         value = pltpu.roll(compact[span(tile * POINT_ROWS), :], shift, 1)
-        at = span(places[tile, 0])
+        at = span(places[0, tile])
         packed[at, :] = jnp.where(wide >= shift, value, packed[at, :])
-        packed[span(places[tile, 1]), :] = jnp.where(wide < shift, value, 0.0)
-
-    unroll = 16
+        packed[span(places[1, tile]), :] = jnp.where(wide < shift, value, 0.0)
+
+    unroll = tiles
 
     def several(step, carry):
         for tile in range(unroll):
@@ -163,8 +176,8 @@
         return carry
 
     lax.fori_loop(0, total // unroll, several, 0)
-    near_rows = lax.shift_right_logical(places[total - 1, 3] + TILE_PTS - 1, 7)
-    far_rows = lax.shift_right_logical(places[total - 1, 4] + TILE_PTS - 1, 7)
+    near_rows = lax.shift_right_logical(places[3, total - 1] + TILE_PTS - 1, 7)
+    far_rows = lax.shift_right_logical(places[4, total - 1] + TILE_PTS - 1, 7)
     blank = jnp.zeros((POINT_ROWS, TILE_PTS), jnp.float32)
     for extra in range(ROW_GROUP):
         packed[span((near_rows + extra) * POINT_ROWS), :] = blank
@@ -350,8 +363,8 @@
     count = groups * tiles
     return [
         pltpu.VMEM((count * POINT_ROWS, TILE_PTS), jnp.float32),
-        pltpu.VMEM((count, TILE_PTS), jnp.int32),
-        pltpu.SMEM((count, TILE_PTS), jnp.int32),
+        pltpu.VMEM((8, count), jnp.int32),
+        pltpu.SMEM((8, count), jnp.int32),
         pltpu.SemaphoreType.DMA((1,)),
     ]
 

time: 36.9 us -> 36.1 us (0.978)
  Pallas kernels: 14.4 us -> 12.4 us
  waiting for transfers between devices: 5.58 us -> 6.42 us
  blocking collectives: 10.7 us -> 11.2 us
    pallas_call x1, Pallas kernels: 5.95 us -> 4.75 us  [all_totals(): pl.pallas_call(functools.partial(other_kernel, groups), out_shape=jax.Sha...]
    pallas_call x1, Pallas kernels: 3.36 us -> 2.51 us  [early_rows(): pl.pallas_call(functools.partial(early_kernel, groups), out_shape=(jax.Sh...]
    ppermute x2, waiting for transfers between devices: 3.46 us -> 4.3 us  [trade(): return lax.ppermute(table, 'strip', pairs)]
    all_gather x1, blocking collectives: 10.7 us -> 11.2 us  [local(): all_sums = lax.all_gather(sums, ('seg', 'tile'), axis=0)]
  transfers between devices with their start and end apart: 5 -> 5, of which waited for: 2 -> 2; matrix products, arithmetic and copies ran while one was open for 0% -> 0% of each run, Pallas kernels for 15% -> 13%
where the time goes in v4:
time: 36.1 us
  Pallas kernels  12.4 us (34%)
  blocking collectives  11.2 us (31%)
  waiting for transfers between devices  6.42 us (18%)
  starting transfers between devices  5.33 us (15%)
  between operations  0.69 us (2%)
    all_gather x1, blocking collectives, local(): all_sums = lax.all_gather(sums, ('seg', 'tile'), axis=0)  11.2 us
    pallas_call x1, Pallas kernels, all_totals(): pl.pallas_call(functools.partial(other_kernel, groups), out_shape=jax.Sha...  4.75 us
    ppermute x2, waiting for transfers between devices, trade(): return lax.ppermute(table, 'strip', pairs)  4.3 us
    ppermute x1, starting transfers between devices, local(): arrived.append(lax.ppermute(points, 'tile', pairs))  2.56 us
    pallas_call x1, Pallas kernels, early_rows(): pl.pallas_call(functools.partial(early_kernel, groups), out_shape=(jax.Sh...  2.51 us
    ppermute x2, starting transfers between devices, trade(): return lax.ppermute(table, 'strip', pairs)  2.24 us
    pallas_call x1, Pallas kernels, own_totals(): pl.pallas_call(own_kernel, out_shape=(jax.ShapeDtypeStruct((2, CHANNELS *...  2.15 us
    ppermute x1, waiting for transfers between devices, local(): arrived.append(lax.ppermute(points, 'tile', pairs))  2.12 us
  transfers between devices with their start and end apart: 5, of which 2 were waited for; matrix products, arithmetic and copies ran while one was open for 0% of the time, Pallas kernels for 13%

profile of v4, /device:TPU:0, one launch (start us, length us, event | category | flops | bytes accessed | tf_op | source)
XLA Modules:
  0.0 36.1 jit_solution(15706717467077584356)
XLA Ops:
  0.6 1.1 %shard_map.86 = (f32[9,64,128]{2,1,0:T(8,128)S(1)}, f32[904,128]{1,0:T(8,128)S(1)}) custom-call(f32[3,64,128]{2,1,0:T(8,128)} %bitcast.10, f32[6,64,128]{2,1,0:T(8,128)} %bitcast.9, f32[3,64,128]{2,1,0:T(8,128)} %bitcast.11, f32[64,128]{1,0:T(8,128)} %bitcast.12, s32[64,128]{1,0:T(8,128)} %bitcast.13, s32[1,64]{1,0:T(1,128)} %sides.1, s32[1,64]{1,0:T(1,128)} %knot_ref.1), custom_call_target="tpu_custom_call" | custom-call | tf_op jit(solution)/shard_map/pallas_call | solution.py:549
  1.8 0.5 %collective-permute-start.3 = (f32[904,128]{1,0:T(8,128)S(1)}, f32[904,128]{1,0:T(8,128)S(1)}, u32[]{:S(2)}, u32[]{:S(2)}) collective-permute-start(f32[904,128]{1,0:T(8,128)S(1)} %get-tuple-element.11.refs_0_.points_ref), channel_id=1, source_target_pairs={{0,1},{1,0},{2,3},{3,2},{4,5},{5,4},{6,7},{7,6},{8,9},{9,8},{10,11... | collective-permute-start | bytes 1388552 | tf_op jit(solution)/shard_map/ppermute | solution.py:590
  2.3 2.6 %collective-permute-start = (f32[904,128]{1,0:T(8,128)S(1)}, f32[904,128]{1,0:T(8,128)S(1)}, u32[]{:S(2)}, u32[]{:S(2)}) collective-permute-start(f32[904,128]{1,0:T(8,128)S(1)} %get-tuple-element.11.refs_0_.points_ref), channel_id=1, source_target_pairs={{2,0},{3,1},{0,2},{1,3},{6,4},{7,5},{4,6},{5,7},{10,8},{11,9},{8,1... | collective-permute-start | bytes 1388552 | tf_op jit(solution)/shard_map/ppermute | solution.py:588
  4.9 1.6 %collective-permute-start.1 = (f32[9,64,128]{2,1,0:T(8,128)S(1)}, f32[9,64,128]{2,1,0:T(8,128)S(1)}, u32[]{:S(2)}, u32[]{:S(2)}) collective-permute-start(f32[9,64,128]{2,1,0:T(8,128)S(1)} %get-tuple-element.12), channel_id=1, source_target_pairs={{0,4},{4,0},{8,12},{12,8},{1,5},{5,1},{9,13},{13,9},{2,6},{6,2},{1... | collective-permute-start | bytes 884744 | tf_op jit(solution)/shard_map/ppermute | solution.py:582
  6.4 0.7 %collective-permute-start.2 = (f32[9,64,128]{2,1,0:T(8,128)S(1)}, f32[9,64,128]{2,1,0:T(8,128)S(1)}, u32[]{:S(2)}, u32[]{:S(2)}) collective-permute-start(f32[9,64,128]{2,1,0:T(8,128)S(1)} %get-tuple-element.12), channel_id=1, source_target_pairs={{4,8},{8,4},{5,9},{9,5},{6,10},{10,6},{7,11},{11,7},{20,24},{24,20... | collective-permute-start | bytes 884744 | tf_op jit(solution)/shard_map/ppermute | solution.py:582
  7.1 0.0 collective-permute-done.3.refs_1_
  7.1 2.5 %shard_map.87 = (f32[3072,128]{1,0:T(8,128)S(1)}, s32[8,128]{1,0:T(8,128)S(1)}) custom-call(f32[904,128]{1,0:T(8,128)S(1)} %get-tuple-element.11.refs_0_.points_ref, f32[904,128]{1,0:T(8,128)S(1)} %collective-permute-done.3.refs_1_), custom_call_target="tpu_custom_call" | custom-call | tf_op jit(solution)/shard_map/pallas_call | solution.py:385
  9.6 4.3 %collective-permute-done.1.near = f32[9,64,128]{2,1,0:T(8,128)S(1)} collective-permute-done((f32[9,64,128]{2,1,0:T(8,128)S(1)}, f32[9,64,128]{2,1,0:T(8,128)S(1)}, u32[]{:S(2)}, u32[]{:S(2)}) %collective-permute-start.1) | collective-permute-done | bytes 294944 | tf_op jit(solution)/shard_map/ppermute | solution.py:582
  13.9 0.0 collective-permute-done.2.far
  13.9 2.1 %collective-permute-done.refs_0_ = f32[904,128]{1,0:T(8,128)S(1)} collective-permute-done((f32[904,128]{1,0:T(8,128)S(1)}, f32[904,128]{1,0:T(8,128)S(1)}, u32[]{:S(2)}, u32[]{:S(2)}) %collective-permute-start) | collective-permute-done | bytes 462880 | tf_op jit(solution)/shard_map/ppermute | solution.py:588
  16.1 0.0 collective-permute-start.4
  16.1 0.0 copy-start
  16.1 2.1 %shard_map.88 = (bf16[2,576,256]{2,1,0:T(8,128)(2,1)S(1)}, f32[80,128]{1,0:T(8,128)S(1)}) custom-call(f32[3072,128]{1,0:T(8,128)S(1)} %get-tuple-element.13.packed, s32[8,128]{1,0:T(8,128)S(1)} %get-tuple-element.15.rows_ref, f32[9,64,128]{2,1,0:T(8,128)S(1)} %collective-permute-done.1.near, f32[9,64,128]{2,1,0:T(8,128)S(1)} %collective-permute-done.2.far), custom_call_target="tpu_custom_call" | custom-call | tf_op jit(solution)/shard_map/pallas_call | solution.py:400
  18.2 0.0 collective-permute-done.4.refs_1_
  18.2 4.7 %shard_map.89 = f32[80,128]{1,0:T(8,128)S(1)} custom-call(f32[904,128]{1,0:T(8,128)S(1)} %collective-permute-done.refs_0_, f32[904,128]{1,0:T(8,128)S(1)} %collective-permute-done.4.refs_1_, bf16[2,576,256]{2,1,0:T(8,128)(2,1)S(1)} %get-tuple-element.16.refs_2_, f32[80,128]{1,0:T(8,128)S(1)} %get-tuple-element.17.refs_3_), custom_call_target="tpu_custom_call" | custom-call | tf_op jit(solution)/shard_map/pallas_call | solution.py:416
  23.0 11.2 %all-gather = f32[640,128]{1,0:T(8,128)S(1)} all-gather(f32[80,128]{1,0:T(8,128)S(1)} %shard_map.89), channel_id=2, replica_groups=mesh['seg'=2,'strip'=4,'tile'=4] {'seg','tile'}, dimensions={0}, use_global_device_ids=true | all-gather | bytes 368640 | tf_op jit(solution)/shard_map/all_gather | solution.py:595
  34.2 0.0 copy-done
  34.2 1.8 %shard_map.90 = (f32[3,64,128]{2,1,0:T(8,128)}, f32[6,1,128]{2,1,0:T(1,128)}) custom-call(s32[1,64]{1,0:T(1,128)S(1)} %copy-done, f32[8,80,128]{2,1,0:T(8,128)S(1)} %bitcast.8, f32[904,128]{1,0:T(8,128)S(1)} %get-tuple-element.11.refs_0_.points_ref), custom_call_target="tpu_custom_call" | custom-call | tf_op jit(solution)/shard_map/pallas_call | solution.py:596
Async XLA Ops:
  1.8 5.3 %collective-permute-start.3 = (f32[904,128]{1,0:T(8,128)S(1)}, f32[904,128]{1,0:T(8,128)S(1)}, u32[]{:S(2)}, u32[]{:S(2)}) collective-permute-start(f32[904,128]{1,0:T(8,128)S(1)} %get-tuple-element.11.refs_0_.points_ref), channel_id=1, source_target_pairs={{0,1},{1,0},{2,3},{3,2},{4,5},{5,4},{6,7},{7,6},{8,9},{9,8},{10,11... | collective-permute-start | bytes 1388552 | tf_op jit(solution)/shard_map/ppermute | solution.py:590
  2.3 13.8 %collective-permute-start = (f32[904,128]{1,0:T(8,128)S(1)}, f32[904,128]{1,0:T(8,128)S(1)}, u32[]{:S(2)}, u32[]{:S(2)}) collective-permute-start(f32[904,128]{1,0:T(8,128)S(1)} %get-tuple-element.11.refs_0_.points_ref), channel_id=1, source_target_pairs={{2,0},{3,1},{0,2},{1,3},{6,4},{7,5},{4,6},{5,7},{10,8},{11,9},{8,1... | collective-permute-start | bytes 1388552 | tf_op jit(solution)/shard_map/ppermute | solution.py:588
  4.9 9.1 %collective-permute-start.1 = (f32[9,64,128]{2,1,0:T(8,128)S(1)}, f32[9,64,128]{2,1,0:T(8,128)S(1)}, u32[]{:S(2)}, u32[]{:S(2)}) collective-permute-start(f32[9,64,128]{2,1,0:T(8,128)S(1)} %get-tuple-element.12), channel_id=1, source_target_pairs={{0,4},{4,0},{8,12},{12,8},{1,5},{5,1},{9,13},{13,9},{2,6},{6,2},{1... | collective-permute-start | bytes 884744 | tf_op jit(solution)/shard_map/ppermute | solution.py:582
  6.4 7.5 %collective-permute-start.2 = (f32[9,64,128]{2,1,0:T(8,128)S(1)}, f32[9,64,128]{2,1,0:T(8,128)S(1)}, u32[]{:S(2)}, u32[]{:S(2)}) collective-permute-start(f32[9,64,128]{2,1,0:T(8,128)S(1)} %get-tuple-element.12), channel_id=1, source_target_pairs={{4,8},{8,4},{5,9},{9,5},{6,10},{10,6},{7,11},{11,7},{20,24},{24,20... | collective-permute-start | bytes 884744 | tf_op jit(solution)/shard_map/ppermute | solution.py:582
  16.1 2.2 %collective-permute-start.4 = (f32[904,128]{1,0:T(8,128)S(1)}, f32[904,128]{1,0:T(8,128)S(1)}, u32[]{:S(2)}, u32[]{:S(2)}) collective-permute-start(f32[904,128]{1,0:T(8,128)S(1)} %collective-permute-done.refs_0_), channel_id=1, source_target_pairs={{0,1},{1,0},{2,3},{3,2},{4,5},{5,4},{6,7},{7,6},{8,9},{9,8},{10,11... | collective-permute-start | bytes 1388552 | tf_op jit(solution)/shard_map/ppermute | solution.py:593
  16.1 18.2 %copy-start = (s32[1,64]{1,0:T(1,128)S(1)}, s32[1,64]{1,0:T(1,128)}, u32[]{:S(2)}) copy-start(s32[1,64]{1,0:T(1,128)} %knot_ref.1) | copy-start | bytes 772

commit v5 on v4

--- a/solution.py
+++ b/solution.py
@@ -341,13 +341,22 @@
     rows_ref[4:8, :] = jnp.full((4, TILE_PTS), far_rows, jnp.int32)
 
 
-def own_kernel(packed, rows_ref, near, far, weights, totals_ref, rows_here, sem, *work):
+def near_kernel(packed, rows_ref, near, weights, totals_ref, rows_here, sem, *work):
     copy = pltpu.make_async_copy(rows_ref, rows_here, sem.at[0])
     copy.start()
     weigh_table(near, weights, 0)
+    copy.wait()
+    process(packed, rows_here[0, 0], jnp.int32(0), weights, totals_ref, work)
+
+
+def far_kernel(packed, rows_ref, far, before, before_ref, weights, totals_ref, rows_here, sem, *work):
+    copy = pltpu.make_async_copy(rows_ref, rows_here, sem.at[0])
+    copy.start()
+    weights[0] = before[0]
     weigh_table(far, weights, 1)
     copy.wait()
-    process(packed, rows_here[0, 0], rows_here[4, 0], weights, totals_ref, work)
+    process(packed, jnp.int32(0), rows_here[4, 0], weights, totals_ref, work)
+    totals_ref[...] = totals_ref[...] + before_ref[...]
 
 
 def other_kernel(groups, *refs):
@@ -395,20 +404,20 @@
     )(*points)
 
 
-def own_totals(groups, packed, rows, near, far):
-    tiles = near.shape[1]
+def own_totals(kernel, slots, packed, rows, table, *before):
+    tiles = table.shape[1]
     return pl.pallas_call(
-        own_kernel,
+        kernel,
         out_shape=(
-            jax.ShapeDtypeStruct((2, CHANNELS * tiles, 2 * TILE_PTS), jnp.bfloat16),
+            jax.ShapeDtypeStruct((slots, CHANNELS * tiles, 2 * TILE_PTS), jnp.bfloat16),
             jax.ShapeDtypeStruct((SUM_ROWS, KNOT_DEV), jnp.float32),
         ),
-        in_specs=vmem(4),
+        in_specs=vmem(3 + len(before)),
         out_specs=(pl.BlockSpec(memory_space=pltpu.VMEM),) * 2,
         scratch_shapes=[pltpu.SMEM((8, TILE_PTS), jnp.int32), pltpu.SemaphoreType.DMA((1,))]
-        + process_shapes(groups, tiles),
+        + process_shapes(2, tiles),
         compiler_params=params(14),
-    )(packed, rows, near, far)
+    )(packed, rows, table, *before)
 
 
 def all_totals(points, weights, totals):
@@ -588,8 +597,9 @@
         arrived.append(lax.ppermute(points, "tile", pairs))
     near, far = trade(0), trade(1)
     packed, rows = early_rows([points, lax.ppermute(points, "tile", swap)])
-    weights, totals = own_totals(2, packed, rows, near, far)
-    arrived = lax.optimization_barrier((arrived, near, far, packed))[0]
+    weights, totals = own_totals(near_kernel, 1, packed, rows, near)
+    arrived = lax.optimization_barrier((arrived, totals, far))[0]
+    weights, totals = own_totals(far_kernel, 2, packed, rows, far, weights, totals)
     others = arrived + [lax.ppermute(group, "tile", swap) for group in arrived]
     sums = all_totals(others, weights, totals)
     all_sums = lax.all_gather(sums, ("seg", "tile"), axis=0)

time: 36.1 us -> 35.2 us (0.975)
  blocking collectives: 11.2 us -> 9.44 us
  Pallas kernels: 12.4 us -> 14.1 us
  waiting for transfers between devices: 6.42 us -> 5.44 us
    ppermute x1, waiting for transfers between devices: 2.12 us -> 0.01 us  [local(): arrived.append(lax.ppermute(points, 'tile', pairs))]
    all_gather x1, blocking collectives: 11.2 us -> 9.44 us  [local(): all_sums = lax.all_gather(sums, ('seg', 'tile'), axis=0)]
    pallas_call x1 -> x2, Pallas kernels: 2.15 us -> 3.79 us  [own_totals(): pl.pallas_call(kernel, out_shape=(jax.ShapeDtypeStruct((slots, CHANNELS *...]
    ppermute x1, waiting for transfers between devices: 0.01 us -> 1.15 us  [local(): others = arrived + [lax.ppermute(group, 'tile', swap) for group in arrived]]
  transfers between devices with their start and end apart: 5 -> 5, of which waited for: 2 -> 2; matrix products, arithmetic and copies ran while one was open for 0% -> 0% of each run, Pallas kernels for 13% -> 18%
where the time goes in v5:
time: 35.2 us; the launch traced here: 35.1 us
  Pallas kernels  14.1 us (40%)
  blocking collectives  9.44 us (27%)
  waiting for transfers between devices  5.44 us (15%)
  starting transfers between devices  5.4 us (15%)
  between operations  0.72 us (2%)
    all_gather x1, blocking collectives, local(): all_sums = lax.all_gather(sums, ('seg', 'tile'), axis=0)  9.44 us
    pallas_call x1, Pallas kernels, all_totals(): pl.pallas_call(functools.partial(other_kernel, groups), out_shape=jax.Sha...  4.76 us
    ppermute x2, waiting for transfers between devices, trade(): return lax.ppermute(table, 'strip', pairs)  4.28 us
    pallas_call x2, Pallas kernels, own_totals(): pl.pallas_call(kernel, out_shape=(jax.ShapeDtypeStruct((slots, CHANNELS *...  3.79 us
    ppermute x1, starting transfers between devices, local(): arrived.append(lax.ppermute(points, 'tile', pairs))  2.56 us
    pallas_call x1, Pallas kernels, early_rows(): pl.pallas_call(functools.partial(early_kernel, groups), out_shape=(jax.Sh...  2.54 us
    ppermute x2, starting transfers between devices, trade(): return lax.ppermute(table, 'strip', pairs)  2.24 us
    pallas_call x1, Pallas kernels, local(): pl.pallas_call(functools.partial(step_kernel, segs, members), out_shape=(...  1.83 us
  transfers between devices with their start and end apart: 5, of which 2 were waited for; matrix products, arithmetic and copies ran while one was open for 0% of the time, Pallas kernels for 18%

profile of v5, /device:TPU:0, one launch (start us, length us, event | category | flops | bytes accessed | tf_op | source)
XLA Modules:
  0.0 35.1 jit_solution(17599096075192868255)
XLA Ops:
  0.6 1.1 %shard_map.86 = (f32[9,64,128]{2,1,0:T(8,128)S(1)}, f32[904,128]{1,0:T(8,128)S(1)}) custom-call(f32[3,64,128]{2,1,0:T(8,128)} %bitcast.10, f32[6,64,128]{2,1,0:T(8,128)} %bitcast.9, f32[3,64,128]{2,1,0:T(8,128)} %bitcast.11, f32[64,128]{1,0:T(8,128)} %bitcast.12, s32[64,128]{1,0:T(8,128)} %bitcast.13, s32[1,64]{1,0:T(1,128)} %sides.1, s32[1,64]{1,0:T(1,128)} %knot_ref.1), custom_call_target="tpu_custom_call" | custom-call | tf_op jit(solution)/shard_map/pallas_call | solution.py:558
  1.8 0.5 %collective-permute-start.1 = (f32[904,128]{1,0:T(8,128)S(1)}, f32[904,128]{1,0:T(8,128)S(1)}, u32[]{:S(2)}, u32[]{:S(2)}) collective-permute-start(f32[904,128]{1,0:T(8,128)S(1)} %get-tuple-element.13.refs_0_.points_ref), channel_id=1, source_target_pairs={{0,1},{1,0},{2,3},{3,2},{4,5},{5,4},{6,7},{7,6},{8,9},{9,8},{10,11... | collective-permute-start | bytes 1388552 | tf_op jit(solution)/shard_map/ppermute | solution.py:599
  2.3 2.6 %collective-permute-start = (f32[904,128]{1,0:T(8,128)S(1)}, f32[904,128]{1,0:T(8,128)S(1)}, u32[]{:S(2)}, u32[]{:S(2)}) collective-permute-start(f32[904,128]{1,0:T(8,128)S(1)} %get-tuple-element.13.refs_0_.points_ref), channel_id=1, source_target_pairs={{2,0},{3,1},{0,2},{1,3},{6,4},{7,5},{4,6},{5,7},{10,8},{11,9},{8,1... | collective-permute-start | bytes 1388552 | tf_op jit(solution)/shard_map/ppermute | solution.py:597
  4.9 1.6 %collective-permute-start.2 = (f32[9,64,128]{2,1,0:T(8,128)S(1)}, f32[9,64,128]{2,1,0:T(8,128)S(1)}, u32[]{:S(2)}, u32[]{:S(2)}) collective-permute-start(f32[9,64,128]{2,1,0:T(8,128)S(1)} %get-tuple-element.16), channel_id=1, source_target_pairs={{0,4},{4,0},{8,12},{12,8},{1,5},{5,1},{9,13},{13,9},{2,6},{6,2},{1... | collective-permute-start | bytes 884744 | tf_op jit(solution)/shard_map/ppermute | solution.py:591
  6.4 0.7 %collective-permute-start.3 = (f32[9,64,128]{2,1,0:T(8,128)S(1)}, f32[9,64,128]{2,1,0:T(8,128)S(1)}, u32[]{:S(2)}, u32[]{:S(2)}) collective-permute-start(f32[9,64,128]{2,1,0:T(8,128)S(1)} %get-tuple-element.16), channel_id=1, source_target_pairs={{4,8},{8,4},{5,9},{9,5},{6,10},{10,6},{7,11},{11,7},{20,24},{24,20... | collective-permute-start | bytes 884744 | tf_op jit(solution)/shard_map/ppermute | solution.py:591
  7.1 0.0 collective-permute-done.1.refs_1_
  7.1 2.5 %shard_map.87 = (f32[3072,128]{1,0:T(8,128)S(1)}, s32[8,128]{1,0:T(8,128)S(1)}) custom-call(f32[904,128]{1,0:T(8,128)S(1)} %get-tuple-element.13.refs_0_.points_ref, f32[904,128]{1,0:T(8,128)S(1)} %collective-permute-done.1.refs_1_), custom_call_target="tpu_custom_call" | custom-call | tf_op jit(solution)/shard_map/pallas_call | solution.py:394
  9.7 4.3 %collective-permute-done.2.near = f32[9,64,128]{2,1,0:T(8,128)S(1)} collective-permute-done((f32[9,64,128]{2,1,0:T(8,128)S(1)}, f32[9,64,128]{2,1,0:T(8,128)S(1)}, u32[]{:S(2)}, u32[]{:S(2)}) %collective-permute-start.2) | collective-permute-done | bytes 294944 | tf_op jit(solution)/shard_map/ppermute | solution.py:591
  13.9 3.2 %shard_map.88 = (bf16[1,576,256]{2,1,0:T(8,128)(2,1)S(1)}, f32[80,128]{1,0:T(8,128)S(1)}) custom-call(f32[3072,128]{1,0:T(8,128)S(1)} %get-tuple-element.14.packed, s32[8,128]{1,0:T(8,128)S(1)} %get-tuple-element.15.rows_ref, f32[9,64,128]{2,1,0:T(8,128)S(1)} %collective-permute-done.2.near), custom_call_target="tpu_custom_call" | custom-call | tf_op jit(solution)/shard_map/pallas_call | solution.py:409
  17.1 0.0 collective-permute-done.3.far
  17.1 0.0 collective-permute-done.refs_0_
  17.1 0.1 collective-permute-start.4
  17.2 0.0 copy-start
  17.2 0.6 %shard_map.89 = (bf16[2,576,256]{2,1,0:T(8,128)(2,1)S(1)}, f32[80,128]{1,0:T(8,128)S(1)}) custom-call(f32[3072,128]{1,0:T(8,128)S(1)} %get-tuple-element.14.packed, s32[8,128]{1,0:T(8,128)S(1)} %get-tuple-element.15.rows_ref, f32[9,64,128]{2,1,0:T(8,128)S(1)} %collective-permute-done.3.far, bf16[1,576,256]{2,1,0:T(8,128)(2,1)S(1)} %get-tuple-element.19.before, ...), custom_call_target="tpu_custom_call" | custom-call | tf_op jit(solution)/shard_map/pallas_call | solution.py:409
  17.9 1.2 %collective-permute-done.4.refs_1_ = f32[904,128]{1,0:T(8,128)S(1)} collective-permute-done((f32[904,128]{1,0:T(8,128)S(1)}, f32[904,128]{1,0:T(8,128)S(1)}, u32[]{:S(2)}, u32[]{:S(2)}) %collective-permute-start.4) | collective-permute-done | bytes 462880 | tf_op jit(solution)/shard_map/ppermute | solution.py:603
  19.0 4.8 %shard_map.90 = f32[80,128]{1,0:T(8,128)S(1)} custom-call(f32[904,128]{1,0:T(8,128)S(1)} %collective-permute-done.refs_0_, f32[904,128]{1,0:T(8,128)S(1)} %collective-permute-done.4.refs_1_, bf16[2,576,256]{2,1,0:T(8,128)(2,1)S(1)} %get-tuple-element.20.refs_2_, f32[80,128]{1,0:T(8,128)S(1)} %get-tuple-element.21.refs_3_), custom_call_target="tpu_custom_call" | custom-call | tf_op jit(solution)/shard_map/pallas_call | solution.py:425
  23.8 9.4 %all-gather = f32[640,128]{1,0:T(8,128)S(1)} all-gather(f32[80,128]{1,0:T(8,128)S(1)} %shard_map.90), channel_id=2, replica_groups=mesh['seg'=2,'strip'=4,'tile'=4] {'seg','tile'}, dimensions={0}, use_global_device_ids=true | all-gather | bytes 368640 | tf_op jit(solution)/shard_map/all_gather | solution.py:605
  33.2 0.0 copy-done
  33.2 1.8 %shard_map.91 = (f32[3,64,128]{2,1,0:T(8,128)}, f32[6,1,128]{2,1,0:T(1,128)}) custom-call(s32[1,64]{1,0:T(1,128)S(1)} %copy-done, f32[8,80,128]{2,1,0:T(8,128)S(1)} %bitcast.8, f32[904,128]{1,0:T(8,128)S(1)} %get-tuple-element.13.refs_0_.points_ref), custom_call_target="tpu_custom_call" | custom-call | tf_op jit(solution)/shard_map/pallas_call | solution.py:606
Async XLA Ops:
  1.8 5.3 %collective-permute-start.1 = (f32[904,128]{1,0:T(8,128)S(1)}, f32[904,128]{1,0:T(8,128)S(1)}, u32[]{:S(2)}, u32[]{:S(2)}) collective-permute-start(f32[904,128]{1,0:T(8,128)S(1)} %get-tuple-element.13.refs_0_.points_ref), channel_id=1, source_target_pairs={{0,1},{1,0},{2,3},{3,2},{4,5},{5,4},{6,7},{7,6},{8,9},{9,8},{10,11... | collective-permute-start | bytes 1388552 | tf_op jit(solution)/shard_map/ppermute | solution.py:599
  2.3 14.8 %collective-permute-start = (f32[904,128]{1,0:T(8,128)S(1)}, f32[904,128]{1,0:T(8,128)S(1)}, u32[]{:S(2)}, u32[]{:S(2)}) collective-permute-start(f32[904,128]{1,0:T(8,128)S(1)} %get-tuple-element.13.refs_0_.points_ref), channel_id=1, source_target_pairs={{2,0},{3,1},{0,2},{1,3},{6,4},{7,5},{4,6},{5,7},{10,8},{11,9},{8,1... | collective-permute-start | bytes 1388552 | tf_op jit(solution)/shard_map/ppermute | solution.py:597
  4.9 9.1 %collective-permute-start.2 = (f32[9,64,128]{2,1,0:T(8,128)S(1)}, f32[9,64,128]{2,1,0:T(8,128)S(1)}, u32[]{:S(2)}, u32[]{:S(2)}) collective-permute-start(f32[9,64,128]{2,1,0:T(8,128)S(1)} %get-tuple-element.16), channel_id=1, source_target_pairs={{0,4},{4,0},{8,12},{12,8},{1,5},{5,1},{9,13},{13,9},{2,6},{6,2},{1... | collective-permute-start | bytes 884744 | tf_op jit(solution)/shard_map/ppermute | solution.py:591
  6.4 10.7 %collective-permute-start.3 = (f32[9,64,128]{2,1,0:T(8,128)S(1)}, f32[9,64,128]{2,1,0:T(8,128)S(1)}, u32[]{:S(2)}, u32[]{:S(2)}) collective-permute-start(f32[9,64,128]{2,1,0:T(8,128)S(1)} %get-tuple-element.16), channel_id=1, source_target_pairs={{4,8},{8,4},{5,9},{9,5},{6,10},{10,6},{7,11},{11,7},{20,24},{24,20... | collective-permute-start | bytes 884744 | tf_op jit(solution)/shard_map/ppermute | solution.py:591
  17.1 1.9 %collective-permute-start.4 = (f32[904,128]{1,0:T(8,128)S(1)}, f32[904,128]{1,0:T(8,128)S(1)}, u32[]{:S(2)}, u32[]{:S(2)}) collective-permute-start(f32[904,128]{1,0:T(8,128)S(1)} %collective-permute-done.refs_0_), channel_id=1, source_target_pairs={{0,1},{1,0},{2,3},{3,2},{4,5},{5,4},{6,7},{7,6},{8,9},{9,8},{10,11... | collective-permute-start | bytes 1388552 | tf_op jit(solution)/shard_map/ppermute | solution.py:603
  17.2 16.0 %copy-start = (s32[1,64]{1,0:T(1,128)S(1)}, s32[1,64]{1,0:T(1,128)}, u32[]{:S(2)}) copy-start(s32[1,64]{1,0:T(1,128)} %knot_ref.1) | copy-start | bytes 772

commit v6 on v5

--- a/solution.py
+++ b/solution.py
@@ -12,6 +12,7 @@
 CHANNELS = 9
 BLOCK_TILES = 4
 ROW_GROUP = 16
+SPREAD = 17
 POINT_ROWS = 16
 PARTNER = 13
 KNOT = 14
@@ -239,7 +240,7 @@
         return ids, [jnp.sum(entry, axis=0, keepdims=True) for entry in found]
 
     def body(step, carry):
-        results = [one_block(2 * step), one_block(2 * step + 1)]
+        results = [one_block(3 * step + i) for i in range(3)]
         for ids, flat in results:
             for channel in range(CHANNELS):
                 for j in range(BLOCK_TILES):
@@ -247,10 +248,10 @@
                     target[channel, pl.ds(ids[j], 1), :] = piece
         return carry
 
-    lax.fori_loop(0, lax.shift_right_logical(blocks + 1, 1), body, 0)
+    lax.fori_loop(0, lax.div(blocks + 2, jnp.int32(3)), body, 0)
 
     totals_ref[...] = jnp.zeros_like(totals_ref)
-    terms_ref[75 * ROW_GROUP :, :] = jnp.zeros((5 * ROW_GROUP, TILE_PTS), jnp.float32)
+    terms_ref[75 * SPREAD :, :] = jnp.zeros((5 * SPREAD, TILE_PTS), jnp.float32)
     near_groups = lax.shift_right_logical(near_rows + ROW_GROUP - 1, 4)
     far_groups = lax.shift_right_logical(far_rows + ROW_GROUP - 1, 4)
 
@@ -313,14 +314,14 @@
     for weight in (early, later):
         terms += [entry * weight for entry in gradient]
     for place, term in enumerate(terms):
-        terms_ref[place * group : (place + 1) * group, :] = term
+        terms_ref[place * SPREAD : place * SPREAD + group, :] = term
     knots = own(KNOT).astype(jnp.int32)
     stacked = lax.broadcasted_iota(jnp.int32, (KNOT_DEV, TILE_PTS), 0)
     total = totals_ref[...]
     for row in range(0, group, 2):
         parts, hots = [], []
         for r in (row, row + 1):
-            high, low = split_two(terms_ref[pl.ds(r, SUM_ROWS, stride=group), :])
+            high, low = split_two(terms_ref[pl.ds(r, SUM_ROWS, stride=SPREAD), :])
             parts.append(jnp.concatenate([high, low], axis=0))
             hots.append(jnp.where(stacked == knots[r : r + 1], 1.0, 0.0).astype(jnp.bfloat16))
         sums = lax.dot_general(
@@ -381,7 +382,7 @@
 def process_shapes(groups, tiles):
     return [
         pltpu.VMEM((CHANNELS, row_room(groups, tiles), TILE_PTS), jnp.float32),
-        pltpu.VMEM((SUM_ROWS * ROW_GROUP, TILE_PTS), jnp.float32),
+        pltpu.VMEM((SUM_ROWS * SPREAD, TILE_PTS), jnp.float32),
     ]
 
 

time: 35.2 us -> 34.8 us (0.989)
  blocking collectives: 9.44 us -> 8.74 us
    all_gather x1, blocking collectives: 9.44 us -> 8.74 us  [local(): all_sums = lax.all_gather(sums, ('seg', 'tile'), axis=0)]
    pallas_call x1, Pallas kernels: 4.76 us -> 5.22 us  [all_totals(): pl.pallas_call(functools.partial(other_kernel, groups), out_shape=jax.Sha...]
  transfers between devices with their start and end apart: 5 -> 5, of which waited for: 2 -> 2; matrix products, arithmetic and copies ran while one was open for 0% -> 0% of each run, Pallas kernels for 18% -> 17%
where the time goes in v6:
time: 34.8 us; the launch traced here: 34.5 us
  Pallas kernels  14.2 us (41%)
  blocking collectives  8.74 us (25%)
  waiting for transfers between devices  5.45 us (16%)
  starting transfers between devices  5.4 us (16%)
  between operations  0.72 us (2%)
    all_gather x1, blocking collectives, local(): all_sums = lax.all_gather(sums, ('seg', 'tile'), axis=0)  8.74 us
    pallas_call x1, Pallas kernels, all_totals(): pl.pallas_call(functools.partial(other_kernel, groups), out_shape=jax.Sha...  5.22 us
    ppermute x2, waiting for transfers between devices, trade(): return lax.ppermute(table, 'strip', pairs)  4.29 us
    pallas_call x2, Pallas kernels, own_totals(): pl.pallas_call(kernel, out_shape=(jax.ShapeDtypeStruct((slots, CHANNELS *...  3.51 us
    ppermute x1, starting transfers between devices, local(): arrived.append(lax.ppermute(points, 'tile', pairs))  2.56 us
    pallas_call x1, Pallas kernels, early_rows(): pl.pallas_call(functools.partial(early_kernel, groups), out_shape=(jax.Sh...  2.52 us
    ppermute x2, starting transfers between devices, trade(): return lax.ppermute(table, 'strip', pairs)  2.24 us
    pallas_call x1, Pallas kernels, local(): pl.pallas_call(functools.partial(step_kernel, segs, members), out_shape=(...  1.83 us
  transfers between devices with their start and end apart: 5, of which 2 were waited for; matrix products, arithmetic and copies ran while one was open for 0% of the time, Pallas kernels for 17%

profile of v6, /device:TPU:0, one launch (start us, length us, event | category | flops | bytes accessed | tf_op | source)
XLA Modules:
  0.0 34.5 jit_solution(15792841701051835523)
XLA Ops:
  0.6 1.1 %shard_map.86 = (f32[9,64,128]{2,1,0:T(8,128)S(1)}, f32[904,128]{1,0:T(8,128)S(1)}) custom-call(f32[3,64,128]{2,1,0:T(8,128)} %bitcast.10, f32[6,64,128]{2,1,0:T(8,128)} %bitcast.9, f32[3,64,128]{2,1,0:T(8,128)} %bitcast.11, f32[64,128]{1,0:T(8,128)} %bitcast.12, s32[64,128]{1,0:T(8,128)} %bitcast.13, s32[1,64]{1,0:T(1,128)} %sides.1, s32[1,64]{1,0:T(1,128)} %knot_ref.1), custom_call_target="tpu_custom_call" | custom-call | tf_op jit(solution)/shard_map/pallas_call | solution.py:559
  1.8 0.5 %collective-permute-start.1 = (f32[904,128]{1,0:T(8,128)S(1)}, f32[904,128]{1,0:T(8,128)S(1)}, u32[]{:S(2)}, u32[]{:S(2)}) collective-permute-start(f32[904,128]{1,0:T(8,128)S(1)} %get-tuple-element.13.refs_0_.points_ref), channel_id=1, source_target_pairs={{0,1},{1,0},{2,3},{3,2},{4,5},{5,4},{6,7},{7,6},{8,9},{9,8},{10,11... | collective-permute-start | bytes 1388552 | tf_op jit(solution)/shard_map/ppermute | solution.py:600
  2.3 2.6 %collective-permute-start = (f32[904,128]{1,0:T(8,128)S(1)}, f32[904,128]{1,0:T(8,128)S(1)}, u32[]{:S(2)}, u32[]{:S(2)}) collective-permute-start(f32[904,128]{1,0:T(8,128)S(1)} %get-tuple-element.13.refs_0_.points_ref), channel_id=1, source_target_pairs={{2,0},{3,1},{0,2},{1,3},{6,4},{7,5},{4,6},{5,7},{10,8},{11,9},{8,1... | collective-permute-start | bytes 1388552 | tf_op jit(solution)/shard_map/ppermute | solution.py:598
  4.9 1.6 %collective-permute-start.2 = (f32[9,64,128]{2,1,0:T(8,128)S(1)}, f32[9,64,128]{2,1,0:T(8,128)S(1)}, u32[]{:S(2)}, u32[]{:S(2)}) collective-permute-start(f32[9,64,128]{2,1,0:T(8,128)S(1)} %get-tuple-element.16), channel_id=1, source_target_pairs={{0,4},{4,0},{8,12},{12,8},{1,5},{5,1},{9,13},{13,9},{2,6},{6,2},{1... | collective-permute-start | bytes 884744 | tf_op jit(solution)/shard_map/ppermute | solution.py:592
  6.4 0.7 %collective-permute-start.3 = (f32[9,64,128]{2,1,0:T(8,128)S(1)}, f32[9,64,128]{2,1,0:T(8,128)S(1)}, u32[]{:S(2)}, u32[]{:S(2)}) collective-permute-start(f32[9,64,128]{2,1,0:T(8,128)S(1)} %get-tuple-element.16), channel_id=1, source_target_pairs={{4,8},{8,4},{5,9},{9,5},{6,10},{10,6},{7,11},{11,7},{20,24},{24,20... | collective-permute-start | bytes 884744 | tf_op jit(solution)/shard_map/ppermute | solution.py:592
  7.1 0.0 collective-permute-done.1.refs_1_
  7.1 2.5 %shard_map.87 = (f32[3072,128]{1,0:T(8,128)S(1)}, s32[8,128]{1,0:T(8,128)S(1)}) custom-call(f32[904,128]{1,0:T(8,128)S(1)} %get-tuple-element.13.refs_0_.points_ref, f32[904,128]{1,0:T(8,128)S(1)} %collective-permute-done.1.refs_1_), custom_call_target="tpu_custom_call" | custom-call | tf_op jit(solution)/shard_map/pallas_call | solution.py:395
  9.7 4.3 %collective-permute-done.2.near = f32[9,64,128]{2,1,0:T(8,128)S(1)} collective-permute-done((f32[9,64,128]{2,1,0:T(8,128)S(1)}, f32[9,64,128]{2,1,0:T(8,128)S(1)}, u32[]{:S(2)}, u32[]{:S(2)}) %collective-permute-start.2) | collective-permute-done | bytes 294944 | tf_op jit(solution)/shard_map/ppermute | solution.py:592
  13.9 2.9 %shard_map.88 = (bf16[1,576,256]{2,1,0:T(8,128)(2,1)S(1)}, f32[80,128]{1,0:T(8,128)S(1)}) custom-call(f32[3072,128]{1,0:T(8,128)S(1)} %get-tuple-element.14.packed, s32[8,128]{1,0:T(8,128)S(1)} %get-tuple-element.15.rows_ref, f32[9,64,128]{2,1,0:T(8,128)S(1)} %collective-permute-done.2.near), custom_call_target="tpu_custom_call" | custom-call | tf_op jit(solution)/shard_map/pallas_call | solution.py:410
  16.8 0.0 collective-permute-done.3.far
  16.8 0.0 collective-permute-done.refs_0_
  16.8 0.1 collective-permute-start.4
  16.9 0.0 copy-start
  16.9 0.6 %shard_map.89 = (bf16[2,576,256]{2,1,0:T(8,128)(2,1)S(1)}, f32[80,128]{1,0:T(8,128)S(1)}) custom-call(f32[3072,128]{1,0:T(8,128)S(1)} %get-tuple-element.14.packed, s32[8,128]{1,0:T(8,128)S(1)} %get-tuple-element.15.rows_ref, f32[9,64,128]{2,1,0:T(8,128)S(1)} %collective-permute-done.3.far, bf16[1,576,256]{2,1,0:T(8,128)(2,1)S(1)} %get-tuple-element.19.before, ...), custom_call_target="tpu_custom_call" | custom-call | tf_op jit(solution)/shard_map/pallas_call | solution.py:410
  17.6 1.2 %collective-permute-done.4.refs_1_ = f32[904,128]{1,0:T(8,128)S(1)} collective-permute-done((f32[904,128]{1,0:T(8,128)S(1)}, f32[904,128]{1,0:T(8,128)S(1)}, u32[]{:S(2)}, u32[]{:S(2)}) %collective-permute-start.4) | collective-permute-done | bytes 462880 | tf_op jit(solution)/shard_map/ppermute | solution.py:604
  18.7 5.2 %shard_map.90 = f32[80,128]{1,0:T(8,128)S(1)} custom-call(f32[904,128]{1,0:T(8,128)S(1)} %collective-permute-done.refs_0_, f32[904,128]{1,0:T(8,128)S(1)} %collective-permute-done.4.refs_1_, bf16[2,576,256]{2,1,0:T(8,128)(2,1)S(1)} %get-tuple-element.20.refs_2_, f32[80,128]{1,0:T(8,128)S(1)} %get-tuple-element.21.refs_3_), custom_call_target="tpu_custom_call" | custom-call | tf_op jit(solution)/shard_map/pallas_call | solution.py:426
  24.0 8.7 %all-gather = f32[640,128]{1,0:T(8,128)S(1)} all-gather(f32[80,128]{1,0:T(8,128)S(1)} %shard_map.90), channel_id=2, replica_groups=mesh['seg'=2,'strip'=4,'tile'=4] {'seg','tile'}, dimensions={0}, use_global_device_ids=true | all-gather | bytes 368640 | tf_op jit(solution)/shard_map/all_gather | solution.py:606
  32.7 0.0 copy-done
  32.7 1.8 %shard_map.91 = (f32[3,64,128]{2,1,0:T(8,128)}, f32[6,1,128]{2,1,0:T(1,128)}) custom-call(s32[1,64]{1,0:T(1,128)S(1)} %copy-done, f32[8,80,128]{2,1,0:T(8,128)S(1)} %bitcast.8, f32[904,128]{1,0:T(8,128)S(1)} %get-tuple-element.13.refs_0_.points_ref), custom_call_target="tpu_custom_call" | custom-call | tf_op jit(solution)/shard_map/pallas_call | solution.py:607
Async XLA Ops:
  1.8 5.3 %collective-permute-start.1 = (f32[904,128]{1,0:T(8,128)S(1)}, f32[904,128]{1,0:T(8,128)S(1)}, u32[]{:S(2)}, u32[]{:S(2)}) collective-permute-start(f32[904,128]{1,0:T(8,128)S(1)} %get-tuple-element.13.refs_0_.points_ref), channel_id=1, source_target_pairs={{0,1},{1,0},{2,3},{3,2},{4,5},{5,4},{6,7},{7,6},{8,9},{9,8},{10,11... | collective-permute-start | bytes 1388552 | tf_op jit(solution)/shard_map/ppermute | solution.py:600
  2.3 14.5 %collective-permute-start = (f32[904,128]{1,0:T(8,128)S(1)}, f32[904,128]{1,0:T(8,128)S(1)}, u32[]{:S(2)}, u32[]{:S(2)}) collective-permute-start(f32[904,128]{1,0:T(8,128)S(1)} %get-tuple-element.13.refs_0_.points_ref), channel_id=1, source_target_pairs={{2,0},{3,1},{0,2},{1,3},{6,4},{7,5},{4,6},{5,7},{10,8},{11,9},{8,1... | collective-permute-start | bytes 1388552 | tf_op jit(solution)/shard_map/ppermute | solution.py:598
  4.9 9.1 %collective-permute-start.2 = (f32[9,64,128]{2,1,0:T(8,128)S(1)}, f32[9,64,128]{2,1,0:T(8,128)S(1)}, u32[]{:S(2)}, u32[]{:S(2)}) collective-permute-start(f32[9,64,128]{2,1,0:T(8,128)S(1)} %get-tuple-element.16), channel_id=1, source_target_pairs={{0,4},{4,0},{8,12},{12,8},{1,5},{5,1},{9,13},{13,9},{2,6},{6,2},{1... | collective-permute-start | bytes 884744 | tf_op jit(solution)/shard_map/ppermute | solution.py:592
  6.4 10.4 %collective-permute-start.3 = (f32[9,64,128]{2,1,0:T(8,128)S(1)}, f32[9,64,128]{2,1,0:T(8,128)S(1)}, u32[]{:S(2)}, u32[]{:S(2)}) collective-permute-start(f32[9,64,128]{2,1,0:T(8,128)S(1)} %get-tuple-element.16), channel_id=1, source_target_pairs={{4,8},{8,4},{5,9},{9,5},{6,10},{10,6},{7,11},{11,7},{20,24},{24,20... | collective-permute-start | bytes 884744 | tf_op jit(solution)/shard_map/ppermute | solution.py:592
  16.8 1.9 %collective-permute-start.4 = (f32[904,128]{1,0:T(8,128)S(1)}, f32[904,128]{1,0:T(8,128)S(1)}, u32[]{:S(2)}, u32[]{:S(2)}) collective-permute-start(f32[904,128]{1,0:T(8,128)S(1)} %collective-permute-done.refs_0_), channel_id=1, source_target_pairs={{0,1},{1,0},{2,3},{3,2},{4,5},{5,4},{6,7},{7,6},{8,9},{9,8},{10,11... | collective-permute-start | bytes 1388552 | tf_op jit(solution)/shard_map/ppermute | solution.py:604
  16.9 15.8 %copy-start = (s32[1,64]{1,0:T(1,128)S(1)}, s32[1,64]{1,0:T(1,128)}, u32[]{:S(2)}) copy-start(s32[1,64]{1,0:T(1,128)} %knot_ref.1) | copy-start | bytes 772

commit v7 on v6

--- a/solution.py
+++ b/solution.py
@@ -31,10 +31,6 @@
 
 def vmem(count):
     return [pl.BlockSpec(memory_space=pltpu.VMEM)] * count
-
-
-def smem(count):
-    return [pl.BlockSpec(memory_space=pltpu.SMEM)] * count
 
 
 def pack_kernel(pos, cov, lever, time, partner, sides, knots, table_ref, points_ref, ints, small, sems):
@@ -338,25 +334,21 @@
     points = refs[:groups]
     packed, rows_ref = refs[groups : groups + 2]
     near_rows, far_rows = arrange(points, packed, refs[groups + 2 :])
-    rows_ref[0:4, :] = jnp.full((4, TILE_PTS), near_rows, jnp.int32)
-    rows_ref[4:8, :] = jnp.full((4, TILE_PTS), far_rows, jnp.int32)
-
-
-def near_kernel(packed, rows_ref, near, weights, totals_ref, rows_here, sem, *work):
-    copy = pltpu.make_async_copy(rows_ref, rows_here, sem.at[0])
-    copy.start()
+    rows_ref[0:8, :] = jnp.full((8, TILE_PTS), near_rows, jnp.int32)
+    rows_ref[8:16, :] = jnp.full((8, TILE_PTS), far_rows, jnp.int32)
+
+
+def near_kernel(packed, rows_ref, near, weights, totals_ref, *work):
+    near_rows = jnp.max(rows_ref[0:8, :])
     weigh_table(near, weights, 0)
-    copy.wait()
-    process(packed, rows_here[0, 0], jnp.int32(0), weights, totals_ref, work)
-
-
-def far_kernel(packed, rows_ref, far, before, before_ref, weights, totals_ref, rows_here, sem, *work):
-    copy = pltpu.make_async_copy(rows_ref, rows_here, sem.at[0])
-    copy.start()
+    process(packed, near_rows, jnp.int32(0), weights, totals_ref, work)
+
+
+def far_kernel(packed, rows_ref, far, before, before_ref, weights, totals_ref, *work):
+    far_rows = jnp.max(rows_ref[8:16, :])
     weights[0] = before[0]
     weigh_table(far, weights, 1)
-    copy.wait()
-    process(packed, jnp.int32(0), rows_here[4, 0], weights, totals_ref, work)
+    process(packed, jnp.int32(0), far_rows, weights, totals_ref, work)
     totals_ref[...] = totals_ref[...] + before_ref[...]
 
 
@@ -396,7 +388,7 @@
         functools.partial(early_kernel, groups),
         out_shape=(
             jax.ShapeDtypeStruct(packed_shape(groups, tiles), jnp.float32),
-            jax.ShapeDtypeStruct((8, TILE_PTS), jnp.int32),
+            jax.ShapeDtypeStruct((16, TILE_PTS), jnp.int32),
         ),
         in_specs=vmem(groups),
         out_specs=(pl.BlockSpec(memory_space=pltpu.VMEM),) * 2,
@@ -415,8 +407,7 @@
         ),
         in_specs=vmem(3 + len(before)),
         out_specs=(pl.BlockSpec(memory_space=pltpu.VMEM),) * 2,
-        scratch_shapes=[pltpu.SMEM((8, TILE_PTS), jnp.int32), pltpu.SemaphoreType.DMA((1,))]
-        + process_shapes(2, tiles),
+        scratch_shapes=process_shapes(2, tiles),
         compiler_params=params(14),
     )(packed, rows, table, *before)
 
@@ -468,23 +459,28 @@
     return answer
 
 
-def step_kernel(segs, members, knot_ref, sums_ref, points_ref, adjusted_ref, out_ref, held, index_ref):
-    tiles = knot_ref.shape[1]
-    for tile in range(tiles):
-        index_ref[tile : tile + 1, :] = jnp.full((1, KNOT_DEV), knot_ref[0, tile], jnp.int32)
+def step_kernel(segs, members, sums, points_ref, adjusted_ref, out_ref, held, index_ref):
+    tiles = index_ref.shape[0]
     seg = lax.axis_index("seg")
+    at = TILE_ROW * tiles + 1
+    index_ref[...] = jnp.take_along_axis(
+        jnp.broadcast_to(points_ref[at : at + 1, :], index_ref.shape),
+        lax.broadcasted_iota(jnp.int32, index_ref.shape, 0),
+        axis=1,
+        mode="promise_in_bounds",
+    ).astype(jnp.int32)
+    for place in range(3, 8):
+        held[place * SUM_ROWS : (place + 1) * SUM_ROWS, :] = jnp.zeros(
+            (SUM_ROWS, KNOT_DEV), jnp.float32
+        )
     for place in range(3):
         wanted = seg + place - 1
         there = (wanted >= 0) & (wanted < segs)
         first = jnp.minimum(jnp.maximum(wanted, 0), segs - 1) * members
-        total = sums_ref[first]
+        total = sums[first]
         for other in range(1, members):
-            total = total + sums_ref[first + other]
+            total = total + sums[first + other]
         held[place * SUM_ROWS : (place + 1) * SUM_ROWS, :] = jnp.where(there, total, 0.0)
-    for place in range(3, 8):
-        held[place * SUM_ROWS : (place + 1) * SUM_ROWS, :] = jnp.zeros(
-            (SUM_ROWS, KNOT_DEV), jnp.float32
-        )
     shape = (8, KNOT_DEV)
     lanes = lax.broadcasted_iota(jnp.int32, shape, 1)
     rows = lax.broadcasted_iota(jnp.int32, shape, 0)
@@ -610,14 +606,14 @@
             jax.ShapeDtypeStruct((3, tiles, TILE_PTS), jnp.float32),
             jax.ShapeDtypeStruct((6, 1, KNOT_DEV), jnp.float32),
         ),
-        in_specs=smem(1) + vmem(2),
+        in_specs=vmem(2),
         out_specs=(pl.BlockSpec(memory_space=pltpu.VMEM),) * 2,
         scratch_shapes=[
             pltpu.VMEM((8 * SUM_ROWS, KNOT_DEV), jnp.float32),
             pltpu.VMEM((tiles, KNOT_DEV), jnp.int32),
         ],
         compiler_params=params(6),
-    )(tile_knot, all_sums, points)
+    )(all_sums, points)
     return adjusted.reshape(positions.shape), corrections.reshape(1, 6, KNOT_DEV)
 
 

time: 34.8 us -> 34.1 us (0.980)
  Pallas kernels: 14.2 us -> 11.7 us
  blocking collectives: 8.74 us -> 9.89 us
  waiting for transfers between devices: 5.45 us -> 5.87 us
    all_gather x1, blocking collectives: 8.74 us -> 9.89 us  [local(): all_sums = lax.all_gather(sums, ('seg', 'tile'), axis=0)]
    pallas_call x1, Pallas kernels: 5.22 us -> 4.09 us  [all_totals(): pl.pallas_call(functools.partial(other_kernel, groups), out_shape=jax.Sha...]
    pallas_call x2, Pallas kernels: 3.51 us -> 2.68 us  [own_totals(): pl.pallas_call(kernel, out_shape=(jax.ShapeDtypeStruct((slots, CHANNELS *...]
    pallas_call x1, Pallas kernels: 1.83 us -> 1.29 us  [local(): pl.pallas_call(functools.partial(step_kernel, segs, members), out_shape=(...]
    ppermute x1, waiting for transfers between devices: 1.15 us -> 1.58 us  [local(): others = arrived + [lax.ppermute(group, 'tile', swap) for group in arrived]]
  transfers between devices with their start and end apart: 5 -> 5, of which waited for: 2 -> 2; matrix products, arithmetic and copies ran while one was open for 0% -> 0% of each run, Pallas kernels for 17% -> 16%
where the time goes in v7:
time: 34.1 us; the launch traced here: 33.6 us
  Pallas kernels  11.7 us (34%)
  blocking collectives  9.89 us (29%)
  waiting for transfers between devices  5.87 us (17%)
  starting transfers between devices  5.4 us (16%)
  between operations  0.71 us (2%)
    all_gather x1, blocking collectives, local(): all_sums = lax.all_gather(sums, ('seg', 'tile'), axis=0)  9.89 us
    ppermute x2, waiting for transfers between devices, trade(): return lax.ppermute(table, 'strip', pairs)  4.28 us
    pallas_call x1, Pallas kernels, all_totals(): pl.pallas_call(functools.partial(other_kernel, groups), out_shape=jax.Sha...  4.09 us
    pallas_call x2, Pallas kernels, own_totals(): pl.pallas_call(kernel, out_shape=(jax.ShapeDtypeStruct((slots, CHANNELS *...  2.68 us
    ppermute x1, starting transfers between devices, local(): arrived.append(lax.ppermute(points, 'tile', pairs))  2.56 us
    pallas_call x1, Pallas kernels, early_rows(): pl.pallas_call(functools.partial(early_kernel, groups), out_shape=(jax.Sh...  2.53 us
    ppermute x2, starting transfers between devices, trade(): return lax.ppermute(table, 'strip', pairs)  2.24 us
    ppermute x1, waiting for transfers between devices, local(): others = arrived + [lax.ppermute(group, 'tile', swap) for group in arrived]  1.58 us
  transfers between devices with their start and end apart: 5, of which 2 were waited for; matrix products, arithmetic and copies ran while one was open for 0% of the time, Pallas kernels for 16%

profile of v7, /device:TPU:0, one launch (start us, length us, event | category | flops | bytes accessed | tf_op | source)
XLA Modules:
  0.0 33.6 jit_solution(7027379187286305271)
XLA Ops:
  0.6 1.1 %shard_map.86 = (f32[9,64,128]{2,1,0:T(8,128)S(1)}, f32[904,128]{1,0:T(8,128)S(1)}) custom-call(f32[3,64,128]{2,1,0:T(8,128)} %bitcast.10, f32[6,64,128]{2,1,0:T(8,128)} %bitcast.9, f32[3,64,128]{2,1,0:T(8,128)} %bitcast.11, f32[64,128]{1,0:T(8,128)} %bitcast.12, s32[64,128]{1,0:T(8,128)} %bitcast.13, s32[1,64]{1,0:T(1,128)} %sides.1, s32[1,64]{1,0:T(1,128)} %knots.1), custom_call_target="tpu_custom_call" | custom-call | tf_op jit(solution)/shard_map/pallas_call | solution.py:555
  1.8 0.5 %collective-permute-start.1 = (f32[904,128]{1,0:T(8,128)S(1)}, f32[904,128]{1,0:T(8,128)S(1)}, u32[]{:S(2)}, u32[]{:S(2)}) collective-permute-start(f32[904,128]{1,0:T(8,128)S(1)} %get-tuple-element.13.refs_0_.points_ref), channel_id=1, source_target_pairs={{0,1},{1,0},{2,3},{3,2},{4,5},{5,4},{6,7},{7,6},{8,9},{9,8},{10,11... | collective-permute-start | bytes 1388552 | tf_op jit(solution)/shard_map/ppermute | solution.py:596
  2.3 2.6 %collective-permute-start = (f32[904,128]{1,0:T(8,128)S(1)}, f32[904,128]{1,0:T(8,128)S(1)}, u32[]{:S(2)}, u32[]{:S(2)}) collective-permute-start(f32[904,128]{1,0:T(8,128)S(1)} %get-tuple-element.13.refs_0_.points_ref), channel_id=1, source_target_pairs={{2,0},{3,1},{0,2},{1,3},{6,4},{7,5},{4,6},{5,7},{10,8},{11,9},{8,1... | collective-permute-start | bytes 1388552 | tf_op jit(solution)/shard_map/ppermute | solution.py:594
  4.9 1.6 %collective-permute-start.2 = (f32[9,64,128]{2,1,0:T(8,128)S(1)}, f32[9,64,128]{2,1,0:T(8,128)S(1)}, u32[]{:S(2)}, u32[]{:S(2)}) collective-permute-start(f32[9,64,128]{2,1,0:T(8,128)S(1)} %get-tuple-element.16), channel_id=1, source_target_pairs={{0,4},{4,0},{8,12},{12,8},{1,5},{5,1},{9,13},{13,9},{2,6},{6,2},{1... | collective-permute-start | bytes 884744 | tf_op jit(solution)/shard_map/ppermute | solution.py:588
  6.4 0.7 %collective-permute-start.3 = (f32[9,64,128]{2,1,0:T(8,128)S(1)}, f32[9,64,128]{2,1,0:T(8,128)S(1)}, u32[]{:S(2)}, u32[]{:S(2)}) collective-permute-start(f32[9,64,128]{2,1,0:T(8,128)S(1)} %get-tuple-element.16), channel_id=1, source_target_pairs={{4,8},{8,4},{5,9},{9,5},{6,10},{10,6},{7,11},{11,7},{20,24},{24,20... | collective-permute-start | bytes 884744 | tf_op jit(solution)/shard_map/ppermute | solution.py:588
  7.1 0.0 collective-permute-done.1.refs_1_
  7.1 2.5 %shard_map.87 = (f32[3072,128]{1,0:T(8,128)S(1)}, s32[16,128]{1,0:T(8,128)S(1)}) custom-call(f32[904,128]{1,0:T(8,128)S(1)} %get-tuple-element.13.refs_0_.points_ref, f32[904,128]{1,0:T(8,128)S(1)} %collective-permute-done.1.refs_1_), custom_call_target="tpu_custom_call" | custom-call | tf_op jit(solution)/shard_map/pallas_call | solution.py:387
  9.7 4.3 %collective-permute-done.2.near = f32[9,64,128]{2,1,0:T(8,128)S(1)} collective-permute-done((f32[9,64,128]{2,1,0:T(8,128)S(1)}, f32[9,64,128]{2,1,0:T(8,128)S(1)}, u32[]{:S(2)}, u32[]{:S(2)}) %collective-permute-start.2) | collective-permute-done | bytes 294944 | tf_op jit(solution)/shard_map/ppermute | solution.py:588
  13.9 2.5 %shard_map.88 = (bf16[1,576,256]{2,1,0:T(8,128)(2,1)S(1)}, f32[80,128]{1,0:T(8,128)S(1)}) custom-call(f32[3072,128]{1,0:T(8,128)S(1)} %get-tuple-element.14.packed, s32[16,128]{1,0:T(8,128)S(1)} %get-tuple-element.15.rows_ref, f32[9,64,128]{2,1,0:T(8,128)S(1)} %collective-permute-done.2.near), custom_call_target="tpu_custom_call" | custom-call | tf_op jit(solution)/shard_map/pallas_call | solution.py:402
  16.4 0.0 collective-permute-done.3.far
  16.4 0.0 collective-permute-done.refs_0_
  16.4 0.1 collective-permute-start.4
  16.5 0.2 shard_map.89
  16.7 1.6 %collective-permute-done.4.refs_1_ = f32[904,128]{1,0:T(8,128)S(1)} collective-permute-done((f32[904,128]{1,0:T(8,128)S(1)}, f32[904,128]{1,0:T(8,128)S(1)}, u32[]{:S(2)}, u32[]{:S(2)}) %collective-permute-start.4) | collective-permute-done | bytes 462880 | tf_op jit(solution)/shard_map/ppermute | solution.py:600
  18.3 4.1 %shard_map.90 = f32[80,128]{1,0:T(8,128)S(1)} custom-call(f32[904,128]{1,0:T(8,128)S(1)} %collective-permute-done.refs_0_, f32[904,128]{1,0:T(8,128)S(1)} %collective-permute-done.4.refs_1_, bf16[2,576,256]{2,1,0:T(8,128)(2,1)S(1)} %get-tuple-element.20.refs_2_, f32[80,128]{1,0:T(8,128)S(1)} %get-tuple-element.21.refs_3_), custom_call_target="tpu_custom_call" | custom-call | tf_op jit(solution)/shard_map/pallas_call | solution.py:417
  22.4 9.9 %all-gather = f32[640,128]{1,0:T(8,128)S(1)} all-gather(f32[80,128]{1,0:T(8,128)S(1)} %shard_map.90), channel_id=2, replica_groups=mesh['seg'=2,'strip'=4,'tile'=4] {'seg','tile'}, dimensions={0}, use_global_device_ids=true | all-gather | bytes 368640 | tf_op jit(solution)/shard_map/all_gather | solution.py:602
  32.3 1.3 %shard_map.91 = (f32[3,64,128]{2,1,0:T(8,128)}, f32[6,1,128]{2,1,0:T(1,128)}) custom-call(f32[8,80,128]{2,1,0:T(8,128)S(1)} %bitcast.8, f32[904,128]{1,0:T(8,128)S(1)} %get-tuple-element.13.refs_0_.points_ref), custom_call_target="tpu_custom_call" | custom-call | tf_op jit(solution)/shard_map/pallas_call | solution.py:603
Async XLA Ops:
  1.8 5.3 %collective-permute-start.1 = (f32[904,128]{1,0:T(8,128)S(1)}, f32[904,128]{1,0:T(8,128)S(1)}, u32[]{:S(2)}, u32[]{:S(2)}) collective-permute-start(f32[904,128]{1,0:T(8,128)S(1)} %get-tuple-element.13.refs_0_.points_ref), channel_id=1, source_target_pairs={{0,1},{1,0},{2,3},{3,2},{4,5},{5,4},{6,7},{7,6},{8,9},{9,8},{10,11... | collective-permute-start | bytes 1388552 | tf_op jit(solution)/shard_map/ppermute | solution.py:596
  2.3 14.1 %collective-permute-start = (f32[904,128]{1,0:T(8,128)S(1)}, f32[904,128]{1,0:T(8,128)S(1)}, u32[]{:S(2)}, u32[]{:S(2)}) collective-permute-start(f32[904,128]{1,0:T(8,128)S(1)} %get-tuple-element.13.refs_0_.points_ref), channel_id=1, source_target_pairs={{2,0},{3,1},{0,2},{1,3},{6,4},{7,5},{4,6},{5,7},{10,8},{11,9},{8,1... | collective-permute-start | bytes 1388552 | tf_op jit(solution)/shard_map/ppermute | solution.py:594
  4.9 9.1 %collective-permute-start.2 = (f32[9,64,128]{2,1,0:T(8,128)S(1)}, f32[9,64,128]{2,1,0:T(8,128)S(1)}, u32[]{:S(2)}, u32[]{:S(2)}) collective-permute-start(f32[9,64,128]{2,1,0:T(8,128)S(1)} %get-tuple-element.16), channel_id=1, source_target_pairs={{0,4},{4,0},{8,12},{12,8},{1,5},{5,1},{9,13},{13,9},{2,6},{6,2},{1... | collective-permute-start | bytes 884744 | tf_op jit(solution)/shard_map/ppermute | solution.py:588
  6.4 10.0 %collective-permute-start.3 = (f32[9,64,128]{2,1,0:T(8,128)S(1)}, f32[9,64,128]{2,1,0:T(8,128)S(1)}, u32[]{:S(2)}, u32[]{:S(2)}) collective-permute-start(f32[9,64,128]{2,1,0:T(8,128)S(1)} %get-tuple-element.16), channel_id=1, source_target_pairs={{4,8},{8,4},{5,9},{9,5},{6,10},{10,6},{7,11},{11,7},{20,24},{24,20... | collective-permute-start | bytes 884744 | tf_op jit(solution)/shard_map/ppermute | solution.py:588
  16.4 1.9 %collective-permute-start.4 = (f32[904,128]{1,0:T(8,128)S(1)}, f32[904,128]{1,0:T(8,128)S(1)}, u32[]{:S(2)}, u32[]{:S(2)}) collective-permute-start(f32[904,128]{1,0:T(8,128)S(1)} %collective-permute-done.refs_0_), channel_id=1, source_target_pairs={{0,1},{1,0},{2,3},{3,2},{4,5},{5,4},{6,7},{7,6},{8,9},{9,8},{10,11... | collective-permute-start | bytes 1388552 | tf_op jit(solution)/shard_map/ppermute | solution.py:600

commit v8 on v7

--- a/solution.py
+++ b/solution.py
@@ -165,14 +165,17 @@
         packed[at, :] = jnp.where(wide >= shift, value, packed[at, :])
         packed[span(places[1, tile]), :] = jnp.where(wide < shift, value, 0.0)
 
-    unroll = tiles
+    unroll = total if total <= 2 * TILE_PTS else tiles
 
     def several(step, carry):
         for tile in range(unroll):
             place(step * unroll + tile)
         return carry
 
-    lax.fori_loop(0, total // unroll, several, 0)
+    if unroll == total:
+        several(0, 0)
+    else:
+        lax.fori_loop(0, total // unroll, several, 0)
     near_rows = lax.shift_right_logical(places[3, total - 1] + TILE_PTS - 1, 7)
     far_rows = lax.shift_right_logical(places[4, total - 1] + TILE_PTS - 1, 7)
     blank = jnp.zeros((POINT_ROWS, TILE_PTS), jnp.float32)
@@ -202,7 +205,6 @@
     queries = BLOCK_TILES * TILE_PTS
 
     def one_block(block):
-        block = jnp.minimum(block, blocks - 1)
         far = block >= near_blocks
         slot = far.astype(jnp.int32)
         base = jnp.where(far, room - BLOCK_TILES * (block - near_blocks + 1), block * BLOCK_TILES)
@@ -235,16 +237,33 @@
                 found[channel] = jnp.where(here, picked[begin : begin + 8], found[channel])
         return ids, [jnp.sum(entry, axis=0, keepdims=True) for entry in found]
 
-    def body(step, carry):
-        results = [one_block(3 * step + i) for i in range(3)]
+    def pick(first, count):
+        results = [one_block(first + i) for i in range(count)]
         for ids, flat in results:
             for channel in range(CHANNELS):
                 for j in range(BLOCK_TILES):
                     piece = flat[channel][:, j * TILE_PTS : (j + 1) * TILE_PTS]
                     target[channel, pl.ds(ids[j], 1), :] = piece
+
+    def three(step, carry):
+        pick(3 * step, 3)
         return carry
 
-    lax.fori_loop(0, lax.div(blocks + 2, jnp.int32(3)), body, 0)
+    def one(block, carry):
+        pick(block, 1)
+        return carry
+
+    threes = lax.div(blocks, jnp.int32(3))
+    lax.fori_loop(0, threes, three, 0)
+    rest = blocks - 3 * threes
+
+    @pl.when(rest == 1)
+    def _():
+        pick(3 * threes, 1)
+
+    @pl.when(rest == 2)
+    def _():
+        pick(3 * threes, 2)
 
     totals_ref[...] = jnp.zeros_like(totals_ref)
     terms_ref[75 * SPREAD :, :] = jnp.zeros((5 * SPREAD, TILE_PTS), jnp.float32)

time: 34.1 us -> 33.6 us (0.985)
  blocking collectives: 9.89 us -> 9.53 us
    all_gather x1, blocking collectives: 9.89 us -> 9.53 us  [local(): all_sums = lax.all_gather(sums, ('seg', 'tile'), axis=0)]
  transfers between devices with their start and end apart: 5 -> 5, of which waited for: 2 -> 2; matrix products, arithmetic and copies ran while one was open for 0% -> 0% of each run, Pallas kernels for 16% -> 15%
where the time goes in v8:
time: 33.6 us; the launch traced here: 33.3 us
  Pallas kernels  11.7 us (35%)
  blocking collectives  9.53 us (28%)
  waiting for transfers between devices  5.92 us (18%)
  starting transfers between devices  5.4 us (16%)
  between operations  0.71 us (2%)
    all_gather x1, blocking collectives, local(): all_sums = lax.all_gather(sums, ('seg', 'tile'), axis=0)  9.53 us
    ppermute x2, waiting for transfers between devices, trade(): return lax.ppermute(table, 'strip', pairs)  4.34 us
    pallas_call x1, Pallas kernels, all_totals(): pl.pallas_call(functools.partial(other_kernel, groups), out_shape=jax.Sha...  4.15 us
    pallas_call x2, Pallas kernels, own_totals(): pl.pallas_call(kernel, out_shape=(jax.ShapeDtypeStruct((slots, CHANNELS *...  2.67 us
    ppermute x1, starting transfers between devices, local(): arrived.append(lax.ppermute(points, 'tile', pairs))  2.56 us
    pallas_call x1, Pallas kernels, early_rows(): pl.pallas_call(functools.partial(early_kernel, groups), out_shape=(jax.Sh...  2.47 us
    ppermute x2, starting transfers between devices, trade(): return lax.ppermute(table, 'strip', pairs)  2.24 us
    ppermute x1, waiting for transfers between devices, local(): others = arrived + [lax.ppermute(group, 'tile', swap) for group in arrived]  1.57 us
  transfers between devices with their start and end apart: 5, of which 2 were waited for; matrix products, arithmetic and copies ran while one was open for 0% of the time, Pallas kernels for 15%

profile of v8, /device:TPU:0, one launch (start us, length us, event | category | flops | bytes accessed | tf_op | source)
XLA Modules:
  0.0 33.3 jit_solution(10872766809118965330)
XLA Ops:
  0.6 1.1 %shard_map.86 = (f32[9,64,128]{2,1,0:T(8,128)S(1)}, f32[904,128]{1,0:T(8,128)S(1)}) custom-call(f32[3,64,128]{2,1,0:T(8,128)} %bitcast.10, f32[6,64,128]{2,1,0:T(8,128)} %bitcast.9, f32[3,64,128]{2,1,0:T(8,128)} %bitcast.11, f32[64,128]{1,0:T(8,128)} %bitcast.12, s32[64,128]{1,0:T(8,128)} %bitcast.13, s32[1,64]{1,0:T(1,128)} %sides.1, s32[1,64]{1,0:T(1,128)} %knots.1), custom_call_target="tpu_custom_call" | custom-call | tf_op jit(solution)/shard_map/pallas_call | solution.py:574
  1.8 0.5 %collective-permute-start.1 = (f32[904,128]{1,0:T(8,128)S(1)}, f32[904,128]{1,0:T(8,128)S(1)}, u32[]{:S(2)}, u32[]{:S(2)}) collective-permute-start(f32[904,128]{1,0:T(8,128)S(1)} %get-tuple-element.13.refs_0_.points_ref), channel_id=1, source_target_pairs={{0,1},{1,0},{2,3},{3,2},{4,5},{5,4},{6,7},{7,6},{8,9},{9,8},{10,11... | collective-permute-start | bytes 1388552 | tf_op jit(solution)/shard_map/ppermute | solution.py:615
  2.3 2.6 %collective-permute-start = (f32[904,128]{1,0:T(8,128)S(1)}, f32[904,128]{1,0:T(8,128)S(1)}, u32[]{:S(2)}, u32[]{:S(2)}) collective-permute-start(f32[904,128]{1,0:T(8,128)S(1)} %get-tuple-element.13.refs_0_.points_ref), channel_id=1, source_target_pairs={{2,0},{3,1},{0,2},{1,3},{6,4},{7,5},{4,6},{5,7},{10,8},{11,9},{8,1... | collective-permute-start | bytes 1388552 | tf_op jit(solution)/shard_map/ppermute | solution.py:613
  4.9 1.6 %collective-permute-start.2 = (f32[9,64,128]{2,1,0:T(8,128)S(1)}, f32[9,64,128]{2,1,0:T(8,128)S(1)}, u32[]{:S(2)}, u32[]{:S(2)}) collective-permute-start(f32[9,64,128]{2,1,0:T(8,128)S(1)} %get-tuple-element.16), channel_id=1, source_target_pairs={{0,4},{4,0},{8,12},{12,8},{1,5},{5,1},{9,13},{13,9},{2,6},{6,2},{1... | collective-permute-start | bytes 884744 | tf_op jit(solution)/shard_map/ppermute | solution.py:607
  6.4 0.7 %collective-permute-start.3 = (f32[9,64,128]{2,1,0:T(8,128)S(1)}, f32[9,64,128]{2,1,0:T(8,128)S(1)}, u32[]{:S(2)}, u32[]{:S(2)}) collective-permute-start(f32[9,64,128]{2,1,0:T(8,128)S(1)} %get-tuple-element.16), channel_id=1, source_target_pairs={{4,8},{8,4},{5,9},{9,5},{6,10},{10,6},{7,11},{11,7},{20,24},{24,20... | collective-permute-start | bytes 884744 | tf_op jit(solution)/shard_map/ppermute | solution.py:607
  7.1 0.0 collective-permute-done.1.refs_1_
  7.1 2.5 %shard_map.87 = (f32[3072,128]{1,0:T(8,128)S(1)}, s32[16,128]{1,0:T(8,128)S(1)}) custom-call(f32[904,128]{1,0:T(8,128)S(1)} %get-tuple-element.13.refs_0_.points_ref, f32[904,128]{1,0:T(8,128)S(1)} %collective-permute-done.1.refs_1_), custom_call_target="tpu_custom_call" | custom-call | tf_op jit(solution)/shard_map/pallas_call | solution.py:406
  9.6 4.3 %collective-permute-done.2.near = f32[9,64,128]{2,1,0:T(8,128)S(1)} collective-permute-done((f32[9,64,128]{2,1,0:T(8,128)S(1)}, f32[9,64,128]{2,1,0:T(8,128)S(1)}, u32[]{:S(2)}, u32[]{:S(2)}) %collective-permute-start.2) | collective-permute-done | bytes 294944 | tf_op jit(solution)/shard_map/ppermute | solution.py:607
  13.9 2.4 %shard_map.88 = (bf16[1,576,256]{2,1,0:T(8,128)(2,1)S(1)}, f32[80,128]{1,0:T(8,128)S(1)}) custom-call(f32[3072,128]{1,0:T(8,128)S(1)} %get-tuple-element.14.packed, s32[16,128]{1,0:T(8,128)S(1)} %get-tuple-element.15.rows_ref, f32[9,64,128]{2,1,0:T(8,128)S(1)} %collective-permute-done.2.near), custom_call_target="tpu_custom_call" | custom-call | tf_op jit(solution)/shard_map/pallas_call | solution.py:421
  16.4 0.0 collective-permute-done.3.far
  16.4 0.0 collective-permute-done.refs_0_
  16.4 0.1 collective-permute-start.4
  16.5 0.2 shard_map.89
  16.7 1.6 %collective-permute-done.4.refs_1_ = f32[904,128]{1,0:T(8,128)S(1)} collective-permute-done((f32[904,128]{1,0:T(8,128)S(1)}, f32[904,128]{1,0:T(8,128)S(1)}, u32[]{:S(2)}, u32[]{:S(2)}) %collective-permute-start.4) | collective-permute-done | bytes 462880 | tf_op jit(solution)/shard_map/ppermute | solution.py:619
  18.3 4.2 %shard_map.90 = f32[80,128]{1,0:T(8,128)S(1)} custom-call(f32[904,128]{1,0:T(8,128)S(1)} %collective-permute-done.refs_0_, f32[904,128]{1,0:T(8,128)S(1)} %collective-permute-done.4.refs_1_, bf16[2,576,256]{2,1,0:T(8,128)(2,1)S(1)} %get-tuple-element.20.refs_2_, f32[80,128]{1,0:T(8,128)S(1)} %get-tuple-element.21.refs_3_), custom_call_target="tpu_custom_call" | custom-call | tf_op jit(solution)/shard_map/pallas_call | solution.py:436
  22.5 9.5 %all-gather = f32[640,128]{1,0:T(8,128)S(1)} all-gather(f32[80,128]{1,0:T(8,128)S(1)} %shard_map.90), channel_id=2, replica_groups=mesh['seg'=2,'strip'=4,'tile'=4] {'seg','tile'}, dimensions={0}, use_global_device_ids=true | all-gather | bytes 368640 | tf_op jit(solution)/shard_map/all_gather | solution.py:621
  32.0 1.3 %shard_map.91 = (f32[3,64,128]{2,1,0:T(8,128)}, f32[6,1,128]{2,1,0:T(1,128)}) custom-call(f32[8,80,128]{2,1,0:T(8,128)S(1)} %bitcast.8, f32[904,128]{1,0:T(8,128)S(1)} %get-tuple-element.13.refs_0_.points_ref), custom_call_target="tpu_custom_call" | custom-call | tf_op jit(solution)/shard_map/pallas_call | solution.py:622
Async XLA Ops:
  1.8 5.3 %collective-permute-start.1 = (f32[904,128]{1,0:T(8,128)S(1)}, f32[904,128]{1,0:T(8,128)S(1)}, u32[]{:S(2)}, u32[]{:S(2)}) collective-permute-start(f32[904,128]{1,0:T(8,128)S(1)} %get-tuple-element.13.refs_0_.points_ref), channel_id=1, source_target_pairs={{0,1},{1,0},{2,3},{3,2},{4,5},{5,4},{6,7},{7,6},{8,9},{9,8},{10,11... | collective-permute-start | bytes 1388552 | tf_op jit(solution)/shard_map/ppermute | solution.py:615
  2.3 14.1 %collective-permute-start = (f32[904,128]{1,0:T(8,128)S(1)}, f32[904,128]{1,0:T(8,128)S(1)}, u32[]{:S(2)}, u32[]{:S(2)}) collective-permute-start(f32[904,128]{1,0:T(8,128)S(1)} %get-tuple-element.13.refs_0_.points_ref), channel_id=1, source_target_pairs={{2,0},{3,1},{0,2},{1,3},{6,4},{7,5},{4,6},{5,7},{10,8},{11,9},{8,1... | collective-permute-start | bytes 1388552 | tf_op jit(solution)/shard_map/ppermute | solution.py:613
  4.9 9.1 %collective-permute-start.2 = (f32[9,64,128]{2,1,0:T(8,128)S(1)}, f32[9,64,128]{2,1,0:T(8,128)S(1)}, u32[]{:S(2)}, u32[]{:S(2)}) collective-permute-start(f32[9,64,128]{2,1,0:T(8,128)S(1)} %get-tuple-element.16), channel_id=1, source_target_pairs={{0,4},{4,0},{8,12},{12,8},{1,5},{5,1},{9,13},{13,9},{2,6},{6,2},{1... | collective-permute-start | bytes 884744 | tf_op jit(solution)/shard_map/ppermute | solution.py:607
  6.4 10.0 %collective-permute-start.3 = (f32[9,64,128]{2,1,0:T(8,128)S(1)}, f32[9,64,128]{2,1,0:T(8,128)S(1)}, u32[]{:S(2)}, u32[]{:S(2)}) collective-permute-start(f32[9,64,128]{2,1,0:T(8,128)S(1)} %get-tuple-element.16), channel_id=1, source_target_pairs={{4,8},{8,4},{5,9},{9,5},{6,10},{10,6},{7,11},{11,7},{20,24},{24,20... | collective-permute-start | bytes 884744 | tf_op jit(solution)/shard_map/ppermute | solution.py:607
  16.4 1.9 %collective-permute-start.4 = (f32[904,128]{1,0:T(8,128)S(1)}, f32[904,128]{1,0:T(8,128)S(1)}, u32[]{:S(2)}, u32[]{:S(2)}) collective-permute-start(f32[904,128]{1,0:T(8,128)S(1)} %collective-permute-done.refs_0_), channel_id=1, source_target_pairs={{0,1},{1,0},{2,3},{3,2},{4,5},{5,4},{6,7},{7,6},{8,9},{9,8},{10,11... | collective-permute-start | bytes 1388552 | tf_op jit(solution)/shard_map/ppermute | solution.py:619

commit v9 on v8

--- a/solution.py
+++ b/solution.py
@@ -101,6 +101,19 @@
         wanted = (offset >= 0) & (offset < tiles) & (tile_value(group, 0) != 2.0)
         marks.append(jnp.where(wanted, 1.0, 0.0).astype(jnp.bfloat16))
     marks = jnp.concatenate(marks, axis=0)
+    ranks = jnp.dot(
+        marks, ordered(TILE_PTS, lambda row, lane: row <= lane), preferred_element_type=jnp.float32
+    ).astype(jnp.int32)
+    sources = []
+    for p in range(len(points)):
+        rank = ranks[p * tiles : (p + 1) * tiles]
+        source = jnp.zeros_like(lanes)
+        for jump in (64, 32, 16, 8, 4, 2, 1):
+            there = jnp.take_along_axis(
+                rank, source + (jump - 1), axis=1, mode="promise_in_bounds"
+            )
+            source = jnp.where(there <= lanes, source + jump, source)
+        sources.append(source)
     number = lax.dot_general(
         jnp.ones((16, TILE_PTS), jnp.bfloat16),
         marks,
@@ -130,17 +143,8 @@
     codes[...] = code
     copy = pltpu.make_async_copy(codes, places, sem.at[0])
     copy.start()
-    ranks = jnp.dot(
-        marks, ordered(TILE_PTS, lambda row, lane: row <= lane), preferred_element_type=jnp.float32
-    ).astype(jnp.int32)
     for p, group in enumerate(points):
-        rank = ranks[p * tiles : (p + 1) * tiles]
-        source = jnp.zeros_like(lanes)
-        for jump in (64, 32, 16, 8, 4, 2, 1):
-            there = jnp.take_along_axis(
-                rank, source + (jump - 1), axis=1, mode="promise_in_bounds"
-            )
-            source = jnp.where(there <= lanes, source + jump, source)
+        rank, source = ranks[p * tiles : (p + 1) * tiles], sources[p]
         for channel in range(POINT_ROWS):
             if channel == VALID:
                 value = jnp.where(lanes < jnp.broadcast_to(rank[:, TILE_PTS - 1 :], shape), 1.0, 0.0)

time: 33.6 us -> 33.4 us (level)
  Pallas kernels: 11.7 us -> 11 us
  waiting for transfers between devices: 5.92 us -> 6.45 us
    ppermute x2, waiting for transfers between devices: 4.34 us -> 4.88 us  [trade(): return lax.ppermute(table, 'strip', pairs)]
    pallas_call x1, Pallas kernels: 2.47 us -> 1.94 us  [early_rows(): pl.pallas_call(functools.partial(early_kernel, groups), out_shape=(jax.Sh...]
  transfers between devices with their start and end apart: 5 -> 5, of which waited for: 2 -> 2; matrix products, arithmetic and copies ran while one was open for 0% -> 0% of each run, Pallas kernels for 15% -> 14%
where the time goes in v9:
time: 33.4 us; the launch traced here: 33.3 us
  Pallas kernels  11 us (33%)
  blocking collectives  9.69 us (29%)
  waiting for transfers between devices  6.45 us (19%)
  starting transfers between devices  5.4 us (16%)
  between operations  0.71 us (2%)
    all_gather x1, blocking collectives, local(): all_sums = lax.all_gather(sums, ('seg', 'tile'), axis=0)  9.69 us
    ppermute x2, waiting for transfers between devices, trade(): return lax.ppermute(table, 'strip', pairs)  4.88 us
    pallas_call x1, Pallas kernels, all_totals(): pl.pallas_call(functools.partial(other_kernel, groups), out_shape=jax.Sha...  4.01 us
    pallas_call x2, Pallas kernels, own_totals(): pl.pallas_call(kernel, out_shape=(jax.ShapeDtypeStruct((slots, CHANNELS *...  2.67 us
    ppermute x1, starting transfers between devices, local(): arrived.append(lax.ppermute(points, 'tile', pairs))  2.56 us
    ppermute x2, starting transfers between devices, trade(): return lax.ppermute(table, 'strip', pairs)  2.24 us
    pallas_call x1, Pallas kernels, early_rows(): pl.pallas_call(functools.partial(early_kernel, groups), out_shape=(jax.Sh...  1.94 us
    ppermute x1, waiting for transfers between devices, local(): others = arrived + [lax.ppermute(group, 'tile', swap) for group in arrived]  1.57 us
  transfers between devices with their start and end apart: 5, of which 2 were waited for; matrix products, arithmetic and copies ran while one was open for 0% of the time, Pallas kernels for 14%

profile of v9, /device:TPU:0, one launch (start us, length us, event | category | flops | bytes accessed | tf_op | source)
XLA Modules:
  0.0 33.3 jit_solution(12758911780455351412)
XLA Ops:
  0.6 1.1 %shard_map.86 = (f32[9,64,128]{2,1,0:T(8,128)S(1)}, f32[904,128]{1,0:T(8,128)S(1)}) custom-call(f32[3,64,128]{2,1,0:T(8,128)} %bitcast.10, f32[6,64,128]{2,1,0:T(8,128)} %bitcast.9, f32[3,64,128]{2,1,0:T(8,128)} %bitcast.11, f32[64,128]{1,0:T(8,128)} %bitcast.12, s32[64,128]{1,0:T(8,128)} %bitcast.13, s32[1,64]{1,0:T(1,128)} %sides.1, s32[1,64]{1,0:T(1,128)} %knots.1), custom_call_target="tpu_custom_call" | custom-call | tf_op jit(solution)/shard_map/pallas_call | solution.py:578
  1.8 0.5 %collective-permute-start.1 = (f32[904,128]{1,0:T(8,128)S(1)}, f32[904,128]{1,0:T(8,128)S(1)}, u32[]{:S(2)}, u32[]{:S(2)}) collective-permute-start(f32[904,128]{1,0:T(8,128)S(1)} %get-tuple-element.13.refs_0_.points_ref), channel_id=1, source_target_pairs={{0,1},{1,0},{2,3},{3,2},{4,5},{5,4},{6,7},{7,6},{8,9},{9,8},{10,11... | collective-permute-start | bytes 1388552 | tf_op jit(solution)/shard_map/ppermute | solution.py:619
  2.3 2.6 %collective-permute-start = (f32[904,128]{1,0:T(8,128)S(1)}, f32[904,128]{1,0:T(8,128)S(1)}, u32[]{:S(2)}, u32[]{:S(2)}) collective-permute-start(f32[904,128]{1,0:T(8,128)S(1)} %get-tuple-element.13.refs_0_.points_ref), channel_id=1, source_target_pairs={{2,0},{3,1},{0,2},{1,3},{6,4},{7,5},{4,6},{5,7},{10,8},{11,9},{8,1... | collective-permute-start | bytes 1388552 | tf_op jit(solution)/shard_map/ppermute | solution.py:617
  4.9 1.6 %collective-permute-start.2 = (f32[9,64,128]{2,1,0:T(8,128)S(1)}, f32[9,64,128]{2,1,0:T(8,128)S(1)}, u32[]{:S(2)}, u32[]{:S(2)}) collective-permute-start(f32[9,64,128]{2,1,0:T(8,128)S(1)} %get-tuple-element.16), channel_id=1, source_target_pairs={{0,4},{4,0},{8,12},{12,8},{1,5},{5,1},{9,13},{13,9},{2,6},{6,2},{1... | collective-permute-start | bytes 884744 | tf_op jit(solution)/shard_map/ppermute | solution.py:611
  6.4 0.7 %collective-permute-start.3 = (f32[9,64,128]{2,1,0:T(8,128)S(1)}, f32[9,64,128]{2,1,0:T(8,128)S(1)}, u32[]{:S(2)}, u32[]{:S(2)}) collective-permute-start(f32[9,64,128]{2,1,0:T(8,128)S(1)} %get-tuple-element.16), channel_id=1, source_target_pairs={{4,8},{8,4},{5,9},{9,5},{6,10},{10,6},{7,11},{11,7},{20,24},{24,20... | collective-permute-start | bytes 884744 | tf_op jit(solution)/shard_map/ppermute | solution.py:611
  7.1 0.0 collective-permute-done.1.refs_1_
  7.1 1.9 %shard_map.87 = (f32[3072,128]{1,0:T(8,128)S(1)}, s32[16,128]{1,0:T(8,128)S(1)}) custom-call(f32[904,128]{1,0:T(8,128)S(1)} %get-tuple-element.13.refs_0_.points_ref, f32[904,128]{1,0:T(8,128)S(1)} %collective-permute-done.1.refs_1_), custom_call_target="tpu_custom_call" | custom-call | tf_op jit(solution)/shard_map/pallas_call | solution.py:410
  9.1 4.9 %collective-permute-done.2.near = f32[9,64,128]{2,1,0:T(8,128)S(1)} collective-permute-done((f32[9,64,128]{2,1,0:T(8,128)S(1)}, f32[9,64,128]{2,1,0:T(8,128)S(1)}, u32[]{:S(2)}, u32[]{:S(2)}) %collective-permute-start.2) | collective-permute-done | bytes 294944 | tf_op jit(solution)/shard_map/ppermute | solution.py:611
  13.9 2.4 %shard_map.88 = (bf16[1,576,256]{2,1,0:T(8,128)(2,1)S(1)}, f32[80,128]{1,0:T(8,128)S(1)}) custom-call(f32[3072,128]{1,0:T(8,128)S(1)} %get-tuple-element.14.packed, s32[16,128]{1,0:T(8,128)S(1)} %get-tuple-element.15.rows_ref, f32[9,64,128]{2,1,0:T(8,128)S(1)} %collective-permute-done.2.near), custom_call_target="tpu_custom_call" | custom-call | tf_op jit(solution)/shard_map/pallas_call | solution.py:425
  16.4 0.0 collective-permute-done.3.far
  16.4 0.0 collective-permute-done.refs_0_
  16.4 0.1 collective-permute-start.4
  16.5 0.2 shard_map.89
  16.7 1.6 %collective-permute-done.4.refs_1_ = f32[904,128]{1,0:T(8,128)S(1)} collective-permute-done((f32[904,128]{1,0:T(8,128)S(1)}, f32[904,128]{1,0:T(8,128)S(1)}, u32[]{:S(2)}, u32[]{:S(2)}) %collective-permute-start.4) | collective-permute-done | bytes 462880 | tf_op jit(solution)/shard_map/ppermute | solution.py:623
  18.3 4.0 %shard_map.90 = f32[80,128]{1,0:T(8,128)S(1)} custom-call(f32[904,128]{1,0:T(8,128)S(1)} %collective-permute-done.refs_0_, f32[904,128]{1,0:T(8,128)S(1)} %collective-permute-done.4.refs_1_, bf16[2,576,256]{2,1,0:T(8,128)(2,1)S(1)} %get-tuple-element.20.refs_2_, f32[80,128]{1,0:T(8,128)S(1)} %get-tuple-element.21.refs_3_), custom_call_target="tpu_custom_call" | custom-call | tf_op jit(solution)/shard_map/pallas_call | solution.py:440
  22.3 9.7 %all-gather = f32[640,128]{1,0:T(8,128)S(1)} all-gather(f32[80,128]{1,0:T(8,128)S(1)} %shard_map.90), channel_id=2, replica_groups=mesh['seg'=2,'strip'=4,'tile'=4] {'seg','tile'}, dimensions={0}, use_global_device_ids=true | all-gather | bytes 368640 | tf_op jit(solution)/shard_map/all_gather | solution.py:625
  32.0 1.3 %shard_map.91 = (f32[3,64,128]{2,1,0:T(8,128)}, f32[6,1,128]{2,1,0:T(1,128)}) custom-call(f32[8,80,128]{2,1,0:T(8,128)S(1)} %bitcast.8, f32[904,128]{1,0:T(8,128)S(1)} %get-tuple-element.13.refs_0_.points_ref), custom_call_target="tpu_custom_call" | custom-call | tf_op jit(solution)/shard_map/pallas_call | solution.py:626
Async XLA Ops:
  1.8 5.3 %collective-permute-start.1 = (f32[904,128]{1,0:T(8,128)S(1)}, f32[904,128]{1,0:T(8,128)S(1)}, u32[]{:S(2)}, u32[]{:S(2)}) collective-permute-start(f32[904,128]{1,0:T(8,128)S(1)} %get-tuple-element.13.refs_0_.points_ref), channel_id=1, source_target_pairs={{0,1},{1,0},{2,3},{3,2},{4,5},{5,4},{6,7},{7,6},{8,9},{9,8},{10,11... | collective-permute-start | bytes 1388552 | tf_op jit(solution)/shard_map/ppermute | solution.py:619
  2.3 14.1 %collective-permute-start = (f32[904,128]{1,0:T(8,128)S(1)}, f32[904,128]{1,0:T(8,128)S(1)}, u32[]{:S(2)}, u32[]{:S(2)}) collective-permute-start(f32[904,128]{1,0:T(8,128)S(1)} %get-tuple-element.13.refs_0_.points_ref), channel_id=1, source_target_pairs={{2,0},{3,1},{0,2},{1,3},{6,4},{7,5},{4,6},{5,7},{10,8},{11,9},{8,1... | collective-permute-start | bytes 1388552 | tf_op jit(solution)/shard_map/ppermute | solution.py:617
  4.9 9.1 %collective-permute-start.2 = (f32[9,64,128]{2,1,0:T(8,128)S(1)}, f32[9,64,128]{2,1,0:T(8,128)S(1)}, u32[]{:S(2)}, u32[]{:S(2)}) collective-permute-start(f32[9,64,128]{2,1,0:T(8,128)S(1)} %get-tuple-element.16), channel_id=1, source_target_pairs={{0,4},{4,0},{8,12},{12,8},{1,5},{5,1},{9,13},{13,9},{2,6},{6,2},{1... | collective-permute-start | bytes 884744 | tf_op jit(solution)/shard_map/ppermute | solution.py:611
  6.4 10.0 %collective-permute-start.3 = (f32[9,64,128]{2,1,0:T(8,128)S(1)}, f32[9,64,128]{2,1,0:T(8,128)S(1)}, u32[]{:S(2)}, u32[]{:S(2)}) collective-permute-start(f32[9,64,128]{2,1,0:T(8,128)S(1)} %get-tuple-element.16), channel_id=1, source_target_pairs={{4,8},{8,4},{5,9},{9,5},{6,10},{10,6},{7,11},{11,7},{20,24},{24,20... | collective-permute-start | bytes 884744 | tf_op jit(solution)/shard_map/ppermute | solution.py:611
  16.4 1.9 %collective-permute-start.4 = (f32[904,128]{1,0:T(8,128)S(1)}, f32[904,128]{1,0:T(8,128)S(1)}, u32[]{:S(2)}, u32[]{:S(2)}) collective-permute-start(f32[904,128]{1,0:T(8,128)S(1)} %collective-permute-done.refs_0_), channel_id=1, source_target_pairs={{0,1},{1,0},{2,3},{3,2},{4,5},{5,4},{6,7},{7,6},{8,9},{9,8},{10,11... | collective-permute-start | bytes 1388552 | tf_op jit(solution)/shard_map/ppermute | solution.py:623

commit v10 on v9

--- a/solution.py
+++ b/solution.py
@@ -277,13 +277,15 @@
     def add(step, carry):
         far = step >= near_groups
         base = jnp.where(far, room - ROW_GROUP * (step - near_groups + 1), step * ROW_GROUP)
-        add_rows(pl.multiple_of(base, ROW_GROUP), packed, target, totals_ref, terms_ref)
+        used = jnp.where(far, far_rows - ROW_GROUP * (step - near_groups), near_rows - ROW_GROUP * step)
+        base = pl.multiple_of(base, ROW_GROUP)
+        add_rows(base, far, used, packed, target, totals_ref, terms_ref)
         return carry
 
     lax.fori_loop(0, near_groups + far_groups, add, 0)
 
 
-def add_rows(base, packed, target, totals_ref, terms_ref):
+def add_rows(base, far, used, packed, target, totals_ref, terms_ref):
     group = ROW_GROUP
     span = pl.ds(base, group)
 
@@ -334,23 +336,32 @@
         terms += [entry * weight for entry in gradient]
     for place, term in enumerate(terms):
         terms_ref[place * SPREAD : place * SPREAD + group, :] = term
-    knots = own(KNOT).astype(jnp.int32)
     stacked = lax.broadcasted_iota(jnp.int32, (KNOT_DEV, TILE_PTS), 0)
-    total = totals_ref[...]
-    for row in range(0, group, 2):
-        parts, hots = [], []
-        for r in (row, row + 1):
-            high, low = split_two(terms_ref[pl.ds(r, SUM_ROWS, stride=SPREAD), :])
-            parts.append(jnp.concatenate([high, low], axis=0))
-            hots.append(jnp.where(stacked == knots[r : r + 1], 1.0, 0.0).astype(jnp.bfloat16))
-        sums = lax.dot_general(
-            jnp.concatenate(parts, axis=1),
-            jnp.concatenate(hots, axis=1),
-            (((1,), (1,)), ((), ())),
-            preferred_element_type=jnp.float32,
-        )
-        total = total + sums[0:SUM_ROWS] + sums[SUM_ROWS:]
-    totals_ref[...] = total
+
+    def add(first, count):
+        total = totals_ref[...]
+        for place in range(first, first + count, 2):
+            parts, hots = [], []
+            for r in (place, place + 1):
+                r = jnp.where(far, group - 1 - r, r)
+                high, low = split_two(terms_ref[pl.ds(r, SUM_ROWS, stride=SPREAD), :])
+                parts.append(jnp.concatenate([high, low], axis=0))
+                knots = packed[pl.ds((base + r) * POINT_ROWS + KNOT, 1), :].astype(jnp.int32)
+                hots.append(jnp.where(stacked == knots, 1.0, 0.0).astype(jnp.bfloat16))
+            sums = lax.dot_general(
+                jnp.concatenate(parts, axis=1),
+                jnp.concatenate(hots, axis=1),
+                (((1,), (1,)), ((), ())),
+                preferred_element_type=jnp.float32,
+            )
+            total = total + sums[0:SUM_ROWS] + sums[SUM_ROWS:]
+        totals_ref[...] = total
+
+    add(0, 12)
+
+    @pl.when(used > 12)
+    def _():
+        add(12, group - 12)
 
 
 def early_kernel(groups, *refs):

time: 33.4 us -> 33.7 us (level)
  Pallas kernels: 11 us -> 11.6 us
  blocking collectives: 9.69 us -> 9.28 us
    all_gather x1, blocking collectives: 9.69 us -> 9.28 us  [local(): all_sums = lax.all_gather(sums, ('seg', 'tile'), axis=0)]
    pallas_call x1, Pallas kernels: 4.01 us -> 4.4 us  [all_totals(): pl.pallas_call(functools.partial(other_kernel, groups), out_shape=jax.Sha...]
where the time goes in v10:
time: 33.7 us; the launch traced here: 33.5 us
  Pallas kernels  11.6 us (34%)
  blocking collectives  9.28 us (28%)
  waiting for transfers between devices  6.45 us (19%)
  starting transfers between devices  5.4 us (16%)
  between operations  0.71 us (2%)
    all_gather x1, blocking collectives, local(): all_sums = lax.all_gather(sums, ('seg', 'tile'), axis=0)  9.28 us
    ppermute x2, waiting for transfers between devices, trade(): return lax.ppermute(table, 'strip', pairs)  4.87 us
    pallas_call x1, Pallas kernels, all_totals(): pl.pallas_call(functools.partial(other_kernel, groups), out_shape=jax.Sha...  4.4 us
    pallas_call x2, Pallas kernels, own_totals(): pl.pallas_call(kernel, out_shape=(jax.ShapeDtypeStruct((slots, CHANNELS *...  2.88 us
    ppermute x1, starting transfers between devices, local(): arrived.append(lax.ppermute(points, 'tile', pairs))  2.56 us
    ppermute x2, starting transfers between devices, trade(): return lax.ppermute(table, 'strip', pairs)  2.24 us
    pallas_call x1, Pallas kernels, early_rows(): pl.pallas_call(functools.partial(early_kernel, groups), out_shape=(jax.Sh...  1.94 us
    ppermute x1, waiting for transfers between devices, local(): others = arrived + [lax.ppermute(group, 'tile', swap) for group in arrived]  1.57 us
  transfers between devices with their start and end apart: 5, of which 2 were waited for; matrix products, arithmetic and copies ran while one was open for 0% of the time, Pallas kernels for 14%

profile of v10, /device:TPU:0, one launch (start us, length us, event | category | flops | bytes accessed | tf_op | source)
XLA Modules:
  0.0 33.5 jit_solution(10023856281528300969)
XLA Ops:
  0.6 1.1 %shard_map.86 = (f32[9,64,128]{2,1,0:T(8,128)S(1)}, f32[904,128]{1,0:T(8,128)S(1)}) custom-call(f32[3,64,128]{2,1,0:T(8,128)} %bitcast.10, f32[6,64,128]{2,1,0:T(8,128)} %bitcast.9, f32[3,64,128]{2,1,0:T(8,128)} %bitcast.11, f32[64,128]{1,0:T(8,128)} %bitcast.12, s32[64,128]{1,0:T(8,128)} %bitcast.13, s32[1,64]{1,0:T(1,128)} %sides.1, s32[1,64]{1,0:T(1,128)} %knots.1), custom_call_target="tpu_custom_call" | custom-call | tf_op jit(solution)/shard_map/pallas_call | solution.py:589
  1.8 0.5 %collective-permute-start.1 = (f32[904,128]{1,0:T(8,128)S(1)}, f32[904,128]{1,0:T(8,128)S(1)}, u32[]{:S(2)}, u32[]{:S(2)}) collective-permute-start(f32[904,128]{1,0:T(8,128)S(1)} %get-tuple-element.13.refs_0_.points_ref), channel_id=1, source_target_pairs={{0,1},{1,0},{2,3},{3,2},{4,5},{5,4},{6,7},{7,6},{8,9},{9,8},{10,11... | collective-permute-start | bytes 1388552 | tf_op jit(solution)/shard_map/ppermute | solution.py:630
  2.3 2.6 %collective-permute-start = (f32[904,128]{1,0:T(8,128)S(1)}, f32[904,128]{1,0:T(8,128)S(1)}, u32[]{:S(2)}, u32[]{:S(2)}) collective-permute-start(f32[904,128]{1,0:T(8,128)S(1)} %get-tuple-element.13.refs_0_.points_ref), channel_id=1, source_target_pairs={{2,0},{3,1},{0,2},{1,3},{6,4},{7,5},{4,6},{5,7},{10,8},{11,9},{8,1... | collective-permute-start | bytes 1388552 | tf_op jit(solution)/shard_map/ppermute | solution.py:628
  4.9 1.6 %collective-permute-start.2 = (f32[9,64,128]{2,1,0:T(8,128)S(1)}, f32[9,64,128]{2,1,0:T(8,128)S(1)}, u32[]{:S(2)}, u32[]{:S(2)}) collective-permute-start(f32[9,64,128]{2,1,0:T(8,128)S(1)} %get-tuple-element.16), channel_id=1, source_target_pairs={{0,4},{4,0},{8,12},{12,8},{1,5},{5,1},{9,13},{13,9},{2,6},{6,2},{1... | collective-permute-start | bytes 884744 | tf_op jit(solution)/shard_map/ppermute | solution.py:622
  6.4 0.7 %collective-permute-start.3 = (f32[9,64,128]{2,1,0:T(8,128)S(1)}, f32[9,64,128]{2,1,0:T(8,128)S(1)}, u32[]{:S(2)}, u32[]{:S(2)}) collective-permute-start(f32[9,64,128]{2,1,0:T(8,128)S(1)} %get-tuple-element.16), channel_id=1, source_target_pairs={{4,8},{8,4},{5,9},{9,5},{6,10},{10,6},{7,11},{11,7},{20,24},{24,20... | collective-permute-start | bytes 884744 | tf_op jit(solution)/shard_map/ppermute | solution.py:622
  7.1 0.0 collective-permute-done.1.refs_1_
  7.1 1.9 %shard_map.87 = (f32[3072,128]{1,0:T(8,128)S(1)}, s32[16,128]{1,0:T(8,128)S(1)}) custom-call(f32[904,128]{1,0:T(8,128)S(1)} %get-tuple-element.13.refs_0_.points_ref, f32[904,128]{1,0:T(8,128)S(1)} %collective-permute-done.1.refs_1_), custom_call_target="tpu_custom_call" | custom-call | tf_op jit(solution)/shard_map/pallas_call | solution.py:421
  9.1 4.9 %collective-permute-done.2.near = f32[9,64,128]{2,1,0:T(8,128)S(1)} collective-permute-done((f32[9,64,128]{2,1,0:T(8,128)S(1)}, f32[9,64,128]{2,1,0:T(8,128)S(1)}, u32[]{:S(2)}, u32[]{:S(2)}) %collective-permute-start.2) | collective-permute-done | bytes 294944 | tf_op jit(solution)/shard_map/ppermute | solution.py:622
  13.9 2.6 %shard_map.88 = (bf16[1,576,256]{2,1,0:T(8,128)(2,1)S(1)}, f32[80,128]{1,0:T(8,128)S(1)}) custom-call(f32[3072,128]{1,0:T(8,128)S(1)} %get-tuple-element.14.packed, s32[16,128]{1,0:T(8,128)S(1)} %get-tuple-element.15.rows_ref, f32[9,64,128]{2,1,0:T(8,128)S(1)} %collective-permute-done.2.near), custom_call_target="tpu_custom_call" | custom-call | tf_op jit(solution)/shard_map/pallas_call | solution.py:436
  16.6 0.0 collective-permute-done.3.far
  16.6 0.0 collective-permute-done.refs_0_
  16.6 0.1 collective-permute-start.4
  16.7 0.2 shard_map.89
  16.9 1.6 %collective-permute-done.4.refs_1_ = f32[904,128]{1,0:T(8,128)S(1)} collective-permute-done((f32[904,128]{1,0:T(8,128)S(1)}, f32[904,128]{1,0:T(8,128)S(1)}, u32[]{:S(2)}, u32[]{:S(2)}) %collective-permute-start.4) | collective-permute-done | bytes 462880 | tf_op jit(solution)/shard_map/ppermute | solution.py:634
  18.5 4.4 %shard_map.90 = f32[80,128]{1,0:T(8,128)S(1)} custom-call(f32[904,128]{1,0:T(8,128)S(1)} %collective-permute-done.refs_0_, f32[904,128]{1,0:T(8,128)S(1)} %collective-permute-done.4.refs_1_, bf16[2,576,256]{2,1,0:T(8,128)(2,1)S(1)} %get-tuple-element.20.refs_2_, f32[80,128]{1,0:T(8,128)S(1)} %get-tuple-element.21.refs_3_), custom_call_target="tpu_custom_call" | custom-call | tf_op jit(solution)/shard_map/pallas_call | solution.py:451
  22.9 9.3 %all-gather = f32[640,128]{1,0:T(8,128)S(1)} all-gather(f32[80,128]{1,0:T(8,128)S(1)} %shard_map.90), channel_id=2, replica_groups=mesh['seg'=2,'strip'=4,'tile'=4] {'seg','tile'}, dimensions={0}, use_global_device_ids=true | all-gather | bytes 368640 | tf_op jit(solution)/shard_map/all_gather | solution.py:636
  32.2 1.3 %shard_map.91 = (f32[3,64,128]{2,1,0:T(8,128)}, f32[6,1,128]{2,1,0:T(1,128)}) custom-call(f32[8,80,128]{2,1,0:T(8,128)S(1)} %bitcast.8, f32[904,128]{1,0:T(8,128)S(1)} %get-tuple-element.13.refs_0_.points_ref), custom_call_target="tpu_custom_call" | custom-call | tf_op jit(solution)/shard_map/pallas_call | solution.py:637
Async XLA Ops:
  1.8 5.3 %collective-permute-start.1 = (f32[904,128]{1,0:T(8,128)S(1)}, f32[904,128]{1,0:T(8,128)S(1)}, u32[]{:S(2)}, u32[]{:S(2)}) collective-permute-start(f32[904,128]{1,0:T(8,128)S(1)} %get-tuple-element.13.refs_0_.points_ref), channel_id=1, source_target_pairs={{0,1},{1,0},{2,3},{3,2},{4,5},{5,4},{6,7},{7,6},{8,9},{9,8},{10,11... | collective-permute-start | bytes 1388552 | tf_op jit(solution)/shard_map/ppermute | solution.py:630
  2.3 14.3 %collective-permute-start = (f32[904,128]{1,0:T(8,128)S(1)}, f32[904,128]{1,0:T(8,128)S(1)}, u32[]{:S(2)}, u32[]{:S(2)}) collective-permute-start(f32[904,128]{1,0:T(8,128)S(1)} %get-tuple-element.13.refs_0_.points_ref), channel_id=1, source_target_pairs={{2,0},{3,1},{0,2},{1,3},{6,4},{7,5},{4,6},{5,7},{10,8},{11,9},{8,1... | collective-permute-start | bytes 1388552 | tf_op jit(solution)/shard_map/ppermute | solution.py:628
  4.9 9.1 %collective-permute-start.2 = (f32[9,64,128]{2,1,0:T(8,128)S(1)}, f32[9,64,128]{2,1,0:T(8,128)S(1)}, u32[]{:S(2)}, u32[]{:S(2)}) collective-permute-start(f32[9,64,128]{2,1,0:T(8,128)S(1)} %get-tuple-element.16), channel_id=1, source_target_pairs={{0,4},{4,0},{8,12},{12,8},{1,5},{5,1},{9,13},{13,9},{2,6},{6,2},{1... | collective-permute-start | bytes 884744 | tf_op jit(solution)/shard_map/ppermute | solution.py:622
  6.4 10.2 %collective-permute-start.3 = (f32[9,64,128]{2,1,0:T(8,128)S(1)}, f32[9,64,128]{2,1,0:T(8,128)S(1)}, u32[]{:S(2)}, u32[]{:S(2)}) collective-permute-start(f32[9,64,128]{2,1,0:T(8,128)S(1)} %get-tuple-element.16), channel_id=1, source_target_pairs={{4,8},{8,4},{5,9},{9,5},{6,10},{10,6},{7,11},{11,7},{20,24},{24,20... | collective-permute-start | bytes 884744 | tf_op jit(solution)/shard_map/ppermute | solution.py:622
  16.6 1.9 %collective-permute-start.4 = (f32[904,128]{1,0:T(8,128)S(1)}, f32[904,128]{1,0:T(8,128)S(1)}, u32[]{:S(2)}, u32[]{:S(2)}) collective-permute-start(f32[904,128]{1,0:T(8,128)S(1)} %collective-permute-done.refs_0_), channel_id=1, source_target_pairs={{0,1},{1,0},{2,3},{3,2},{4,5},{5,4},{6,7},{7,6},{8,9},{9,8},{10,11... | collective-permute-start | bytes 1388552 | tf_op jit(solution)/shard_map/ppermute | solution.py:634
